TPU v7x, 128 devices: a whole 4x4x4 slice. The times are simulated.
128 devices in a mesh: sec: 32 (over x, y, z_hi), tile: 4 (over z_lo, core).
Axes of the slice: x: 4, y: 4, z: 4 (z_hi: 2, z_lo: 2; z = z_hi * 2 + z_lo), core: 2. Of those that a mesh axis runs over, the one named last changes fastest.
Arguments:
- features: bfloat16 [96, 32, 64, 128], P('sec', None, 'tile'), may hold values from -6 to 6
- vote_grad: float32 [96, 2, 64, 128], P('sec', None, 'tile'), may hold values from -6 to 6
- sharpness: float32 [96], P('sec')
- valid_rows: int32 [96], P('sec'), may hold values from 32 to 64
- first_kernel: bfloat16 [3, 3, 64, 64], replicated, may hold values from -0.25 to 0.25
- first_bias: float32 [64], replicated, may hold values from -3 to 3
- second_kernel: bfloat16 [3, 3, 2, 64], replicated, may hold values from -0.25 to 0.25
- second_bias: float32 [2], replicated, may hold values from -3 to 3
Outputs:
- voted_field: float32 [96, 2, 64, 128], P('sec', None, 'tile')
- feature_grad: float32 [96, 32, 64, 128], P('sec', None, 'tile')
All inputs are finite; a program needn't handle non-finite values.
Results may differ from a plain program's by a relative error of at most 0.03.
Values may be sent and summed in bfloat16 or wider, within the bound.
No kernel may reach another device: no remote copies, remote signals or barrier semaphores. Data moves between devices by JAX's collectives and lax.ppermute only.
A program may use at most 128 MiB of HBM per device.

v0:
```python
import jax
import jax.numpy as jnp
from jax import lax
from jax.experimental import pallas as pl
from jax.experimental.pallas import tpu as pltpu
from jax.sharding import PartitionSpec as P

F32 = jnp.float32
BF16 = jnp.bfloat16
OWN = 3
CH = 32
HID = 64
TR = 16
COLS = 128
HALO = 4
FEAT_ROWS = TR + 2 * HALO
HID_ROWS = FEAT_ROWS - 2
FLD_ROWS = FEAT_ROWS - 4
DH_ROWS = FEAT_ROWS - 6
EDGE = HALO * OWN * CH
EDGE_ALL = EDGE + 32


def lane(shape):
    return lax.broadcasted_iota(jnp.int32, shape, len(shape) - 1)


def from_left(x):
    return jnp.where(lane(x.shape) == 0, 0.0, pltpu.roll(x, 1, x.ndim - 1))


def from_right(x):
    return jnp.where(lane(x.shape) == COLS - 1, 0.0, pltpu.roll(x, COLS - 1, x.ndim - 1))


def dot(a, b):
    return jnp.dot(a, b, preferred_element_type=F32)


def edges_kernel(info, valid, feat, vgrad, top, bottom, wide, ext):
    row0 = info[0]
    for out, first, cot_first in ((top, 0, 0), (bottom, TR - HALO, TR - 2)):
        ext[...] = jnp.zeros((32, COLS), F32)
        for s in range(OWN):
            pos = row0 + cot_first + lax.broadcasted_iota(jnp.int32, (2, COLS), 0)
            for c in range(2):
                cot = jnp.where(pos < valid[s], vgrad[s, c, cot_first : cot_first + 2, :], 0.0)
                high = cot.astype(BF16).astype(F32)
                at = s * 4 + c * 2
                ext[at : at + 2, :] = high
                ext[12 + at : 14 + at, :] = cot - high
        out[EDGE:, :] = ext[...].astype(BF16)
    for s in range(OWN):
        wide[...] = feat[s].astype(F32)
        for out, first in ((top, 0), (bottom, TR - HALO)):
            for r in range(HALO):
                at = (r * OWN + s) * CH
                out[at : at + CH, :] = wide[:, first + r, :].astype(BF16)


def edges(info, valid, feat, vgrad):
    smem = pl.BlockSpec(memory_space=pltpu.SMEM)
    vmem = pl.BlockSpec(memory_space=pltpu.VMEM)
    shape = jax.ShapeDtypeStruct((EDGE_ALL, COLS), BF16)
    return pl.pallas_call(
        edges_kernel,
        out_shape=(shape, shape),
        in_specs=[smem, smem, vmem, vmem],
        out_specs=(vmem, vmem),
        scratch_shapes=[pltpu.VMEM((CH, TR, COLS), F32), pltpu.VMEM((32, COLS), F32)],
        name="edges",
    )(info, valid, feat, vgrad)


def spread_row(x, xd, j, r):
    xd[j, r, 0:CH, :] = from_left(x).astype(BF16)
    xd[j, r, CH : 2 * CH, :] = x.astype(BF16)
    xd[j, r, 2 * CH :, :] = from_right(x).astype(BF16)


def spread(feat, above, below, keep, has_above, has_below, xd, j0, wide):
    for s in range(OWN):
        wide[s] = feat[s].astype(F32) * keep
    scale_above = keep * has_above
    scale_below = keep * has_below
    for s in range(OWN):
        for r in range(TR):
            spread_row(wide[s, :, r, :], xd, j0 + s, HALO + r)
        for r in range(HALO):
            at = (r * OWN + s) * CH
            spread_row(above[at : at + CH, :].astype(F32) * scale_above, xd, j0 + s, r)
            spread_row(
                below[at : at + CH, :].astype(F32) * scale_below, xd, j0 + s, HALO + TR + r
            )


def taps(ref, rows, pick):
    return jnp.concatenate(
        [jnp.concatenate([pick(ref, r), pick(ref, r + 1)], axis=1) for r in rows], axis=0
    )


def hidden_stage(row0, xd, wcur, wear, wboth, bias, w2f, hid, tsum):
    def step(i, carry):
        r = 2 * i
        pos = row0 - 3 + r
        keep = jnp.concatenate(
            [
                jnp.full((HID, COLS), ((pos + d >= 0) & (pos + d < 4 * TR)).astype(F32))
                for d in range(2)
            ],
            axis=1,
        )
        cur, ear = {}, {}
        for j in range(6):
            rhs = taps(xd, (r, r + 1, r + 2), lambda ref, q, j=j: ref[j, q])
            if j < 3:
                ear[j] = dot(wear[...], rhs)
            elif j < 5:
                both = dot(wboth[...], rhs)
                cur[j] = both[:HID] + bias[...]
                ear[j] = both[HID:]
            else:
                cur[j] = dot(wcur[...], rhs) + bias[...]
        for s in range(OWN):
            parts = []
            for k in (1, 2, 3):
                h = jnp.maximum(cur[3 + s] + ear[3 + s - k], 0.0) * keep
                parts.append(h.astype(BF16))
            h3 = jnp.concatenate(parts, axis=0)
            hid[r, 192 * s : 192 * s + 192, :] = h3[:, :COLS]
            hid[r + 1, 192 * s : 192 * s + 192, :] = h3[:, COLS:]
            t = dot(w2f[...], h3)
            tsum[s, r] = t[:, :COLS]
            tsum[s, r + 1] = t[:, COLS:]
        return carry

    lax.fori_loop(0, HID_ROWS // 2, step, 0)


def vote_stage(row0, sharp, valid, vgrad, above, below, has, bias2, tsum, fld, cot, grd, g3, voted):
    ends = [
        (above[EDGE:, :].astype(F32) * has[0], 0),
        (below[EDGE:, :].astype(F32) * has[1], TR + 2),
    ]
    for s in range(OWN):
        for c in range(2):
            at = s * 4 + c * 2
            for ext, first in ends:
                cot[s, c, first : first + 2, :] = ext[at : at + 2] + ext[12 + at : 14 + at]
            pos = row0 + lax.broadcasted_iota(jnp.int32, (TR, COLS), 0)
            cot[s, c, 2 : 2 + TR, :] = jnp.where(pos < valid[s], vgrad[s, c], 0.0)

    def field_row(r, carry):
        for s in range(OWN):
            sums = []
            for dx in range(3):
                acc = tsum[s, r, 8 * dx : 8 * dx + 8, :]
                for dy in (1, 2):
                    at = 8 * (3 * dy + dx)
                    acc = acc + tsum[s, r + dy, at : at + 8, :]
                sums.append(acc)
            fld[s, r] = sums[1] + from_left(sums[0]) + from_right(sums[2]) + bias2[...]
        return carry

    lax.fori_loop(0, FLD_ROWS, field_row, 0, unroll=2)

    for s in range(OWN):
        f = [[fld[s, :, 2 * k + c, :] for c in range(2)] for k in range(3)]
        beta = sharp[s]
        diff = {}
        dist = {}
        for a, b in ((0, 1), (0, 2), (1, 2)):
            diff[a, b] = [f[a][c] - f[b][c] for c in range(2)]
            dist[a, b] = diff[a, b][0] * diff[a, b][0] + diff[a, b][1] * diff[a, b][1]
        score = [dist[0, 1] + dist[0, 2], dist[0, 1] + dist[1, 2], dist[0, 2] + dist[1, 2]]
        logit = [-beta * q for q in score]
        top = jnp.maximum(jnp.maximum(logit[0], logit[1]), logit[2])
        expo = [jnp.exp(q - top) for q in logit]
        inv = 1.0 / (expo[0] + expo[1] + expo[2])
        w = [q * inv for q in expo]
        v = [w[0] * f[0][c] + w[1] * f[1][c] + w[2] * f[2][c] for c in range(2)]
        for c in range(2):
            voted[s, c] = v[c][2 : 2 + TR]
        g = [cot[s, c, 0:FLD_ROWS, :] for c in range(2)]
        e = [
            -beta * w[k] * (g[0] * (f[k][0] - v[0]) + g[1] * (f[k][1] - v[1])) for k in range(3)
        ]
        pair = {key: 2.0 * (e[key[0]] + e[key[1]]) for key in diff}
        for c in range(2):
            m01 = pair[0, 1] * diff[0, 1][c]
            m02 = pair[0, 2] * diff[0, 2][c]
            m12 = pair[1, 2] * diff[1, 2][c]
            grd[s, :, 0 + c, :] = w[0] * g[c] + m01 + m02
            grd[s, :, 2 + c, :] = w[1] * g[c] - m01 + m12
            grd[s, :, 4 + c, :] = w[2] * g[c] - m02 - m12
        grd[s, :, 6, :] = jnp.zeros((FLD_ROWS, COLS), F32)
        grd[s, :, 7, :] = jnp.zeros((FLD_ROWS, COLS), F32)

    def spread_grad(r, carry):
        for s in range(OWN):
            x = grd[s, r]
            g3[s, r] = jnp.concatenate(
                [from_right(x), x, from_left(x), jnp.zeros_like(x)], axis=0
            ).astype(BF16)
        return carry

    lax.fori_loop(0, FLD_ROWS, spread_grad, 0, unroll=2)


def hidden_grad_stage(w2b, g3, hid, dlow, down):
    def step(i, carry):
        q = 2 * i
        masked = {}
        for s in range(OWN):
            rhs = taps(g3, (q + 2, q + 1, q), lambda ref, r, s=s: ref[s, r])
            dh = dot(w2b[...], rhs)
            h = jnp.concatenate(
                [hid[q + 2 + d, 192 * s : 192 * s + 192, :] for d in range(2)], axis=1
            )
            dh = jnp.where(h.astype(F32) > 0.0, dh, 0.0)
            for k in (1, 2, 3):
                masked[s, k] = dh[HID * (k - 1) : HID * k]
        low = jnp.concatenate(
            [
                masked[0, 3],
                masked[0, 2] + masked[1, 3],
                masked[0, 1] + masked[1, 2] + masked[2, 3],
            ],
            axis=0,
        ).astype(BF16)
        cur = [masked[s, 1] + masked[s, 2] + masked[s, 3] for s in range(OWN)]
        own = jnp.concatenate(
            [cur[0], masked[1, 1] + masked[2, 2], cur[1], masked[2, 1], cur[2]], axis=0
        ).astype(BF16)
        for d in range(2):
            dlow[q + d] = low[:, COLS * d : COLS * d + COLS]
            down[q + d] = own[:, COLS * d : COLS * d + COLS]
        return carry

    lax.fori_loop(0, DH_ROWS // 2, step, 0)


def gather_columns(p):
    return from_right(p[:CH]) + p[CH : 2 * CH] + from_left(p[2 * CH :])


def feature_grad_stage(dref, jobs):
    def step(i, carry):
        r = 2 * i
        for first, size, weight, out, s in jobs:
            rhs = taps(
                dref,
                (r + 2, r + 1, r),
                lambda ref, q, first=first, size=size: ref[q, first : first + size, :],
            )
            p = dot(weight[...], rhs)
            for d in range(2):
                out[r + d, s] = gather_columns(p[:, COLS * d : COLS * d + COLS]).astype(out.dtype)
        return carry

    lax.fori_loop(0, TR // 2, step, 0)


def main_kernel(
    info, valid, sharp,
    feat, prev, above, below, pabove, pbelow, vgrad,
    wcur, wear, wboth, bias, w2f, bias2, w2b, wgcur, wgear, wgboth,
    voted, low, own,
    wide, xd, hid, tsum, fld, cot, grd, g3, dlow, down,
):
    row0 = info[0]
    has = [(info[1] > 0).astype(F32), (info[2] > 0).astype(F32)]
    keep_prev = (info[3] > 0).astype(F32)
    spread(feat, above, below, 1.0, has[0], has[1], xd, 3, wide)
    spread(prev, pabove, pbelow, keep_prev, has[0], has[1], xd, 0, wide)
    hidden_stage(row0, xd, wcur, wear, wboth, bias, w2f, hid, tsum)
    vote_stage(
        row0, sharp, valid, vgrad, above, below, has, bias2, tsum, fld, cot, grd, g3, voted
    )
    hidden_grad_stage(w2b, g3, hid, dlow, down)
    feature_grad_stage(dlow, [(64 * s, 64, wgear, low, s) for s in range(OWN)])
    feature_grad_stage(
        down, [(0, 128, wgboth, own, 0), (128, 128, wgboth, own, 1), (256, 64, wgcur, own, 2)]
    )


def main(*args):
    smem = pl.BlockSpec(memory_space=pltpu.SMEM)
    vmem = pl.BlockSpec(memory_space=pltpu.VMEM)
    return pl.pallas_call(
        main_kernel,
        out_shape=(
            jax.ShapeDtypeStruct((OWN, 2, TR, COLS), F32),
            jax.ShapeDtypeStruct((TR, OWN, CH, COLS), BF16),
            jax.ShapeDtypeStruct((TR, OWN, CH, COLS), F32),
        ),
        in_specs=[smem] * 3 + [vmem] * (len(args) - 3),
        out_specs=(vmem, vmem, vmem),
        scratch_shapes=[
            pltpu.VMEM((OWN, CH, TR, COLS), F32),
            pltpu.VMEM((6, FEAT_ROWS, 3 * CH, COLS), BF16),
            pltpu.VMEM((HID_ROWS, 9 * HID, COLS), BF16),
            pltpu.VMEM((OWN, HID_ROWS, 72, COLS), F32),
            pltpu.VMEM((OWN, FLD_ROWS, 8, COLS), F32),
            pltpu.VMEM((OWN, 2, 24, COLS), F32),
            pltpu.VMEM((OWN, FLD_ROWS, 8, COLS), F32),
            pltpu.VMEM((OWN, FLD_ROWS, 32, COLS), BF16),
            pltpu.VMEM((DH_ROWS, 3 * HID, COLS), BF16),
            pltpu.VMEM((DH_ROWS, 5 * HID, COLS), BF16),
        ],
        compiler_params=pltpu.CompilerParams(vmem_limit_bytes=40 << 20),
        name="main",
    )(*args)


def finish_kernel(info, own, back, out):
    keep = (info[4] > 0).astype(F32)

    def step(r, carry):
        for s in range(OWN):
            out[s, :, r, :] = own[r, s] + back[r, s].astype(F32) * keep
        return carry

    for r in range(TR):
        step(r, 0)


def finish(info, own, back):
    smem = pl.BlockSpec(memory_space=pltpu.SMEM)
    vmem = pl.BlockSpec(memory_space=pltpu.VMEM)
    return pl.pallas_call(
        finish_kernel,
        out_shape=jax.ShapeDtypeStruct((OWN, CH, TR, COLS), F32),
        in_specs=[smem, vmem, vmem],
        out_specs=vmem,
        name="finish",
    )(info, own, back)


def shift(value, secs, tiles):
    n, m = lax.axis_size("sec"), lax.axis_size("tile")
    pairs = [
        (a * m + b, ((a + secs) % n) * m + (b + tiles) % m) for a in range(n) for b in range(m)
    ]
    return lax.ppermute(value, ("sec", "tile"), pairs)


def body(
    features, vote_grad, sharpness, valid_rows, first_kernel, first_bias, second_kernel, second_bias
):
    sec, tile = lax.axis_index("sec"), lax.axis_index("tile")
    info = jnp.stack(
        [tile * TR, tile, lax.axis_size("tile") - 1 - tile, sec, lax.axis_size("sec") - 1 - sec]
    ).astype(jnp.int32)

    prev = shift(features, 1, 0)
    top, bottom = edges(info, valid_rows, features, vote_grad)
    above = shift(bottom, 0, 1)
    below = shift(top, 0, -1)
    pabove = shift(bottom, 1, 1)
    pbelow = shift(top, 1, -1)

    k1 = first_kernel
    forward = k1.transpose(2, 0, 1, 3)
    wcur = forward[..., :CH].reshape(HID, 9 * CH)
    wear = forward[..., CH:].reshape(HID, 9 * CH)
    wboth = jnp.concatenate([wcur, wear], axis=0)
    backward = k1.transpose(1, 3, 0, 2)
    wgcur = backward[:, :CH].reshape(3 * CH, 3 * HID)
    wgear = backward[:, CH:].reshape(3 * CH, 3 * HID)
    wgboth = jnp.stack([backward[:, :CH], backward[:, CH:]], axis=3).reshape(3 * CH, 6 * HID)
    eye = jnp.eye(4, 3, dtype=BF16)
    w2 = second_kernel[:, :, None, :, None, :] * eye[None, None, :, None, :, None]
    w2f = w2.reshape(72, 3 * HID)
    w2b = jnp.pad(w2.reshape(3, 24, 3 * HID), ((0, 0), (0, 8), (0, 0))).reshape(96, 3 * HID).T
    bias = first_bias[:, None]
    bias2 = jnp.tile(second_bias, 4)[:, None]

    voted, low, own = main(
        info, valid_rows, sharpness,
        features, prev, above, below, pabove, pbelow, vote_grad,
        wcur, wear, wboth, bias, w2f, bias2, w2b, wgcur, wgear, wgboth,
    )
    back = shift(low, -1, 0)
    return (voted, finish(info, own, back))


def solution(mesh):
    return jax.shard_map(
        body,
        mesh=mesh,
        in_specs=(
            P("sec", None, "tile", None),
            P("sec", None, "tile", None),
            P("sec"),
            P("sec"),
            P(),
            P(),
            P(),
            P(),
        ),
        out_specs=(P("sec", None, "tile", None), P("sec", None, "tile", None)),
        check_vma=False,
    )
```

profile of v0, /device:TPU:0, one launch (start us, length us, event | category | flops | bytes accessed | tf_op | source)
XLA Modules:
  0.0 63.3 jit_solution(4687062788605264758)
XLA Ops:
  0.6 0.0 copy-start
  0.6 0.6 stack.32.info
  1.3 2.1 %edges.1 = (bf16[416,128]{1,0:T(8,128)(2,1)}, bf16[416,128]{1,0:T(8,128)(2,1)}) custom-call(s32[5]{0:T(128)} %stack.32.info, s32[3]{0:T(128)} %valid.3, bf16[3,32,16,128]{3,2,1,0:T(8,128)(2,1)} %feat.3, f32[3,2,16,128]{3,2,1,0:T(8,128)} %vgrad.3), custom_call_target="tpu_custom_call" | custom-call | tf_op jit(solution)/shard_map/edges/pallas_call | solution.py:65
  3.4 3.4 %collective-permute-start.3 = (bf16[416,128]{1,0:T(8,128)(2,1)}, bf16[416,128]{1,0:T(8,128)(2,1)S(1)}, u32[]{:S(2)}, u32[]{:S(2)}) collective-permute-start(bf16[416,128]{1,0:T(8,128)(2,1)} %get-tuple-element.7), channel_id=1, source_target_pairs={{0,5},{1,6},{2,7},{3,4},{4,9},{5,10},{6,11},{7,8},{8,13},{9,14},{1... | collective-permute-start | bytes 319496 | tf_op jit(solution)/shard_map/ppermute | solution.py:346
  6.8 0.8 %collective-permute-start.1 = (bf16[416,128]{1,0:T(8,128)(2,1)}, bf16[416,128]{1,0:T(8,128)(2,1)S(1)}, u32[]{:S(2)}, u32[]{:S(2)}) collective-permute-start(bf16[416,128]{1,0:T(8,128)(2,1)} %get-tuple-element.7), channel_id=1, source_target_pairs={{0,1},{1,2},{2,3},{3,0},{4,5},{5,6},{6,7},{7,4},{8,9},{9,10},{10,1... | collective-permute-start | bytes 319496 | tf_op jit(solution)/shard_map/ppermute | solution.py:346
  7.6 0.0 copy-start.10
  7.6 0.1 collective-permute-start.4
  7.7 1.4 %collective-permute-start.2 = (bf16[416,128]{1,0:T(8,128)(2,1)}, bf16[416,128]{1,0:T(8,128)(2,1)S(1)}, u32[]{:S(2)}, u32[]{:S(2)}) collective-permute-start(bf16[416,128]{1,0:T(8,128)(2,1)} %get-tuple-element.8), channel_id=1, source_target_pairs={{0,3},{1,0},{2,1},{3,2},{4,7},{5,4},{6,5},{7,6},{8,11},{9,8},{10,9... | collective-permute-start | bytes 319496 | tf_op jit(solution)/shard_map/ppermute | solution.py:346
  9.1 0.0 copy-done
  9.1 3.6 %collective-permute-start = (bf16[3,32,16,128]{3,2,1,0:T(8,128)(2,1)S(1)}, bf16[3,32,16,128]{3,2,1,0:T(8,128)(2,1)S(1)}, u32[]{:S(2)}, u32[]{:S(2)}) collective-permute-start(bf16[3,32,16,128]{3,2,1,0:T(8,128)(2,1)S(1)} %copy-done), channel_id=1, source_target_pairs={{0,4},{1,5},{2,6},{3,7},{4,8},{5,9},{6,10},{7,11},{8,12},{9,13},{1... | collective-permute-start | bytes 1179656 | tf_op jit(solution)/shard_map/ppermute | solution.py:346
  12.7 0.0 copy-done.10
  12.7 0.1 broadcast_in_dim_tile.4.bias2
  12.8 0.1 mul.37
  12.9 0.1 mul.38
  13.0 0.0 copy-start.9
  13.0 0.7 %copy-done.9 = f32[64]{0:T(128)S(1)} copy-done((f32[64]{0:T(128)S(1)}, f32[64]{0:T(128)}, u32[]{:S(2)}) %copy-start.9) | copy-done | bytes 280
  13.6 0.0 copy-start.8
  13.6 0.1 copy.29.bias
  13.7 0.6 copy-done.8
  14.3 0.1 broadcast_multiply_fusion
  14.4 0.1 mul.35.w2f
  14.5 0.1 mul.36
  14.7 0.0 copy-start.6
  14.7 0.1 copy.23
  14.8 0.8 %copy-done.6 = bf16[3,3,64,64]{3,2,1,0:T(8,128)(2,1)S(1)} copy-done((bf16[3,3,64,64]{3,2,1,0:T(8,128)(2,1)S(1)}, bf16[3,3,64,64]{3,2,1,0:T(8,128)(2,1)}, u32[]{:S(2)}) %copy-start.6) | copy-done | bytes 73752
  15.6 0.1 fusion.1
  15.7 0.1 copy.20
  15.8 0.1 copy.28.wear
  15.9 0.1 copy.19
  16.1 0.1 copy.27.wcur
  16.2 0.1 slice_bitcast_fusion.1
  16.3 0.1 pad_maximum_fusion
  16.4 0.2 copy.26
  16.5 0.2 reshape.44.wgboth
  16.7 0.1 copy.25
  16.8 0.1 reshape.43.wgear
  17.0 0.1 copy.24
  17.1 0.1 reshape.42.wgcur
  17.2 0.0 copy-start.2
  17.3 0.0 copy-start.3
  17.3 0.0 copy-start.4
  17.3 0.0 copy-start.5
  17.3 0.0 collective-permute-done.3.pabove
  17.3 0.0 collective-permute-done.1.above
  17.3 1.6 %collective-permute-done.4.pbelow = bf16[416,128]{1,0:T(8,128)(2,1)S(1)} collective-permute-done((bf16[416,128]{1,0:T(8,128)(2,1)}, bf16[416,128]{1,0:T(8,128)(2,1)S(1)}, u32[]{:S(2)}, u32[]{:S(2)}) %collective-permute-start.4) | collective-permute-done | bytes 106528 | tf_op jit(solution)/shard_map/ppermute | solution.py:346
  18.9 0.0 collective-permute-done.2.below
  18.9 8.4 %collective-permute-done.prev = bf16[3,32,16,128]{3,2,1,0:T(8,128)(2,1)S(1)} collective-permute-done((bf16[3,32,16,128]{3,2,1,0:T(8,128)(2,1)S(1)}, bf16[3,32,16,128]{3,2,1,0:T(8,128)(2,1)S(1)}, u32[]{:S(2)}, u32[]{:S(2)}) %collective-permute-start) | collective-permute-done | bytes 393248 | tf_op jit(solution)/shard_map/ppermute | solution.py:346
  27.3 0.0 copy-done.2
  27.4 0.0 copy-done.3
  27.4 0.0 copy-done.4
  27.4 0.0 copy-done.5
  27.4 19.1 %main.1 = (f32[3,2,16,128]{3,2,1,0:T(8,128)}, bf16[16,3,32,128]{3,2,1,0:T(8,128)(2,1)S(1)}, f32[16,3,32,128]{3,2,1,0:T(8,128)S(1)}) custom-call(s32[5]{0:T(128)S(1)} %copy-done.3, s32[3]{0:T(128)S(1)} %copy-done.4, f32[3]{0:T(128)S(1)} %copy-done.5, bf16[3,32,16,128]{3,2,1,0:T(8,128)(2,1)S(1)} %copy-done, ...), custom_call_target="tpu_custom_call" | custom-call | tf_op jit(solution)/shard_map/main/pallas_call | solution.py:291
  46.5 0.0 copy-start.1
  46.5 0.9 %copy-done.1 = f32[16,3,32,128]{3,2,1,0:T(8,128)} copy-done((f32[16,3,32,128]{3,2,1,0:T(8,128)}, f32[16,3,32,128]{3,2,1,0:T(8,128)S(1)}, u32[]{:S(2)}) %copy-start.1) | copy-done | bytes 786456
  47.3 2.1 %collective-permute-start.5 = (bf16[16,3,32,128]{3,2,1,0:T(8,128)(2,1)S(1)}, bf16[16,3,32,128]{3,2,1,0:T(8,128)(2,1)S(1)}, u32[]{:S(2)}, u32[]{:S(2)}) collective-permute-start(bf16[16,3,32,128]{3,2,1,0:T(8,128)(2,1)S(1)} %get-tuple-element.11), channel_id=1, source_target_pairs={{0,124},{1,125},{2,126},{3,127},{4,0},{5,1},{6,2},{7,3},{8,4},{9,5... | collective-permute-start | bytes 1179656 | tf_op jit(solution)/shard_map/ppermute | solution.py:346
  49.5 10.4 %collective-permute-done.5.back = bf16[16,3,32,128]{3,2,1,0:T(8,128)(2,1)S(1)} collective-permute-done((bf16[16,3,32,128]{3,2,1,0:T(8,128)(2,1)S(1)}, bf16[16,3,32,128]{3,2,1,0:T(8,128)(2,1)S(1)}, u32[]{:S(2)}, u32[]{:S(2)}) %collective-permute-start.5) | collective-permute-done | bytes 393248 | tf_op jit(solution)/shard_map/ppermute | solution.py:346
  59.9 0.0 copy-start.7
  59.9 0.8 %copy-done.7 = bf16[16,3,32,128]{3,2,1,0:T(8,128)(2,1)} copy-done((bf16[16,3,32,128]{3,2,1,0:T(8,128)(2,1)}, bf16[16,3,32,128]{3,2,1,0:T(8,128)(2,1)S(1)}, u32[]{:S(2)}) %copy-start.7) | copy-done | bytes 393240
  60.7 2.6 %finish.1 = f32[3,32,16,128]{3,2,1,0:T(8,128)} custom-call(s32[5]{0:T(128)} %stack.32.info, f32[16,3,32,128]{3,2,1,0:T(8,128)} %copy-done.1, bf16[16,3,32,128]{3,2,1,0:T(8,128)(2,1)} %copy-done.7), custom_call_target="tpu_custom_call" | custom-call | tf_op jit(solution)/shard_map/finish/pallas_call | solution.py:332
  (6 shorter events, 0.1 us)
Async XLA Ops:
  0.6 8.5 %copy-start = (bf16[3,32,16,128]{3,2,1,0:T(8,128)(2,1)S(1)}, bf16[3,32,16,128]{3,2,1,0:T(8,128)(2,1)}, u32[]{:S(2)}) copy-start(bf16[3,32,16,128]{3,2,1,0:T(8,128)(2,1)} %feat.3) | copy-start | bytes 1179652
  3.4 13.9 %collective-permute-start.3 = (bf16[416,128]{1,0:T(8,128)(2,1)}, bf16[416,128]{1,0:T(8,128)(2,1)S(1)}, u32[]{:S(2)}, u32[]{:S(2)}) collective-permute-start(bf16[416,128]{1,0:T(8,128)(2,1)} %get-tuple-element.7), channel_id=1, source_target_pairs={{0,5},{1,6},{2,7},{3,4},{4,9},{5,10},{6,11},{7,8},{8,13},{9,14},{1... | collective-permute-start | bytes 319496 | tf_op jit(solution)/shard_map/ppermute | solution.py:346
  6.8 10.5 %collective-permute-start.1 = (bf16[416,128]{1,0:T(8,128)(2,1)}, bf16[416,128]{1,0:T(8,128)(2,1)S(1)}, u32[]{:S(2)}, u32[]{:S(2)}) collective-permute-start(bf16[416,128]{1,0:T(8,128)(2,1)} %get-tuple-element.7), channel_id=1, source_target_pairs={{0,1},{1,2},{2,3},{3,0},{4,5},{5,6},{6,7},{7,4},{8,9},{9,10},{10,1... | collective-permute-start | bytes 319496 | tf_op jit(solution)/shard_map/ppermute | solution.py:346
  7.6 5.1 %copy-start.10 = (f32[2]{0:T(128)S(1)}, f32[2]{0:T(128)}, u32[]{:S(2)}) copy-start(f32[2]{0:T(128)} %param.15) | copy-start | bytes 28
  7.6 11.3 %collective-permute-start.4 = (bf16[416,128]{1,0:T(8,128)(2,1)}, bf16[416,128]{1,0:T(8,128)(2,1)S(1)}, u32[]{:S(2)}, u32[]{:S(2)}) collective-permute-start(bf16[416,128]{1,0:T(8,128)(2,1)} %get-tuple-element.8), channel_id=1, source_target_pairs={{0,7},{1,4},{2,5},{3,6},{4,11},{5,8},{6,9},{7,10},{8,15},{9,12},{1... | collective-permute-start | bytes 319496 | tf_op jit(solution)/shard_map/ppermute | solution.py:346
  7.7 11.2 %collective-permute-start.2 = (bf16[416,128]{1,0:T(8,128)(2,1)}, bf16[416,128]{1,0:T(8,128)(2,1)S(1)}, u32[]{:S(2)}, u32[]{:S(2)}) collective-permute-start(bf16[416,128]{1,0:T(8,128)(2,1)} %get-tuple-element.8), channel_id=1, source_target_pairs={{0,3},{1,0},{2,1},{3,2},{4,7},{5,4},{6,5},{7,6},{8,11},{9,8},{10,9... | collective-permute-start | bytes 319496 | tf_op jit(solution)/shard_map/ppermute | solution.py:346
  9.1 18.2 %collective-permute-start = (bf16[3,32,16,128]{3,2,1,0:T(8,128)(2,1)S(1)}, bf16[3,32,16,128]{3,2,1,0:T(8,128)(2,1)S(1)}, u32[]{:S(2)}, u32[]{:S(2)}) collective-permute-start(bf16[3,32,16,128]{3,2,1,0:T(8,128)(2,1)S(1)} %copy-done), channel_id=1, source_target_pairs={{0,4},{1,5},{2,6},{3,7},{4,8},{5,9},{6,10},{7,11},{8,12},{9,13},{1... | collective-permute-start | bytes 1179656 | tf_op jit(solution)/shard_map/ppermute | solution.py:346
  13.0 0.7 %copy-start.9 = (f32[64]{0:T(128)S(1)}, f32[64]{0:T(128)}, u32[]{:S(2)}) copy-start(f32[64]{0:T(128)} %param.13) | copy-start | bytes 772
  13.6 0.7 %copy-start.8 = (bf16[3,3,2,64]{3,2,1,0:T(2,128)(2,1)S(1)}, bf16[3,3,2,64]{3,2,1,0:T(2,128)(2,1)}, u32[]{:S(2)}) copy-start(bf16[3,3,2,64]{3,2,1,0:T(2,128)(2,1)} %param.14) | copy-start | bytes 6916
  14.7 0.9 %copy-start.6 = (bf16[3,3,64,64]{3,2,1,0:T(8,128)(2,1)S(1)}, bf16[3,3,64,64]{3,2,1,0:T(8,128)(2,1)}, u32[]{:S(2)}) copy-start(bf16[3,3,64,64]{3,2,1,0:T(8,128)(2,1)} %param.12) | copy-start | bytes 221188
  17.2 10.1 %copy-start.2 = (f32[3,2,16,128]{3,2,1,0:T(8,128)S(1)}, f32[3,2,16,128]{3,2,1,0:T(8,128)}, u32[]{:S(2)}) copy-start(f32[3,2,16,128]{3,2,1,0:T(8,128)} %vgrad.3) | copy-start | bytes 147460
  17.3 10.1 %copy-start.3 = (s32[5]{0:T(128)S(1)}, s32[5]{0:T(128)}, u32[]{:S(2)}) copy-start(s32[5]{0:T(128)} %stack.32.info) | copy-start | bytes 64
  17.3 10.1 %copy-start.4 = (s32[3]{0:T(128)S(1)}, s32[3]{0:T(128)}, u32[]{:S(2)}) copy-start(s32[3]{0:T(128)} %valid.3) | copy-start | bytes 40
  17.3 10.1 %copy-start.5 = (f32[3]{0:T(128)S(1)}, f32[3]{0:T(128)}, u32[]{:S(2)}) copy-start(f32[3]{0:T(128)} %sharp.1) | copy-start | bytes 40
  46.5 0.9 %copy-start.1 = (f32[16,3,32,128]{3,2,1,0:T(8,128)}, f32[16,3,32,128]{3,2,1,0:T(8,128)S(1)}, u32[]{:S(2)}) copy-start(f32[16,3,32,128]{3,2,1,0:T(8,128)S(1)} %get-tuple-element.10.own) | copy-start | bytes 2359300
  47.3 12.5 %collective-permute-start.5 = (bf16[16,3,32,128]{3,2,1,0:T(8,128)(2,1)S(1)}, bf16[16,3,32,128]{3,2,1,0:T(8,128)(2,1)S(1)}, u32[]{:S(2)}, u32[]{:S(2)}) collective-permute-start(bf16[16,3,32,128]{3,2,1,0:T(8,128)(2,1)S(1)} %get-tuple-element.11), channel_id=1, source_target_pairs={{0,124},{1,125},{2,126},{3,127},{4,0},{5,1},{6,2},{7,3},{8,4},{9,5... | collective-permute-start | bytes 1179656 | tf_op jit(solution)/shard_map/ppermute | solution.py:346
  59.9 0.8 %copy-start.7 = (bf16[16,3,32,128]{3,2,1,0:T(8,128)(2,1)}, bf16[16,3,32,128]{3,2,1,0:T(8,128)(2,1)S(1)}, u32[]{:S(2)}) copy-start(bf16[16,3,32,128]{3,2,1,0:T(8,128)(2,1)S(1)} %collective-permute-done.5.back) | copy-start | bytes 1179652
where the time goes:
time: 63.6 us; the launch traced here: 63.3 us
  Pallas kernels  23.8 us (37%)
  waiting for transfers between devices  20.5 us (32%)
  starting transfers between devices  11.4 us (18%)
  local copies, waits for them, and re-layouts  6.59 us (10%)
  between operations  0.81 us (1%)
    ppermute x6, waiting for transfers between devices, shift(): return lax.ppermute(value, ('sec', 'tile'), pairs)  20.5 us
    pallas_call x1, Pallas kernels, main(): pl.pallas_call(main_kernel, out_shape=(jax.ShapeDtypeStruct((OWN, 2, TR,...  19.1 us
    ppermute x6, starting transfers between devices, shift(): return lax.ppermute(value, ('sec', 'tile'), pairs)  11.4 us
    unnamed x22, local copies, waits for them, and re-layouts  3.7 us
    pallas_call x1, Pallas kernels, finish(): pl.pallas_call(finish_kernel, out_shape=jax.ShapeDtypeStruct((OWN, CH, TR...  2.63 us
    pallas_call x1, Pallas kernels, edges(): pl.pallas_call(edges_kernel, out_shape=(shape, shape), in_specs=[smem, sm...  2.12 us
  transfers between devices with their start and end apart: 6, of which 3 were waited for; matrix products, arithmetic and copies ran while one was open for 4% of the time, Pallas kernels for 0%

commit v1 on v0

v1 whole, which is shorter than its diff:
```python
import jax
import jax.numpy as jnp
from jax import lax
from jax.experimental import pallas as pl
from jax.experimental.pallas import tpu as pltpu
from jax.sharding import PartitionSpec as P

F32 = jnp.float32
BF16 = jnp.bfloat16
OWN = 3
CH = 32
HID = 64
TR = 16
COLS = 128
HALO = 4
FEAT_ROWS = TR + 2 * HALO
HID_ROWS = FEAT_ROWS - 2
FLD_ROWS = FEAT_ROWS - 4
DH_ROWS = FEAT_ROWS - 6
EDGE = HALO * OWN * CH
EDGE_ALL = EDGE + 32


def lane(shape):
    return lax.broadcasted_iota(jnp.int32, shape, len(shape) - 1)


def from_left(x):
    return jnp.where(lane(x.shape) == 0, 0.0, pltpu.roll(x, 1, x.ndim - 1))


def from_right(x):
    return jnp.where(lane(x.shape) == COLS - 1, 0.0, pltpu.roll(x, COLS - 1, x.ndim - 1))


def dot(a, b):
    return jnp.dot(a, b, preferred_element_type=F32)


def params(mib):
    return pltpu.CompilerParams(vmem_limit_bytes=mib << 20)


def call(kernel, outs, scratch, mib, name, scalars, *args):
    smem = pl.BlockSpec(memory_space=pltpu.SMEM)
    vmem = pl.BlockSpec(memory_space=pltpu.VMEM)
    return pl.pallas_call(
        kernel,
        out_shape=tuple(jax.ShapeDtypeStruct(shape, kind) for shape, kind in outs),
        in_specs=[smem] * scalars + [vmem] * (len(args) - scalars),
        out_specs=(vmem,) * len(outs),
        scratch_shapes=[pltpu.VMEM(shape, kind) for shape, kind in scratch],
        compiler_params=params(mib),
        cost_estimate=pl.CostEstimate(flops=0, bytes_accessed=0, transcendentals=0),
        name=name,
    )(*args)


def first_row():
    return lax.axis_index("tile") * TR


def has_tiles():
    tile = lax.axis_index("tile")
    return (tile > 0).astype(F32), (tile < lax.axis_size("tile") - 1).astype(F32)


def edges_kernel(valid, feat, vgrad, top, bottom, wide, ext):
    row0 = first_row()
    for out, cot_first in ((top, 0), (bottom, TR - 2)):
        ext[...] = jnp.zeros((32, COLS), F32)
        for s in range(OWN):
            pos = row0 + cot_first + lax.broadcasted_iota(jnp.int32, (2, COLS), 0)
            for c in range(2):
                cot = jnp.where(pos < valid[s], vgrad[s, c, cot_first : cot_first + 2, :], 0.0)
                high = cot.astype(BF16).astype(F32)
                at = s * 4 + c * 2
                ext[at : at + 2, :] = high
                ext[12 + at : 14 + at, :] = cot - high
        out[EDGE:, :] = ext[...].astype(BF16)
    for s in range(OWN):
        wide[s] = feat[s].astype(F32)
    for s in range(OWN):
        for out, first in ((top, 0), (bottom, TR - HALO)):
            for r in range(HALO):
                at = (r * OWN + s) * CH
                out[at : at + CH, :] = wide[s, :, first + r, :].astype(BF16)


def edges(valid, feat, vgrad):
    return call(
        edges_kernel,
        [((EDGE_ALL, COLS), BF16)] * 2,
        [((OWN, CH, TR, COLS), F32), ((32, COLS), F32)],
        4,
        "edges",
        1,
        valid,
        feat,
        vgrad,
    )


def weights_kernel(
    k1, k2, wcur, wear, wboth, w2own, w2first, w2rest, w2b, w2brest, wgear, wgcur, wgboth,
    fwd, bwd, both, two, sq,
):
    for dy in range(3):
        for dx in range(3):
            k = k1[dy, dx].astype(F32)
            t = CH * (3 * dy + dx)
            fwd[0:HID, t : t + CH] = k[:, :CH]
            fwd[HID:, t : t + CH] = k[:, CH:]
            kt = k.T
            rows = slice(CH * dx, CH * dx + CH)
            bwd[rows, HID * dy : HID * dy + HID] = kt[:CH]
            bwd[3 * CH + CH * dx : 4 * CH + CH * dx, HID * dy : HID * dy + HID] = kt[CH:]
            both[rows, 2 * HID * dy : 2 * HID * dy + HID] = kt[:CH]
            both[rows, 2 * HID * dy + HID : 2 * HID * dy + 2 * HID] = kt[CH:]
    wcur[...] = fwd[0:HID, :].astype(BF16)
    wear[...] = fwd[HID:, :].astype(BF16)
    wboth[...] = fwd[...].astype(BF16)
    wgcur[...] = bwd[0 : 3 * CH, :].astype(BF16)
    wgear[...] = bwd[3 * CH :, :].astype(BF16)
    wgboth[...] = both[...].astype(BF16)

    def put(ref, row, col, lags):
        for i, lag in enumerate(lags):
            for dy in range(3):
                for dx in range(3):
                    at = row + 8 * (3 * dy + dx) + 2 * lag
                    c = col + HID * i
                    ref[at : at + 2, c : c + HID] = k2[dy, dx].astype(F32)

    two[...] = jnp.zeros(two.shape, F32)
    put(two, 0, 0, (0, 1, 2))
    w2first[...] = two[0:72, :].astype(BF16)
    two[...] = jnp.zeros(two.shape, F32)
    put(two, 0, 0, (1, 2))
    put(two, 72, 2 * HID, (2,))
    w2rest[...] = two[...].astype(BF16)
    two[...] = jnp.zeros(two.shape, F32)
    put(two, 0, 0, (0,))
    put(two, 72, HID, (0, 1))
    w2own[...] = two[...].astype(BF16)

    def lay(row, col, lags):
        for i, lag in enumerate(lags):
            for dy in range(3):
                for dx in range(3):
                    at = row + 32 * dy + 8 * dx + 2 * lag
                    c = col + HID * i
                    sq[at : at + 2, c : c + HID] = k2[dy, dx].astype(F32)

    sq[...] = jnp.zeros(sq.shape, F32)
    lay(0, 0, (0, 1, 2))
    w2b[...] = sq[0:96, :].T.astype(BF16)
    sq[...] = jnp.zeros(sq.shape, F32)
    lay(0, 0, (1, 2))
    lay(96, 2 * HID, (2,))
    w2brest[...] = sq[...].T.astype(BF16)


def weights(k1, k2):
    return call(
        weights_kernel,
        [
            ((HID, 9 * CH), BF16),
            ((HID, 9 * CH), BF16),
            ((2 * HID, 9 * CH), BF16),
            ((144, 192), BF16),
            ((72, 192), BF16),
            ((144, 192), BF16),
            ((192, 96), BF16),
            ((192, 192), BF16),
            ((3 * CH, 3 * HID), BF16),
            ((3 * CH, 3 * HID), BF16),
            ((3 * CH, 6 * HID), BF16),
        ],
        [
            ((2 * HID, 9 * CH), F32),
            ((6 * CH, 3 * HID), F32),
            ((3 * CH, 6 * HID), F32),
            ((144, 192), F32),
            ((192, 192), F32),
        ],
        4,
        "weights",
        0,
        k1,
        k2,
    )


def spread_row(x, xd, j, r):
    xd[j, r, 0:CH, :] = from_left(x).astype(BF16)
    xd[j, r, CH : 2 * CH, :] = x.astype(BF16)
    xd[j, r, 2 * CH :, :] = from_right(x).astype(BF16)


def spread(feat, above, below, keep, has, xd, wide):
    for s in range(OWN):
        x = feat[s].astype(F32)
        wide[s] = x if keep is None else x * keep
    scale = has if keep is None else [keep * h for h in has]
    for s in range(OWN):
        for r in range(TR):
            spread_row(wide[s, :, r, :], xd, s, HALO + r)
        for r in range(HALO):
            at = (r * OWN + s) * CH
            spread_row(above[at : at + CH, :].astype(F32) * scale[0], xd, s, r)
            spread_row(below[at : at + CH, :].astype(F32) * scale[1], xd, s, HALO + TR + r)


def taps(rows, pick):
    return jnp.concatenate(
        [jnp.concatenate([pick(r), pick(r + 1)], axis=1) for r in rows], axis=0
    )


def halves(ref, r, first, x):
    n = x.shape[0]
    ref[r, first : first + n, :] = x[:, :COLS]
    ref[r + 1, first : first + n, :] = x[:, COLS:]


def pair_row(ref, r, first, n):
    return jnp.concatenate(
        [ref[r, first : first + n, :], ref[r + 1, first : first + n, :]], axis=1
    )


def gather_columns(p):
    return from_right(p[:CH]) + p[CH : 2 * CH] + from_left(p[2 * CH :])


def own_kernel(
    valid, feat, above, below, vgrad, wcur, wboth, bias, w2own,
    cur, hown, town, cot,
    wide, xd,
):
    row0 = first_row()
    has = has_tiles()
    ends = [
        (above[EDGE:, :].astype(F32) * has[0], 0),
        (below[EDGE:, :].astype(F32) * has[1], TR + 2),
    ]
    for s in range(OWN):
        for c in range(2):
            at = s * 4 + c * 2
            for ext, first in ends:
                cot[s, c, first : first + 2, :] = ext[at : at + 2] + ext[12 + at : 14 + at]
            pos = row0 + lax.broadcasted_iota(jnp.int32, (TR, COLS), 0)
            cot[s, c, 2 : 2 + TR, :] = jnp.where(pos < valid[s], vgrad[s, c], 0.0)
    spread(feat, above, below, None, has, xd, wide)

    def step(i, carry):
        r = 2 * i
        rhs = [taps((r, r + 1, r + 2), lambda q, j=j: xd[j, q]) for j in range(OWN)]
        ear = []
        for j in range(2):
            both = dot(wboth[...], rhs[j])
            halves(cur, r, HID * j, both[:HID] + bias[...])
            ear.append(both[HID:])
            if j == 1:
                mid = both[:HID] + bias[...]
        last = dot(wcur[...], rhs[2]) + bias[...]
        halves(cur, r, 2 * HID, last)
        h = jnp.concatenate(
            [jnp.maximum(mid + ear[0], 0.0), jnp.maximum(last + ear[1], 0.0),
             jnp.maximum(last + ear[0], 0.0)],
            axis=0,
        ).astype(BF16)
        halves(hown, r, 0, h)
        halves(town, r, 0, dot(w2own[...], h))
        return carry

    lax.fori_loop(0, HID_ROWS // 2, step, 0, unroll=True)


def own(valid, *args):
    return call(
        own_kernel,
        [
            ((HID_ROWS, OWN * HID, COLS), F32),
            ((HID_ROWS, 3 * HID, COLS), BF16),
            ((HID_ROWS, 144, COLS), F32),
            ((OWN, 2, 24, COLS), F32),
        ],
        [((OWN, CH, TR, COLS), F32), ((OWN, FEAT_ROWS, 3 * CH, COLS), BF16)],
        8,
        "own",
        1,
        valid,
        *args,
    )


def fields_stage(hmid, town, w2first, w2rest, bias2, has, tsum, fld):
    def step(i, carry):
        r = 2 * i
        halves(tsum, r, 0, dot(w2first[...], pair_row(hmid, r, 0, 192)))
        rest = dot(w2rest[...], pair_row(hmid, r, 192, 192))
        halves(tsum, r, 72, rest + pair_row(town, r, 0, 144))
        return carry

    lax.fori_loop(0, HID_ROWS // 2, step, 0, unroll=True)
    for r in range(FLD_ROWS):
        for s in range(OWN):
            sums = []
            for dx in range(3):
                terms = []
                for dy in range(3):
                    at = 72 * s + 8 * (3 * dy + dx)
                    t = tsum[r + dy, at : at + 8, :]
                    if r + dy < 3:
                        t = t * has[0]
                    elif r + dy > HID_ROWS - 4:
                        t = t * has[1]
                    terms.append(t)
                sums.append(terms[0] + terms[1] + terms[2])
            fld[s, r] = (sums[1] + bias2[...]) + (from_left(sums[0]) + from_right(sums[2]))


def vote_stage(sharp, cot, fld, grd, g3, votes):
    for s in range(OWN):
        f = [[fld[s, :, 2 * k + c, :] for c in range(2)] for k in range(3)]
        beta = sharp[s]
        diff = {}
        dist = {}
        for a, b in ((0, 1), (0, 2), (1, 2)):
            diff[a, b] = [f[a][c] - f[b][c] for c in range(2)]
            dist[a, b] = diff[a, b][0] * diff[a, b][0] + diff[a, b][1] * diff[a, b][1]
        score = [dist[0, 1] + dist[0, 2], dist[0, 1] + dist[1, 2], dist[0, 2] + dist[1, 2]]
        logit = [-beta * q for q in score]
        top = jnp.maximum(jnp.maximum(logit[0], logit[1]), logit[2])
        expo = [jnp.exp(q - top) for q in logit]
        inv = 1.0 / (expo[0] + expo[1] + expo[2])
        w = [q * inv for q in expo]
        v = [w[0] * f[0][c] + w[1] * f[1][c] + w[2] * f[2][c] for c in range(2)]
        for c in range(2):
            votes[s, c, 0:FLD_ROWS, :] = v[c]
        g = [cot[s, c, 0:FLD_ROWS, :] for c in range(2)]
        e = [
            -beta * w[k] * (g[0] * (f[k][0] - v[0]) + g[1] * (f[k][1] - v[1])) for k in range(3)
        ]
        pair = {key: 2.0 * (e[key[0]] + e[key[1]]) for key in diff}
        for c in range(2):
            m01 = pair[0, 1] * diff[0, 1][c]
            m02 = pair[0, 2] * diff[0, 2][c]
            m12 = pair[1, 2] * diff[1, 2][c]
            grd[s, :, 0 + c, :] = w[0] * g[c] + m01 + m02
            grd[s, :, 2 + c, :] = w[1] * g[c] - m01 + m12
            grd[s, :, 4 + c, :] = w[2] * g[c] - m02 - m12
        grd[s, :, 6, :] = jnp.zeros((FLD_ROWS, COLS), F32)
        grd[s, :, 7, :] = jnp.zeros((FLD_ROWS, COLS), F32)
    for r in range(FLD_ROWS):
        for s in range(OWN):
            x = grd[s, r]
            g3[s, r] = jnp.concatenate(
                [from_right(x), x, from_left(x), jnp.zeros_like(x)], axis=0
            ).astype(BF16)


def inside(ref, has):
    for r, h in ((0, has[0]), (DH_ROWS - 1, has[1])):
        ref[r] = (ref[r].astype(F32) * h).astype(BF16)


def low_grad_stage(w2b, w2brest, g3, hmid, has, dlow):
    def step(i, carry):
        q = 2 * i
        rhs = [taps((q + 2, q + 1, q), lambda r, s=s: g3[s, r]) for s in range(OWN)]
        h = [pair_row(hmid, q + 2, 192 * j, 192).astype(F32) for j in range(2)]
        first = jnp.where(h[0] > 0.0, dot(w2b[...], rhs[0]), 0.0)
        rest = jnp.where(
            h[1] > 0.0, dot(w2brest[...], jnp.concatenate([rhs[1], rhs[2]], axis=0)), 0.0
        )
        low = jnp.concatenate(
            [
                first[2 * HID :],
                first[HID : 2 * HID] + rest[HID : 2 * HID],
                first[:HID] + rest[:HID] + rest[2 * HID :],
            ],
            axis=0,
        ).astype(BF16)
        halves(dlow, q, 0, low)
        return carry

    lax.fori_loop(0, DH_ROWS // 2, step, 0, unroll=True)
    inside(dlow, has)


def feature_grad_stage(dref, jobs):
    def step(i, carry):
        r = 2 * i
        for first, size, weight, out, s in jobs:
            rhs = taps((r + 2, r + 1, r), lambda q: dref[q, first : first + size, :])
            p = dot(weight[...], rhs)
            for d in range(2):
                out[r + d, s] = gather_columns(p[:, COLS * d : COLS * d + COLS]).astype(out.dtype)
        return carry

    lax.fori_loop(0, TR // 2, step, 0, unroll=True)


def borrowed_kernel(
    sharp, prev, pabove, pbelow, cur, town, cot, wear, w2first, w2rest, bias2, w2b, w2brest, wgear,
    low, hmid, g3, votes,
    wide, xd, tsum, fld, grd, dlow,
):
    has = has_tiles()
    keep = (lax.axis_index("sec") > 0).astype(F32)
    spread(prev, pabove, pbelow, keep, has, xd, wide)

    def step(i, carry):
        r = 2 * i
        ear = [
            dot(wear[...], taps((r, r + 1, r + 2), lambda q, j=j: xd[j, q])) for j in range(OWN)
        ]
        c = pair_row(cur, r, 0, OWN * HID)
        c = [c[HID * s : HID * s + HID] for s in range(OWN)]
        h = jnp.concatenate(
            [
                jnp.maximum(c[s] + ear[3 + s - k], 0.0)
                for s, k in ((0, 1), (0, 2), (0, 3), (1, 2), (1, 3), (2, 3))
            ],
            axis=0,
        ).astype(BF16)
        halves(hmid, r, 0, h)
        return carry

    lax.fori_loop(0, HID_ROWS // 2, step, 0, unroll=True)
    fields_stage(hmid, town, w2first, w2rest, bias2, has, tsum, fld)
    vote_stage(sharp, cot, fld, grd, g3, votes)
    low_grad_stage(w2b, w2brest, g3, hmid, has, dlow)
    feature_grad_stage(dlow, [(64 * s, 64, wgear, low, s) for s in range(OWN)])


def borrowed(sharp, *args):
    return call(
        borrowed_kernel,
        [
            ((TR, OWN, CH, COLS), BF16),
            ((HID_ROWS, 6 * HID, COLS), BF16),
            ((OWN, FLD_ROWS, 32, COLS), BF16),
            ((OWN, 2, 24, COLS), F32),
        ],
        [
            ((OWN, CH, TR, COLS), F32),
            ((OWN, FEAT_ROWS, 3 * CH, COLS), BF16),
            ((HID_ROWS, OWN * 72, COLS), F32),
            ((OWN, FLD_ROWS, 8, COLS), F32),
            ((OWN, FLD_ROWS, 8, COLS), F32),
            ((DH_ROWS, 3 * HID, COLS), BF16),
        ],
        12,
        "borrowed",
        1,
        sharp,
        *args,
    )


def own_grad_kernel(votes, g3, hown, hmid, w2b, wgcur, wgboth, voted, grad, down):
    has = has_tiles()
    for s in range(OWN):
        for c in range(2):
            voted[s, c] = votes[s, c, 2 : 2 + TR, :]

    def step(i, carry):
        q = 2 * i
        ho = pair_row(hown, q + 2, 0, 192)
        hm = pair_row(hmid, q + 2, 0, 384)
        h = [
            hm[:192],
            jnp.concatenate([ho[:64], hm[192:320]], axis=0),
            jnp.concatenate([ho[64:], hm[320:]], axis=0),
        ]
        m = []
        for s in range(OWN):
            dh = dot(w2b[...], taps((q + 2, q + 1, q), lambda r, s=s: g3[s, r]))
            dh = jnp.where(h[s].astype(F32) > 0.0, dh, 0.0)
            m.append([dh[HID * k : HID * k + HID] for k in range(3)])
        c = [m[s][0] + m[s][1] + m[s][2] for s in range(OWN)]
        d = jnp.concatenate([c[0], m[1][0] + m[2][1], c[1], m[2][0], c[2]], axis=0).astype(BF16)
        halves(down, q, 0, d)
        return carry

    lax.fori_loop(0, DH_ROWS // 2, step, 0, unroll=3)
    inside(down, has)
    feature_grad_stage(
        down, [(0, 128, wgboth, grad, 0), (128, 128, wgboth, grad, 1), (256, 64, wgcur, grad, 2)]
    )


def own_grad(*args):
    return call(
        own_grad_kernel,
        [((OWN, 2, TR, COLS), F32), ((TR, OWN, CH, COLS), F32)],
        [((DH_ROWS, 5 * HID, COLS), BF16)],
        6,
        "own_grad",
        0,
        *args,
    )


def finish_kernel(grad, back, out):
    keep = (lax.axis_index("sec") < lax.axis_size("sec") - 1).astype(F32)
    for s in range(OWN):
        for r in range(TR):
            out[s, :, r, :] = grad[r, s] + back[r, s].astype(F32) * keep


def finish(grad, back):
    return call(finish_kernel, [((OWN, CH, TR, COLS), F32)], [], 4, "finish", 0, grad, back)[0]


def shift(value, secs, tiles):
    n, m = lax.axis_size("sec"), lax.axis_size("tile")
    pairs = [
        (a * m + b, ((a + secs) % n) * m + (b + tiles) % m) for a in range(n) for b in range(m)
    ]
    return lax.ppermute(value, ("sec", "tile"), pairs)


def body(
    features, vote_grad, sharpness, valid_rows, first_kernel, first_bias, second_kernel, second_bias
):
    prev = shift(features, 1, 0)
    top, bottom = edges(valid_rows, features, vote_grad)
    above = shift(bottom, 0, 1)
    below = shift(top, 0, -1)
    pabove = shift(bottom, 1, 1)
    pbelow = shift(top, 1, -1)
    (
        wcur, wear, wboth, w2own, w2first, w2rest, w2b, w2brest, wgear, wgcur, wgboth,
    ) = weights(first_kernel, second_kernel)
    bias = first_bias[:, None]
    bias2 = jnp.tile(second_bias, 4)[:, None]
    cur, hown, town, cot = own(
        valid_rows, features, above, below, vote_grad, wcur, wboth, bias, w2own
    )
    low, hmid, g3, votes = borrowed(
        sharpness, prev, pabove, pbelow, cur, town, cot,
        wear, w2first, w2rest, bias2, w2b, w2brest, wgear,
    )
    back = shift(low, -1, 0)
    voted, grad = own_grad(votes, g3, hown, hmid, w2b, wgcur, wgboth)
    return (voted, finish(grad, back))


def solution(mesh):
    return jax.shard_map(
        body,
        mesh=mesh,
        in_specs=(
            P("sec", None, "tile", None),
            P("sec", None, "tile", None),
            P("sec"),
            P("sec"),
            P(),
            P(),
            P(),
            P(),
        ),
        out_specs=(P("sec", None, "tile", None), P("sec", None, "tile", None)),
        check_vma=False,
    )
```

time: 63.6 us -> 50.1 us (0.79)
  waiting for transfers between devices: 20.5 us -> 6.23 us
  Pallas kernels: 23.8 us -> 15.7 us
  starting transfers between devices: 11.4 us -> 18.2 us
  local copies, waits for them, and re-layouts: 6.59 us -> 8.65 us
    ppermute x6, waiting for transfers between devices: 20.5 us -> 6.23 us  [shift(): return lax.ppermute(value, ('sec', 'tile'), pairs)]
    pallas_call x3 -> x6, Pallas kernels: 23.8 us -> 15.7 us  [call(): pl.pallas_call(kernel, out_shape=tuple((jax.ShapeDtypeStruct(shape, kind)...]
    ppermute x6, starting transfers between devices: 11.4 us -> 18.2 us  [shift(): return lax.ppermute(value, ('sec', 'tile'), pairs)]
    unnamed x22 -> x18, local copies, waits for them, and re-layouts: 3.7 us -> 7.17 us
    another operation x3 -> x0, local copies, waits for them, and re-layouts: 0.91 us -> none  [the longest x1 0.63 us: body(): jnp.stack([tile * TR, tile, lax.axis_size('tile') - 1 - tile, sec, lax.ax...]
    reshape x6 -> x0, local copies, waits for them, and re-layouts: 0.71 us -> none  [the longest x1 0.15 us: body(): jnp.stack([backward[:, :CH], backward[:, CH:]], axis=3)]
    slice x5 -> x0, local copies, waits for them, and re-layouts: 0.66 us -> none  [the longest x2 0.24 us: body(): wear = forward[..., CH:].reshape(HID, 9 * CH)]
    another operation x2, local copies, waits for them, and re-layouts: 0.08 us -> 0.73 us  [body(): bias2 = jnp.tile(second_bias, 4)[:, None]]
  transfers between devices with their start and end apart: 6 -> 6, of which waited for: 3 -> 1; matrix products, arithmetic and copies ran while one was open for 4% -> 3% of each run, Pallas kernels for 0% -> 18%
where the time goes in v1:
time: 50.1 us; the launch traced here: 49.5 us
  starting transfers between devices  18.2 us (36%)
  Pallas kernels  15.7 us (31%)
  local copies, waits for them, and re-layouts  8.65 us (17%)
  waiting for transfers between devices  6.23 us (12%)
  between operations  0.73 us (1%)
    ppermute x6, starting transfers between devices, shift(): return lax.ppermute(value, ('sec', 'tile'), pairs)  18.2 us
    pallas_call x6, Pallas kernels, call(): pl.pallas_call(kernel, out_shape=tuple((jax.ShapeDtypeStruct(shape, kind)...  15.7 us
    unnamed x18, local copies, waits for them, and re-layouts  7.17 us
    ppermute x6, waiting for transfers between devices, shift(): return lax.ppermute(value, ('sec', 'tile'), pairs)  6.23 us
  transfers between devices with their start and end apart: 6, of which 1 were waited for; matrix products, arithmetic and copies ran while one was open for 3% of the time, Pallas kernels for 18%

profile of v1, /device:TPU:0, one launch (start us, length us, event | category | flops | bytes accessed | tf_op | source)
XLA Modules:
  0.0 49.5 jit_solution(6858905545936484337)
XLA Ops:
  0.6 4.0 %collective-permute-start = (bf16[3,32,16,128]{3,2,1,0:T(8,128)(2,1)}, bf16[3,32,16,128]{3,2,1,0:T(8,128)(2,1)S(1)}, u32[]{:S(2)}, u32[]{:S(2)}) collective-permute-start(bf16[3,32,16,128]{3,2,1,0:T(8,128)(2,1)} %feat.3), channel_id=1, source_target_pairs={{0,4},{1,5},{2,6},{3,7},{4,8},{5,9},{6,10},{7,11},{8,12},{9,13},{1... | collective-permute-start | bytes 1179656 | tf_op jit(solution)/shard_map/ppermute | solution.py:525
  4.7 0.0 copy-start
  4.7 1.0 %copy-done = bf16[3,32,16,128]{3,2,1,0:T(8,128)(2,1)S(1)} copy-done((bf16[3,32,16,128]{3,2,1,0:T(8,128)(2,1)S(1)}, bf16[3,32,16,128]{3,2,1,0:T(8,128)(2,1)}, u32[]{:S(2)}) %copy-start) | copy-done | bytes 393240
  5.7 0.0 copy-start.2
  5.7 0.8 %copy-done.2 = f32[3,2,16,128]{3,2,1,0:T(8,128)S(1)} copy-done((f32[3,2,16,128]{3,2,1,0:T(8,128)S(1)}, f32[3,2,16,128]{3,2,1,0:T(8,128)}, u32[]{:S(2)}) %copy-start.2) | copy-done | bytes 49176
  6.5 0.0 copy-start.6
  6.5 0.7 %copy-done.6 = s32[3]{0:T(128)S(1)} copy-done((s32[3]{0:T(128)S(1)}, s32[3]{0:T(128)}, u32[]{:S(2)}) %copy-start.6) | copy-done | bytes 36
  7.1 1.0 %edges.1 = (bf16[416,128]{1,0:T(8,128)(2,1)S(1)}, bf16[416,128]{1,0:T(8,128)(2,1)S(1)}) custom-call(s32[3]{0:T(128)S(1)} %copy-done.6, bf16[3,32,16,128]{3,2,1,0:T(8,128)(2,1)S(1)} %copy-done, f32[3,2,16,128]{3,2,1,0:T(8,128)S(1)} %copy-done.2), custom_call_target="tpu_custom_call" | custom-call | tf_op jit(solution)/shard_map/edges/pallas_call | solution.py:47
  8.1 0.1 collective-permute-start.3
  8.2 1.7 %collective-permute-start.4 = (bf16[416,128]{1,0:T(8,128)(2,1)S(1)}, bf16[416,128]{1,0:T(8,128)(2,1)S(1)}, u32[]{:S(2)}, u32[]{:S(2)}) collective-permute-start(bf16[416,128]{1,0:T(8,128)(2,1)S(1)} %get-tuple-element.26), channel_id=1, source_target_pairs={{0,3},{1,0},{2,1},{3,2},{4,7},{5,4},{6,5},{7,6},{8,11},{9,8},{10,9... | collective-permute-start | bytes 319496 | tf_op jit(solution)/shard_map/ppermute | solution.py:525
  10.0 1.2 %collective-permute-start.1 = (bf16[416,128]{1,0:T(8,128)(2,1)S(1)}, bf16[416,128]{1,0:T(8,128)(2,1)S(1)}, u32[]{:S(2)}, u32[]{:S(2)}) collective-permute-start(bf16[416,128]{1,0:T(8,128)(2,1)S(1)} %get-tuple-element.25), channel_id=1, source_target_pairs={{0,5},{1,6},{2,7},{3,4},{4,9},{5,10},{6,11},{7,8},{8,13},{9,14},{1... | collective-permute-start | bytes 319496 | tf_op jit(solution)/shard_map/ppermute | solution.py:525
  11.1 2.8 %collective-permute-start.2 = (bf16[416,128]{1,0:T(8,128)(2,1)S(1)}, bf16[416,128]{1,0:T(8,128)(2,1)S(1)}, u32[]{:S(2)}, u32[]{:S(2)}) collective-permute-start(bf16[416,128]{1,0:T(8,128)(2,1)S(1)} %get-tuple-element.26), channel_id=1, source_target_pairs={{0,7},{1,4},{2,5},{3,6},{4,11},{5,8},{6,9},{7,10},{8,15},{9,12},{1... | collective-permute-start | bytes 319496 | tf_op jit(solution)/shard_map/ppermute | solution.py:525
  13.9 0.7 %tile.2 = f32[4,2]{1,0:T(4,128)S(1)} broadcast(f32[2]{0:T(128)} %param.15), dimensions={1} | broadcast | bytes 40 | tf_op jit(solution)/shard_map/tile | solution.py:541
  14.6 0.1 broadcast_in_dim_tile.4.bias2
  14.7 0.7 %copy.12.bias = f32[64,1]{1,0:T(8,128)S(1)} copy(f32[64,1]{0,1:T(1,128)} %bitcast.1) | data formatting | bytes 512 | tf_op jit(solution)/shard_map/broadcast_in_dim | solution.py:540
  15.4 0.0 copy-start.4
  15.4 0.9 %copy-done.4 = bf16[3,3,64,64]{3,2,1,0:T(8,128)(2,1)S(1)} copy-done((bf16[3,3,64,64]{3,2,1,0:T(8,128)(2,1)S(1)}, bf16[3,3,64,64]{3,2,1,0:T(8,128)(2,1)}, u32[]{:S(2)}) %copy-start.4) | copy-done | bytes 73752
  16.3 0.0 copy-start.5
  16.3 0.7 %copy-done.5 = bf16[3,3,2,64]{3,2,1,0:T(2,128)(2,1)S(1)} copy-done((bf16[3,3,2,64]{3,2,1,0:T(2,128)(2,1)S(1)}, bf16[3,3,2,64]{3,2,1,0:T(2,128)(2,1)}, u32[]{:S(2)}) %copy-start.5) | copy-done | bytes 2328
  17.0 0.5 %weights.1 = (bf16[64,288]{1,0:T(8,128)(2,1)S(1)}, bf16[64,288]{1,0:T(8,128)(2,1)S(1)}, bf16[128,288]{1,0:T(8,128)(2,1)S(1)}, bf16[144,192]{1,0:T(8,128)(2,1)S(1...) custom-call(bf16[3,3,64,64]{3,2,1,0:T(8,128)(2,1)S(1)} %copy-done.4,, ...), custom_call_target="tpu_custom_call" | custom-call | tf_op jit(solution)/shard_map/weights/pallas_call | solution.py:47
  17.5 0.0 collective-permute-done.3.above
  17.5 0.0 collective-permute-done.4.below
  17.6 0.0 copy-start.1
  17.6 1.0 %copy-done.1 = bf16[3,32,16,128]{3,2,1,0:T(8,128)(2,1)S(1)} copy-done((bf16[3,32,16,128]{3,2,1,0:T(8,128)(2,1)S(1)}, bf16[3,32,16,128]{3,2,1,0:T(8,128)(2,1)}, u32[]{:S(2)}) %copy-start.1) | copy-done | bytes 393240
  18.6 0.0 copy-start.3
  18.6 0.8 %copy-done.3 = f32[3,2,16,128]{3,2,1,0:T(8,128)S(1)} copy-done((f32[3,2,16,128]{3,2,1,0:T(8,128)S(1)}, f32[3,2,16,128]{3,2,1,0:T(8,128)}, u32[]{:S(2)}) %copy-start.3) | copy-done | bytes 49176
  19.4 0.0 copy-start.7
  19.4 0.7 %copy-done.7 = s32[3]{0:T(128)S(1)} copy-done((s32[3]{0:T(128)S(1)}, s32[3]{0:T(128)}, u32[]{:S(2)}) %copy-start.7) | copy-done | bytes 36
  20.0 4.9 %own.1 = (f32[22,192,128]{2,1,0:T(8,128)S(1)}, bf16[22,192,128]{2,1,0:T(8,128)(2,1)S(1)}, f32[22,144,128]{2,1,0:T(8,128)S(1)}, f32[3,2,24,128]{3,2,1,0:T(8,128)S(1)}) custom-call(s32[3]{0:T(128)S(1)} %copy-done.7, bf16[3,32,16,128]{3,2,1,0:T(8,128)(2,1)S(1)} %copy-done.1, bf16[416,128]{1,0:T(8,128)(2,1)S(1)} %collective-permute-done.3.above, ...), custom_call_target="tpu_custom_call" | custom-call | tf_op jit(solution)/shard_map/own/pallas_call | solution.py:47
  24.9 0.0 collective-permute-done.1.pabove
  24.9 0.0 collective-permute-done.2.pbelow
  24.9 0.0 collective-permute-done.prev
  24.9 0.0 copy-start.8
  24.9 0.6 %copy-done.8 = f32[3]{0:T(128)S(1)} copy-done((f32[3]{0:T(128)S(1)}, f32[3]{0:T(128)}, u32[]{:S(2)}) %copy-start.8) | copy-done | bytes 36
  25.6 5.4 %borrowed.1 = (bf16[16,3,32,128]{3,2,1,0:T(8,128)(2,1)S(1)}, bf16[22,384,128]{2,1,0:T(8,128)(2,1)S(1)}, bf16[3,20,32,128]{3,2,1,0:T(8,128)(2,1)S(1)}, f32[3,2,24,128]{3,2,1,0:T(8,128)S(1)}) custom-call(f32[3]{0:T(128)S(1)} %copy-done.8, bf16[3,32,16,128]{3,2,1,0:T(8,128)(2,1)S(1)} %collective-permute-done.prev, ...), custom_call_target="tpu_custom_call" | custom-call | tf_op jit(solution)/shard_map/borrowed/pallas_call | solution.py:47
  31.0 8.4 %collective-permute-start.5 = (bf16[16,3,32,128]{3,2,1,0:T(8,128)(2,1)S(1)}, bf16[16,3,32,128]{3,2,1,0:T(8,128)(2,1)S(1)}, u32[]{:S(2)}, u32[]{:S(2)}) collective-permute-start(bf16[16,3,32,128]{3,2,1,0:T(8,128)(2,1)S(1)} %get-tuple-element.47), channel_id=1, source_target_pairs={{0,124},{1,125},{2,126},{3,127},{4,0},{5,1},{6,2},{7,3},{8,4},{9,5... | collective-permute-start | bytes 1179656 | tf_op jit(solution)/shard_map/ppermute | solution.py:525
  39.4 2.4 %own_grad.1 = (f32[3,2,16,128]{3,2,1,0:T(8,128)}, f32[16,3,32,128]{3,2,1,0:T(8,128)S(1)}) custom-call(f32[3,2,24,128]{3,2,1,0:T(8,128)S(1)} %get-tuple-element.39.votes, bf16[3,20,32,128]{3,2,1,0:T(8,128)(2,1)S(1)} %get-tuple-element.40.g3, bf16[22,192,128]{2,1,0:T(8,128)(2,1)S(1)} %get-tuple-element.41.hown, ...), custom_call_target="tpu_custom_call" | custom-call | tf_op jit(solution)/shard_map/own_grad/pallas_call | solution.py:47
  41.9 6.2 %collective-permute-done.5.back = bf16[16,3,32,128]{3,2,1,0:T(8,128)(2,1)S(1)} collective-permute-done((bf16[16,3,32,128]{3,2,1,0:T(8,128)(2,1)S(1)}, bf16[16,3,32,128]{3,2,1,0:T(8,128)(2,1)S(1)}, u32[]{:S(2)}, u32[]{:S(2)}) %collective-permute-start.5) | collective-permute-done | bytes 393248 | tf_op jit(solution)/shard_map/ppermute | solution.py:525
  48.1 1.4 %finish.1 = f32[3,32,16,128]{3,2,1,0:T(8,128)} custom-call(f32[16,3,32,128]{3,2,1,0:T(8,128)S(1)} %get-tuple-element.46.grad, bf16[16,3,32,128]{3,2,1,0:T(8,128)(2,1)S(1)} %collective-permute-done.5.back), custom_call_target="tpu_custom_call" | custom-call | tf_op jit(solution)/shard_map/finish/pallas_call | solution.py:47
Async XLA Ops:
  0.6 24.3 %collective-permute-start = (bf16[3,32,16,128]{3,2,1,0:T(8,128)(2,1)}, bf16[3,32,16,128]{3,2,1,0:T(8,128)(2,1)S(1)}, u32[]{:S(2)}, u32[]{:S(2)}) collective-permute-start(bf16[3,32,16,128]{3,2,1,0:T(8,128)(2,1)} %feat.3), channel_id=1, source_target_pairs={{0,4},{1,5},{2,6},{3,7},{4,8},{5,9},{6,10},{7,11},{8,12},{9,13},{1... | collective-permute-start | bytes 1179656 | tf_op jit(solution)/shard_map/ppermute | solution.py:525
  4.7 1.0 %copy-start = (bf16[3,32,16,128]{3,2,1,0:T(8,128)(2,1)S(1)}, bf16[3,32,16,128]{3,2,1,0:T(8,128)(2,1)}, u32[]{:S(2)}) copy-start(bf16[3,32,16,128]{3,2,1,0:T(8,128)(2,1)} %feat.3) | copy-start | bytes 1179652
  5.7 0.8 %copy-start.2 = (f32[3,2,16,128]{3,2,1,0:T(8,128)S(1)}, f32[3,2,16,128]{3,2,1,0:T(8,128)}, u32[]{:S(2)}) copy-start(f32[3,2,16,128]{3,2,1,0:T(8,128)} %vgrad.3) | copy-start | bytes 147460
  6.5 0.7 %copy-start.6 = (s32[3]{0:T(128)S(1)}, s32[3]{0:T(128)}, u32[]{:S(2)}) copy-start(s32[3]{0:T(128)} %valid.3) | copy-start | bytes 40
  8.1 9.4 %collective-permute-start.3 = (bf16[416,128]{1,0:T(8,128)(2,1)S(1)}, bf16[416,128]{1,0:T(8,128)(2,1)S(1)}, u32[]{:S(2)}, u32[]{:S(2)}) collective-permute-start(bf16[416,128]{1,0:T(8,128)(2,1)S(1)} %get-tuple-element.25), channel_id=1, source_target_pairs={{0,1},{1,2},{2,3},{3,0},{4,5},{5,6},{6,7},{7,4},{8,9},{9,10},{10,1... | collective-permute-start | bytes 319496 | tf_op jit(solution)/shard_map/ppermute | solution.py:525
  8.2 9.3 %collective-permute-start.4 = (bf16[416,128]{1,0:T(8,128)(2,1)S(1)}, bf16[416,128]{1,0:T(8,128)(2,1)S(1)}, u32[]{:S(2)}, u32[]{:S(2)}) collective-permute-start(bf16[416,128]{1,0:T(8,128)(2,1)S(1)} %get-tuple-element.26), channel_id=1, source_target_pairs={{0,3},{1,0},{2,1},{3,2},{4,7},{5,4},{6,5},{7,6},{8,11},{9,8},{10,9... | collective-permute-start | bytes 319496 | tf_op jit(solution)/shard_map/ppermute | solution.py:525
  10.0 15.0 %collective-permute-start.1 = (bf16[416,128]{1,0:T(8,128)(2,1)S(1)}, bf16[416,128]{1,0:T(8,128)(2,1)S(1)}, u32[]{:S(2)}, u32[]{:S(2)}) collective-permute-start(bf16[416,128]{1,0:T(8,128)(2,1)S(1)} %get-tuple-element.25), channel_id=1, source_target_pairs={{0,5},{1,6},{2,7},{3,4},{4,9},{5,10},{6,11},{7,8},{8,13},{9,14},{1... | collective-permute-start | bytes 319496 | tf_op jit(solution)/shard_map/ppermute | solution.py:525
  11.1 13.8 %collective-permute-start.2 = (bf16[416,128]{1,0:T(8,128)(2,1)S(1)}, bf16[416,128]{1,0:T(8,128)(2,1)S(1)}, u32[]{:S(2)}, u32[]{:S(2)}) collective-permute-start(bf16[416,128]{1,0:T(8,128)(2,1)S(1)} %get-tuple-element.26), channel_id=1, source_target_pairs={{0,7},{1,4},{2,5},{3,6},{4,11},{5,8},{6,9},{7,10},{8,15},{9,12},{1... | collective-permute-start | bytes 319496 | tf_op jit(solution)/shard_map/ppermute | solution.py:525
  15.4 0.9 %copy-start.4 = (bf16[3,3,64,64]{3,2,1,0:T(8,128)(2,1)S(1)}, bf16[3,3,64,64]{3,2,1,0:T(8,128)(2,1)}, u32[]{:S(2)}) copy-start(bf16[3,3,64,64]{3,2,1,0:T(8,128)(2,1)} %k1.1) | copy-start | bytes 221188
  16.3 0.7 %copy-start.5 = (bf16[3,3,2,64]{3,2,1,0:T(2,128)(2,1)S(1)}, bf16[3,3,2,64]{3,2,1,0:T(2,128)(2,1)}, u32[]{:S(2)}) copy-start(bf16[3,3,2,64]{3,2,1,0:T(2,128)(2,1)} %k2.1) | copy-start | bytes 6916
  17.6 1.0 %copy-start.1 = (bf16[3,32,16,128]{3,2,1,0:T(8,128)(2,1)S(1)}, bf16[3,32,16,128]{3,2,1,0:T(8,128)(2,1)}, u32[]{:S(2)}) copy-start(bf16[3,32,16,128]{3,2,1,0:T(8,128)(2,1)} %feat.3) | copy-start | bytes 1179652
  18.6 0.8 %copy-start.3 = (f32[3,2,16,128]{3,2,1,0:T(8,128)S(1)}, f32[3,2,16,128]{3,2,1,0:T(8,128)}, u32[]{:S(2)}) copy-start(f32[3,2,16,128]{3,2,1,0:T(8,128)} %vgrad.3) | copy-start | bytes 147460
  19.4 0.7 %copy-start.7 = (s32[3]{0:T(128)S(1)}, s32[3]{0:T(128)}, u32[]{:S(2)}) copy-start(s32[3]{0:T(128)} %valid.3) | copy-start | bytes 40
  24.9 0.7 %copy-start.8 = (f32[3]{0:T(128)S(1)}, f32[3]{0:T(128)}, u32[]{:S(2)}) copy-start(f32[3]{0:T(128)} %sharp.1) | copy-start | bytes 40
  31.0 17.0 %collective-permute-start.5 = (bf16[16,3,32,128]{3,2,1,0:T(8,128)(2,1)S(1)}, bf16[16,3,32,128]{3,2,1,0:T(8,128)(2,1)S(1)}, u32[]{:S(2)}, u32[]{:S(2)}) collective-permute-start(bf16[16,3,32,128]{3,2,1,0:T(8,128)(2,1)S(1)} %get-tuple-element.47), channel_id=1, source_target_pairs={{0,124},{1,125},{2,126},{3,127},{4,0},{5,1},{6,2},{7,3},{8,4},{9,5... | collective-permute-start | bytes 1179656 | tf_op jit(solution)/shard_map/ppermute | solution.py:525

commit v2 on v1

v2 whole, which is shorter than its diff:
```python
import jax
import jax.numpy as jnp
from jax import lax
from jax.experimental import pallas as pl
from jax.experimental.pallas import tpu as pltpu
from jax.sharding import PartitionSpec as P

F32 = jnp.float32
BF16 = jnp.bfloat16
OWN = 3
CH = 32
HID = 64
TR = 16
COLS = 128
HALO = 4
FEAT_ROWS = TR + 2 * HALO
HID_ROWS = FEAT_ROWS - 2
FLD_ROWS = FEAT_ROWS - 4
DH_ROWS = FEAT_ROWS - 6
EDGE = HALO * OWN * CH
EDGE_ALL = EDGE + 32


def lane(shape):
    return lax.broadcasted_iota(jnp.int32, shape, len(shape) - 1)


def from_left(x):
    return jnp.where(lane(x.shape) == 0, 0.0, pltpu.roll(x, 1, x.ndim - 1))


def from_right(x):
    return jnp.where(lane(x.shape) == COLS - 1, 0.0, pltpu.roll(x, COLS - 1, x.ndim - 1))


def dot(a, b):
    return jnp.dot(a, b, preferred_element_type=F32)


def params(mib):
    return pltpu.CompilerParams(vmem_limit_bytes=mib << 20)


COST = {
    "own_rim": 0,
    "edges": 0,
    "weights": 0,
    "own_inner": 0,
    "middle": 2306,
    "borrowed": 3459,
    "own_grad": 3459,
    "finish": 1153,
}
INNER = TR - 2
RIM = HID_ROWS - INNER
INNER_PAIRS = [HALO + 2 * i for i in range(INNER // 2)]
RIM_PAIRS = [0, 2, HALO + INNER, HALO + INNER + 2]


def call(kernel, outs, scratch, mib, name, specs, *args):
    space = {"v": pltpu.VMEM, "h": pltpu.HBM}
    args = [
        pltpu.with_memory_space_constraint(x, pltpu.HBM) if c == "h" else x
        for x, c in zip(args, specs, strict=True)
    ]
    return pl.pallas_call(
        kernel,
        out_shape=tuple(jax.ShapeDtypeStruct(shape, kind) for shape, kind in outs),
        in_specs=[pl.BlockSpec(memory_space=space[c]) for c in specs],
        out_specs=(pl.BlockSpec(memory_space=pltpu.VMEM),) * len(outs),
        scratch_shapes=[
            item[0](item[1], item[2]) if len(item) == 3 else pltpu.VMEM(*item) for item in scratch
        ],
        compiler_params=params(mib),
        cost_estimate=pl.CostEstimate(
            flops=COST[name] * 10**6, bytes_accessed=0, transcendentals=0
        ),
        name=name,
    )(*args)


def sems(shape, _):
    return pltpu.SemaphoreType.DMA(shape)


def fetch(sems, *moves):
    copies = [pltpu.make_async_copy(a, b, sems.at[i]) for i, (a, b) in enumerate(moves)]
    for c in copies:
        c.start()
    for c in copies:
        c.wait()


def odd_tile():
    return lax.axis_index("tile") % 2 == 1


def has_tiles():
    tile = lax.axis_index("tile")
    return (tile > 0).astype(F32), (tile < lax.axis_size("tile") - 1).astype(F32)


class Rows:
    def __init__(self, inner, rim):
        self.inner, self.rim = inner, rim

    def at(self, r):
        if r < HALO:
            return self.rim, r
        if r < HALO + INNER:
            return self.inner, r - HALO
        return self.rim, r - INNER

    def pair(self, r, first, n):
        ref, i = self.at(r)
        return pair_row(ref, i, first, n)

    def put(self, r, first, x):
        ref, i = self.at(r)
        halves(ref, i, first, x)


def edges_kernel(
    valid_hbm, sharp_hbm, b2_hbm, feat_hbm, vgrad_hbm,
    sibling, outer, wide, cot, consts,
    valid, sharp, b2, feat, vgrad, ext, sems,
):
    fetch(
        sems,
        (feat_hbm, feat), (vgrad_hbm, vgrad), (valid_hbm, valid), (sharp_hbm, sharp), (b2_hbm, b2),
    )
    row0 = lax.axis_index("tile") * TR
    odd = odd_tile()
    for s in range(OWN):
        wide[s] = feat[s].astype(F32)
        pos = row0 + lax.broadcasted_iota(jnp.int32, (TR, COLS), 0)
        for c in range(2):
            cot[s, c] = jnp.where(pos < valid[s], vgrad[s, c], 0.0)
        consts[s] = jnp.full((8, COLS), sharp[s], F32)
    even_row = lax.broadcasted_iota(jnp.int32, (8, COLS), 0) % 2 == 0
    consts[OWN] = jnp.where(even_row, b2[0], b2[1])
    for out, last in ((sibling, jnp.logical_not(odd)), (outer, odd)):
        ext[...] = jnp.zeros((32, COLS), F32)
        for s in range(OWN):
            for c in range(2):
                x = jnp.where(last, cot[s, c, TR - 2 :, :], cot[s, c, 0:2, :])
                high = x.astype(BF16).astype(F32)
                at = s * 4 + c * 2
                ext[at : at + 2, :] = high
                ext[12 + at : 14 + at, :] = x - high
        out[EDGE:, :] = ext[...].astype(BF16)
        for s in range(OWN):
            for r in range(HALO):
                at = (r * OWN + s) * CH
                x = jnp.where(last, wide[s, :, TR - HALO + r, :], wide[s, :, r, :])
                out[at : at + CH, :] = x.astype(BF16)


def edges(*args):
    return call(
        edges_kernel,
        [
            ((EDGE_ALL, COLS), BF16),
            ((EDGE_ALL, COLS), BF16),
            ((OWN, CH, TR, COLS), F32),
            ((OWN, 2, TR, COLS), F32),
            ((OWN + 1, 8, COLS), F32),
        ],
        [
            (pltpu.SMEM, (OWN,), jnp.int32),
            (pltpu.SMEM, (OWN,), F32),
            (pltpu.SMEM, (2,), F32),
            ((OWN, CH, TR, COLS), BF16),
            ((OWN, 2, TR, COLS), F32),
            ((32, COLS), F32),
            (sems, (5,), None),
        ],
        3,
        "edges",
        "hhhhh",
        *args,
    )


def weights_kernel(
    k1_hbm, k2_hbm, b1_hbm, wcur, wear, wboth, w2own, w2first, w2rest, w2b, w2brest, wgear, wgcur, wgboth, bias,
    k1, k2, b1, fwd, bwd, both, two, sq, sems,
):
    fetch(sems, (k1_hbm, k1), (k2_hbm, k2), (b1_hbm, b1))
    bias[...] = jnp.broadcast_to(b1[...], (COLS, HID)).T
    for dy in range(3):
        for dx in range(3):
            k = k1[dy, dx].astype(F32)
            t = CH * (3 * dy + dx)
            fwd[0:HID, t : t + CH] = k[:, :CH]
            fwd[HID:, t : t + CH] = k[:, CH:]
            kt = k.T
            rows = slice(CH * dx, CH * dx + CH)
            bwd[rows, HID * dy : HID * dy + HID] = kt[:CH]
            bwd[3 * CH + CH * dx : 4 * CH + CH * dx, HID * dy : HID * dy + HID] = kt[CH:]
            both[rows, 2 * HID * dy : 2 * HID * dy + HID] = kt[:CH]
            both[rows, 2 * HID * dy + HID : 2 * HID * dy + 2 * HID] = kt[CH:]
    wcur[...] = fwd[0:HID, :].astype(BF16)
    wear[...] = fwd[HID:, :].astype(BF16)
    wboth[...] = fwd[...].astype(BF16)
    wgcur[...] = bwd[0 : 3 * CH, :].astype(BF16)
    wgear[...] = bwd[3 * CH :, :].astype(BF16)
    wgboth[...] = both[...].astype(BF16)

    def put(ref, row, col, lags):
        for i, lag in enumerate(lags):
            for dy in range(3):
                for dx in range(3):
                    at = row + 8 * (3 * dy + dx) + 2 * lag
                    c = col + HID * i
                    ref[at : at + 2, c : c + HID] = k2[dy, dx].astype(F32)

    two[...] = jnp.zeros(two.shape, F32)
    put(two, 0, 0, (0, 1, 2))
    w2first[...] = two[0:72, :].astype(BF16)
    two[...] = jnp.zeros(two.shape, F32)
    put(two, 0, 0, (1, 2))
    put(two, 72, 2 * HID, (2,))
    w2rest[...] = two[...].astype(BF16)
    two[...] = jnp.zeros(two.shape, F32)
    put(two, 0, 0, (0,))
    put(two, 72, HID, (0, 1))
    w2own[...] = two[...].astype(BF16)

    def lay(row, col, lags):
        for i, lag in enumerate(lags):
            for dy in range(3):
                for dx in range(3):
                    at = row + 32 * dy + 8 * dx + 2 * lag
                    c = col + HID * i
                    sq[at : at + 2, c : c + HID] = k2[dy, dx].astype(F32)

    sq[...] = jnp.zeros(sq.shape, F32)
    lay(0, 0, (0, 1, 2))
    w2b[...] = sq[0:96, :].T.astype(BF16)
    sq[...] = jnp.zeros(sq.shape, F32)
    lay(0, 0, (1, 2))
    lay(96, 2 * HID, (2,))
    w2brest[...] = sq[...].T.astype(BF16)


def weights(k1, k2, b1):
    return call(
        weights_kernel,
        [
            ((HID, 9 * CH), BF16),
            ((HID, 9 * CH), BF16),
            ((2 * HID, 9 * CH), BF16),
            ((144, 192), BF16),
            ((72, 192), BF16),
            ((144, 192), BF16),
            ((192, 96), BF16),
            ((192, 192), BF16),
            ((3 * CH, 3 * HID), BF16),
            ((3 * CH, 3 * HID), BF16),
            ((3 * CH, 6 * HID), BF16),
            ((HID, COLS), F32),
        ],
        [
            (k1.shape, BF16),
            (k2.shape, BF16),
            (b1.shape, F32),
            ((2 * HID, 9 * CH), F32),
            ((6 * CH, 3 * HID), F32),
            ((3 * CH, 6 * HID), F32),
            ((144, 192), F32),
            ((192, 192), F32),
            (sems, (3,), None),
        ],
        4,
        "weights",
        "hhh",
        k1,
        k2,
        b1,
    )


def spread_row(x, xd, j, r):
    xd[j, r, 0:CH, :] = from_left(x).astype(BF16)
    xd[j, r, CH : 2 * CH, :] = x.astype(BF16)
    xd[j, r, 2 * CH :, :] = from_right(x).astype(BF16)


def spread_own(wide, keep, xd):
    for s in range(OWN):
        for r in range(TR):
            x = wide[s, :, r, :]
            spread_row(x if keep is None else x * keep, xd, s, r)


def spread_rim(pick, scale, xr):
    for s in range(OWN):
        for r in range(HALO):
            for side in range(2):
                spread_row(pick(side, s, r) * scale[side], xr, s, HALO * side + r)


def feature_rows(xd, xr):
    def pick(j, r):
        if r < HALO:
            return xr[j, r]
        if r < HALO + TR:
            return xd[j, r - HALO]
        return xr[j, r - TR]

    return pick


def taps(rows, pick):
    return jnp.concatenate(
        [jnp.concatenate([pick(r), pick(r + 1)], axis=1) for r in rows], axis=0
    )


def halves(ref, r, first, x):
    n = x.shape[0]
    ref[r, first : first + n, :] = x[:, :COLS]
    ref[r + 1, first : first + n, :] = x[:, COLS:]


def pair_row(ref, r, first, n):
    return jnp.concatenate(
        [ref[r, first : first + n, :], ref[r + 1, first : first + n, :]], axis=1
    )


def gather_columns(p):
    return from_right(p[:CH]) + p[CH : 2 * CH] + from_left(p[2 * CH :])


def hidden_own(pairs, pick, wcur, wboth, bias, w2own, cur, hown, town):
    b = jnp.concatenate([bias[...], bias[...]], axis=1)
    for r in pairs:
        rhs = [taps((r, r + 1, r + 2), lambda q, j=j: pick(j, q)) for j in range(OWN)]
        both = [dot(wboth[...], rhs[j]) for j in range(2)]
        c = [both[0][:HID] + b, both[1][:HID] + b, dot(wcur[...], rhs[2]) + b]
        ear = [both[0][HID:], both[1][HID:]]
        for s in range(OWN):
            cur.put(r, HID * s, c[s])
        h = jnp.concatenate(
            [jnp.maximum(x, 0.0) for x in (c[1] + ear[0], c[2] + ear[1], c[2] + ear[0])], axis=0
        ).astype(BF16)
        hown.put(r, 0, h)
        town.put(r, 0, dot(w2own[...], h))


def hidden_borrowed(pairs, pick, wear, w2first, w2rest, cur, town, hmid, tsum):
    for r in pairs:
        ear = [
            dot(wear[...], taps((r, r + 1, r + 2), lambda q, j=j: pick(j, q)))
            for j in range(OWN)
        ]
        c = [cur.pair(r, HID * s, HID) for s in range(OWN)]
        h = [
            jnp.concatenate([jnp.maximum(c[s] + ear[3 + s - k], 0.0) for s, k in part], axis=0)
            for part in (((0, 1), (0, 2), (0, 3)), ((1, 2), (1, 3), (2, 3)))
        ]
        h = [x.astype(BF16) for x in h]
        hmid.put(r, 0, h[0])
        hmid.put(r, 192, h[1])
        tsum.put(r, 0, dot(w2first[...], h[0]))
        tsum.put(r, 72, dot(w2rest[...], h[1]) + town.pair(r, 0, 144))


def own_kernel(wide, wcur, wboth, bias, w2own, xd, cur, hown, town):
    spread_own(wide, None, xd)
    hidden_own(
        INNER_PAIRS, feature_rows(xd, None), wcur, wboth, bias, w2own,
        Rows(cur, None), Rows(hown, None), Rows(town, None),
    )


def hidden_outs(n):
    return [
        ((n, OWN * HID, COLS), F32),
        ((n, 3 * HID, COLS), BF16),
        ((n, 144, COLS), F32),
    ]


def own_inner(*args):
    return call(
        own_kernel,
        [((OWN, TR, 3 * CH, COLS), BF16)] + hidden_outs(INNER),
        [],
        2,
        "own_inner",
        "v" * len(args),
        *args,
    )


def rim_kernel(
    sibling, outer, cot16, xd, wcur, wboth, bias, w2own, rcur, rhown, rtown, cot, xr
):
    odd = odd_tile()
    has = has_tiles()

    def halo(side, first, n):
        x, y = sibling[first : first + n, :], outer[first : first + n, :]
        x, y = x.astype(F32), y.astype(F32)
        return jnp.where(odd, x, y) if side == 0 else jnp.where(odd, y, x)

    for side, first in ((0, 0), (1, TR + 2)):
        ext = halo(side, EDGE, 32) * has[side]
        for s in range(OWN):
            for c in range(2):
                at = s * 4 + c * 2
                cot[s, c, first : first + 2, :] = ext[at : at + 2] + ext[12 + at : 14 + at]
    for s in range(OWN):
        for c in range(2):
            cot[s, c, 2 : 2 + TR, :] = cot16[s, c]
    spread_rim(lambda side, s, r: halo(side, (r * OWN + s) * CH, CH), has, xr)
    hidden_own(
        RIM_PAIRS, feature_rows(xd, xr), wcur, wboth, bias, w2own,
        Rows(None, rcur), Rows(None, rhown), Rows(None, rtown),
    )


def own_rim(*args):
    return call(
        rim_kernel,
        hidden_outs(RIM) + [((OWN, 2, 24, COLS), F32)],
        [((OWN, 2 * HALO, 3 * CH, COLS), BF16)],
        2,
        "own_rim",
        "v" * len(args),
        *args,
    )


def middle_kernel(prev, icur, itown, wear, w2first, w2rest, xp, ihmid, itsum, wide):
    keep = (lax.axis_index("sec") > 0).astype(F32)
    for s in range(OWN):
        wide[s] = prev[s].astype(F32)
    spread_own(wide, keep, xp)
    hidden_borrowed(
        INNER_PAIRS, feature_rows(xp, None), wear, w2first, w2rest,
        Rows(icur, None), Rows(itown, None), Rows(ihmid, None), Rows(itsum, None),
    )


def middle(*args):
    return call(
        middle_kernel,
        [
            ((OWN, TR, 3 * CH, COLS), BF16),
            ((INNER, 6 * HID, COLS), BF16),
            ((INNER, OWN * 72, COLS), F32),
        ],
        [((OWN, CH, TR, COLS), F32)],
        3,
        "middle",
        "v" * len(args),
        *args,
    )


def fields_stage(tsum, bias2, has, fld):
    for r in range(FLD_ROWS):
        for s in range(OWN):
            sums = []
            for dx in range(3):
                terms = []
                for dy in range(3):
                    at = 72 * s + 8 * (3 * dy + dx)
                    ref, i = tsum.at(r + dy)
                    t = ref[i, at : at + 8, :]
                    if r + dy < 3:
                        t = t * has[0]
                    elif r + dy > HID_ROWS - 4:
                        t = t * has[1]
                    terms.append(t)
                sums.append(terms[0] + terms[1] + terms[2])
            fld[s, r] = (sums[1] + bias2[...]) + (from_left(sums[0]) + from_right(sums[2]))


def vote_stage(consts, cot, fld, grd, g3, votes):
    for s in range(OWN):
        f = [[fld[s, :, 2 * k + c, :] for c in range(2)] for k in range(3)]
        beta = consts[s, 0:1, :]
        diff = {}
        dist = {}
        for a, b in ((0, 1), (0, 2), (1, 2)):
            diff[a, b] = [f[a][c] - f[b][c] for c in range(2)]
            dist[a, b] = diff[a, b][0] * diff[a, b][0] + diff[a, b][1] * diff[a, b][1]
        score = [dist[0, 1] + dist[0, 2], dist[0, 1] + dist[1, 2], dist[0, 2] + dist[1, 2]]
        logit = [-beta * q for q in score]
        top = jnp.maximum(jnp.maximum(logit[0], logit[1]), logit[2])
        expo = [jnp.exp(q - top) for q in logit]
        inv = 1.0 / (expo[0] + expo[1] + expo[2])
        w = [q * inv for q in expo]
        v = [w[0] * f[0][c] + w[1] * f[1][c] + w[2] * f[2][c] for c in range(2)]
        for c in range(2):
            votes[s, c, 0:FLD_ROWS, :] = v[c]
        g = [cot[s, c, 0:FLD_ROWS, :] for c in range(2)]
        e = [
            -beta * w[k] * (g[0] * (f[k][0] - v[0]) + g[1] * (f[k][1] - v[1])) for k in range(3)
        ]
        pair = {key: 2.0 * (e[key[0]] + e[key[1]]) for key in diff}
        for c in range(2):
            m01 = pair[0, 1] * diff[0, 1][c]
            m02 = pair[0, 2] * diff[0, 2][c]
            m12 = pair[1, 2] * diff[1, 2][c]
            grd[s, :, 0 + c, :] = w[0] * g[c] + m01 + m02
            grd[s, :, 2 + c, :] = w[1] * g[c] - m01 + m12
            grd[s, :, 4 + c, :] = w[2] * g[c] - m02 - m12
        grd[s, :, 6, :] = jnp.zeros((FLD_ROWS, COLS), F32)
        grd[s, :, 7, :] = jnp.zeros((FLD_ROWS, COLS), F32)
    for r in range(FLD_ROWS):
        for s in range(OWN):
            x = grd[s, r]
            g3[s, r] = jnp.concatenate(
                [from_right(x), x, from_left(x), jnp.zeros_like(x)], axis=0
            ).astype(BF16)


def inside(ref, has):
    for r, h in ((0, has[0]), (DH_ROWS - 1, has[1])):
        ref[r] = (ref[r].astype(F32) * h).astype(BF16)


def low_grad_stage(w2b, w2brest, g3, hmid, has, dlow):
    for q in range(0, DH_ROWS, 2):
        rhs = [taps((q + 2, q + 1, q), lambda r, s=s: g3[s, r]) for s in range(OWN)]
        h = [hmid.pair(q + 2, 192 * j, 192).astype(F32) for j in range(2)]
        first = jnp.where(h[0] > 0.0, dot(w2b[...], rhs[0]), 0.0)
        rest = jnp.where(
            h[1] > 0.0, dot(w2brest[...], jnp.concatenate([rhs[1], rhs[2]], axis=0)), 0.0
        )
        low = jnp.concatenate(
            [
                first[2 * HID :],
                first[HID : 2 * HID] + rest[HID : 2 * HID],
                first[:HID] + rest[:HID] + rest[2 * HID :],
            ],
            axis=0,
        ).astype(BF16)
        halves(dlow, q, 0, low)
    inside(dlow, has)


def feature_grad_stage(dref, jobs, unroll):
    def step(i, carry):
        r = 2 * i
        for first, size, weight, out, s in jobs:
            rhs = taps((r + 2, r + 1, r), lambda q: dref[q, first : first + size, :])
            p = dot(weight[...], rhs)
            for d in range(2):
                out[r + d, s] = gather_columns(p[:, COLS * d : COLS * d + COLS]).astype(out.dtype)
        return carry

    lax.fori_loop(0, TR // 2, step, 0, unroll=unroll)


def borrowed_kernel(
    psib, pouter, xp, rcur, rtown, itsum, ihmid, cot, consts,
    wear, w2first, w2rest, w2b, w2brest, wgear,
    low, rhmid, g3, votes,
    wide, xr, rtsum, fld, grd, dlow,
):
    odd = odd_tile()
    has = has_tiles()
    keep = (lax.axis_index("sec") > 0).astype(F32)
    for s in range(OWN):
        wide[s] = psib[s].astype(F32)

    def halo(side, s, r):
        at = (r * OWN + s) * CH
        y = pouter[at : at + CH, :].astype(F32)
        if side == 0:
            return jnp.where(odd, wide[s, :, TR - HALO + r, :], y)
        return jnp.where(odd, y, wide[s, :, r, :])

    spread_rim(halo, [keep * h for h in has], xr)
    hmid, tsum = Rows(ihmid, rhmid), Rows(itsum, rtsum)
    hidden_borrowed(
        RIM_PAIRS, feature_rows(xp, xr), wear, w2first, w2rest,
        Rows(None, rcur), Rows(None, rtown), hmid, tsum,
    )
    fields_stage(tsum, consts.at[OWN], has, fld)
    vote_stage(consts, cot, fld, grd, g3, votes)
    low_grad_stage(w2b, w2brest, g3, hmid, has, dlow)
    feature_grad_stage(dlow, [(64 * s, 64, wgear, low, s) for s in range(OWN)], True)


def borrowed(*args):
    return call(
        borrowed_kernel,
        [
            ((TR, OWN, CH, COLS), BF16),
            ((RIM, 6 * HID, COLS), BF16),
            ((OWN, FLD_ROWS, 32, COLS), BF16),
            ((OWN, 2, 24, COLS), F32),
        ],
        [
            ((OWN, CH, TR, COLS), F32),
            ((OWN, 2 * HALO, 3 * CH, COLS), BF16),
            ((RIM, OWN * 72, COLS), F32),
            ((OWN, FLD_ROWS, 8, COLS), F32),
            ((OWN, FLD_ROWS, 8, COLS), F32),
            ((DH_ROWS, 3 * HID, COLS), BF16),
        ],
        6,
        "borrowed",
        "v" * len(args),
        *args,
    )


def own_grad_kernel(
    votes, g3, ihown, rhown, ihmid, rhmid, w2b, wgcur, wgboth, voted, grad, down
):
    has = has_tiles()
    hown, hmid = Rows(ihown, rhown), Rows(ihmid, rhmid)
    for s in range(OWN):
        for c in range(2):
            voted[s, c] = votes[s, c, 2 : 2 + TR, :]
    for q in range(0, DH_ROWS, 2):
        ho = hown.pair(q + 2, 0, 192)
        hm = hmid.pair(q + 2, 0, 384)
        h = [
            hm[:192],
            jnp.concatenate([ho[:64], hm[192:320]], axis=0),
            jnp.concatenate([ho[64:], hm[320:]], axis=0),
        ]
        m = []
        for s in range(OWN):
            dh = dot(w2b[...], taps((q + 2, q + 1, q), lambda r, s=s: g3[s, r]))
            dh = jnp.where(h[s].astype(F32) > 0.0, dh, 0.0)
            m.append([dh[HID * k : HID * k + HID] for k in range(3)])
        c = [m[s][0] + m[s][1] + m[s][2] for s in range(OWN)]
        d = jnp.concatenate([c[0], m[1][0] + m[2][1], c[1], m[2][0], c[2]], axis=0).astype(BF16)
        halves(down, q, 0, d)
    inside(down, has)
    feature_grad_stage(
        down,
        [(0, 128, wgboth, grad, 0), (128, 128, wgboth, grad, 1), (256, 64, wgcur, grad, 2)],
        4,
    )


def own_grad(*args):
    return call(
        own_grad_kernel,
        [((OWN, 2, TR, COLS), F32), ((TR, OWN, CH, COLS), F32)],
        [((DH_ROWS, 5 * HID, COLS), BF16)],
        4,
        "own_grad",
        "v" * len(args),
        *args,
    )


def finish_kernel(grad, back, out):
    keep = (lax.axis_index("sec") < lax.axis_size("sec") - 1).astype(F32)
    for s in range(OWN):
        for r in range(TR):
            out[s, :, r, :] = grad[r, s] + back[r, s].astype(F32) * keep


def finish(grad, back):
    return call(finish_kernel, [((OWN, CH, TR, COLS), F32)], [], 4, "finish", "vv", grad, back)[0]


def move(value, secs, tile_to):
    n, m = lax.axis_size("sec"), lax.axis_size("tile")
    pairs = [(a * m + b, ((a + secs) % n) * m + tile_to(b)) for a in range(n) for b in range(m)]
    return lax.ppermute(value, ("sec", "tile"), pairs)


def body(
    features, vote_grad, sharpness, valid_rows, first_kernel, first_bias, second_kernel, second_bias
):
    tiles = lax.axis_size("tile")

    def same(b):
        return b

    def to_sibling(b):
        return b + 1 - 2 * (b % 2)

    def to_outer(b):
        return (b - 1 + 2 * (b % 2)) % tiles

    prev = move(features, 1, same)
    for_sibling, for_outer, wide, cot16, consts = edges(
        valid_rows, sharpness, second_bias, features, vote_grad
    )
    sibling = move(for_sibling, 0, to_sibling)
    outer = move(for_outer, 0, to_outer)
    pouter = move(for_outer, 1, to_outer)
    (
        wcur, wear, wboth, w2own, w2first, w2rest, w2b, w2brest, wgear, wgcur, wgboth, bias,
    ) = weights(first_kernel, second_kernel, first_bias[None])
    xd, icur, ihown, itown = own_inner(wide, wcur, wboth, bias, w2own)
    rcur, rhown, rtown, cot = own_rim(
        sibling, outer, cot16, xd, wcur, wboth, bias, w2own
    )
    prev, rcur, pouter = lax.optimization_barrier((prev, rcur, pouter))
    psib = move(prev, 0, to_sibling)
    xp, ihmid, itsum = middle(prev, icur, itown, wear, w2first, w2rest)
    low, rhmid, g3, votes = borrowed(
        psib, pouter, xp, rcur, rtown, itsum, ihmid, cot, consts,
        wear, w2first, w2rest, w2b, w2brest, wgear,
    )
    back = move(low, -1, same)
    voted, grad = own_grad(votes, g3, ihown, rhown, ihmid, rhmid, w2b, wgcur, wgboth)
    return (voted, finish(grad, back))


def solution(mesh):
    return jax.shard_map(
        body,
        mesh=mesh,
        in_specs=(
            P("sec", None, "tile", None),
            P("sec", None, "tile", None),
            P("sec"),
            P("sec"),
            P(),
            P(),
            P(),
            P(),
        ),
        out_specs=(P("sec", None, "tile", None), P("sec", None, "tile", None)),
        check_vma=False,
    )
```

time: 50.1 us -> 41.9 us (0.84)
  local copies, waits for them, and re-layouts: 8.65 us -> 0 us
  starting transfers between devices: 18.2 us -> 11.2 us
  waiting for transfers between devices: 6.23 us -> 12.6 us
  Pallas kernels: 15.7 us -> 16.8 us
    unnamed x18 -> x0, local copies, waits for them, and re-layouts: 7.17 us -> none
    ppermute x6, starting transfers between devices: 18.2 us -> 11.2 us  [move(): return lax.ppermute(value, ('sec', 'tile'), pairs)]
    ppermute x6, waiting for transfers between devices: 6.23 us -> 12.6 us  [move(): return lax.ppermute(value, ('sec', 'tile'), pairs)]
    pallas_call x6 -> x8, Pallas kernels: 15.7 us -> 16.8 us  [call(): pl.pallas_call(kernel, out_shape=tuple((jax.ShapeDtypeStruct(shape, kind)...]
    broadcast_in_dim x1 -> x0, local copies, waits for them, and re-layouts: 0.74 us -> none  [body(): bias = first_bias[:, None]]
    another operation x2 -> x0, local copies, waits for them, and re-layouts: 0.73 us -> none  [body(): bias2 = jnp.tile(second_bias, 4)[:, None]]
  transfers between devices with their start and end apart: 6 -> 6, of which waited for: 1 -> 3; matrix products, arithmetic and copies ran while one was open for 3% -> 0% of each run, Pallas kernels for 18% -> 30%
where the time goes in v2:
time: 41.9 us; the launch traced here: 41.3 us
  Pallas kernels  16.8 us (40%)
  waiting for transfers between devices  12.6 us (30%)
  starting transfers between devices  11.2 us (27%)
  between operations  0.69 us (2%)
    pallas_call x8, Pallas kernels, call(): pl.pallas_call(kernel, out_shape=tuple((jax.ShapeDtypeStruct(shape, kind)...  16.8 us
    ppermute x6, waiting for transfers between devices, move(): return lax.ppermute(value, ('sec', 'tile'), pairs)  12.6 us
    ppermute x6, starting transfers between devices, move(): return lax.ppermute(value, ('sec', 'tile'), pairs)  11.2 us
  transfers between devices with their start and end apart: 6, of which 3 were waited for; matrix products, arithmetic and copies ran while one was open for 0% of the time, Pallas kernels for 30%

profile of v2, /device:TPU:0, one launch (start us, length us, event | category | flops | bytes accessed | tf_op | source)
XLA Modules:
  0.0 41.3 jit_solution(5990688219885249484)
XLA Ops:
  0.6 4.0 %collective-permute-start = (bf16[3,32,16,128]{3,2,1,0:T(8,128)(2,1)}, bf16[3,32,16,128]{3,2,1,0:T(8,128)(2,1)S(1)}, u32[]{:S(2)}, u32[]{:S(2)}) collective-permute-start(bf16[3,32,16,128]{3,2,1,0:T(8,128)(2,1)} %feat_hbm.1), channel_id=1, source_target_pairs={{0,4},{1,5},{2,6},{3,7},{4,8},{5,9},{6,10},{7,11},{8,12},{9,13},{1... | collective-permute-start | bytes 1179656 | tf_op jit(solution)/shard_map/ppermute | solution.py:675
  4.7 1.7 %edges.1 = (bf16[416,128]{1,0:T(8,128)(2,1)S(1)}, bf16[416,128]{1,0:T(8,128)(2,1)S(1)}, f32[3,32,16,128]{3,2,1,0:T(8,128)S(1)}, f32[3,2,16,128]{3,2,1,0:T(8,128)S(1)}, f32[4,8,128]{2,1,0:T(8,128)S(1)}) custom-call(s32[3]{0:T(128)} %valid_hbm.1, f32[3]{0:T(128)} %sharp_hbm.1, f32[2]{0:T(128)} %b2_hbm.1, bf16[3,32,16,128]{3,2,1,0:T(8,128)(2,1)} %feat_hbm.1, ...), custom_call_target="tpu_custom_call" | custom-call | tf_op jit(solution)/shard_map/edges/pallas_call | solution.py:66
  6.3 0.3 collective-permute-start.2
  6.6 1.0 %collective-permute-start.1 = (bf16[416,128]{1,0:T(8,128)(2,1)S(1)}, bf16[416,128]{1,0:T(8,128)(2,1)S(1)}, u32[]{:S(2)}, u32[]{:S(2)}) collective-permute-start(bf16[416,128]{1,0:T(8,128)(2,1)S(1)} %get-tuple-element.39), channel_id=1, source_target_pairs={{0,1},{1,0},{2,3},{3,2},{4,5},{5,4},{6,7},{7,6},{8,9},{9,8},{10,11... | collective-permute-start | bytes 319496 | tf_op jit(solution)/shard_map/ppermute | solution.py:675
  7.6 0.8 %collective-permute-start.3 = (bf16[416,128]{1,0:T(8,128)(2,1)S(1)}, bf16[416,128]{1,0:T(8,128)(2,1)S(1)}, u32[]{:S(2)}, u32[]{:S(2)}) collective-permute-start(bf16[416,128]{1,0:T(8,128)(2,1)S(1)} %get-tuple-element.40), channel_id=1, source_target_pairs={{0,7},{1,6},{2,5},{3,4},{4,11},{5,10},{6,9},{7,8},{8,15},{9,14},{1... | collective-permute-start | bytes 319496 | tf_op jit(solution)/shard_map/ppermute | solution.py:675
  8.4 1.4 %weights.1 = (bf16[64,288]{1,0:T(8,128)(2,1)S(1)}, bf16[64,288]{1,0:T(8,128)(2,1)S(1)}, bf16[128,288]{1,0:T(8,128)(2,1)S(1)}, bf16[144,192]{1,0:T(8,128)(2,1)S(1...) custom-call(bf16[3,3,64,64]{3,2,1,0:T(8,128)(2,1)} %k1_hbm.1, ...), custom_call_target="tpu_custom_call" | custom-call | tf_op jit(solution)/shard_map/weights/pallas_call | solution.py:66
  9.8 2.6 %own_inner.1 = (bf16[3,16,96,128]{3,2,1,0:T(8,128)(2,1)S(1)}, f32[14,192,128]{2,1,0:T(8,128)S(1)}, bf16[14,192,128]{2,1,0:T(8,128)(2,1)S(1)}, f32[14,144,128]{2,1,0:T(8,128)S(1)}) custom-call(f32[3,32,16,128]{3,2,1,0:T(8,128)S(1)} %get-tuple-element.42.wide, bf16[64,288]{1,0:T(8,128)(2,1)S(1)} %get-tuple-element.43.wcur, ...), custom_call_target="tpu_custom_call" | custom-call | tf_op jit(solution)/shard_map/own_inner/pallas_call | solution.py:66
  12.4 3.5 %collective-permute-done.2.outer = bf16[416,128]{1,0:T(8,128)(2,1)S(1)} collective-permute-done((bf16[416,128]{1,0:T(8,128)(2,1)S(1)}, bf16[416,128]{1,0:T(8,128)(2,1)S(1)}, u32[]{:S(2)}, u32[]{:S(2)}) %collective-permute-start.2) | collective-permute-done | bytes 106528 | tf_op jit(solution)/shard_map/ppermute | solution.py:675
  15.9 0.0 collective-permute-done.1.sibling
  15.9 1.3 %own_rim.1 = (f32[8,192,128]{2,1,0:T(8,128)S(1)}, bf16[8,192,128]{2,1,0:T(8,128)(2,1)S(1)}, f32[8,144,128]{2,1,0:T(8,128)S(1)}, f32[3,2,24,128]{3,2,1,0:T(8,128)S(1)}) custom-call(bf16[416,128]{1,0:T(8,128)(2,1)S(1)} %collective-permute-done.1.sibling, bf16[416,128]{1,0:T(8,128)(2,1)S(1)} %collective-permute-done.2.outer, ...), custom_call_target="tpu_custom_call" | custom-call | tf_op jit(solution)/shard_map/own_rim/pallas_call | solution.py:66
  17.2 2.9 %collective-permute-done.3.pouter = bf16[416,128]{1,0:T(8,128)(2,1)S(1)} collective-permute-done((bf16[416,128]{1,0:T(8,128)(2,1)S(1)}, bf16[416,128]{1,0:T(8,128)(2,1)S(1)}, u32[]{:S(2)}, u32[]{:S(2)}) %collective-permute-start.3) | collective-permute-done | bytes 106528 | tf_op jit(solution)/shard_map/ppermute | solution.py:675
  20.1 0.0 collective-permute-done.prev
  20.1 0.8 %collective-permute-start.4 = (bf16[3,32,16,128]{3,2,1,0:T(8,128)(2,1)S(1)}, bf16[3,32,16,128]{3,2,1,0:T(8,128)(2,1)S(1)}, u32[]{:S(2)}, u32[]{:S(2)}) collective-permute-start(bf16[3,32,16,128]{3,2,1,0:T(8,128)(2,1)S(1)} %collective-permute-done.prev), channel_id=1, source_target_pairs={{0,1},{1,0},{2,3},{3,2},{4,5},{5,4},{6,7},{7,6},{8,9},{9,8},{10,11... | collective-permute-start | bytes 1179656 | tf_op jit(solution)/shard_map/ppermute | solution.py:675
  20.9 2.6 %middle.1 = (bf16[3,16,96,128]{3,2,1,0:T(8,128)(2,1)S(1)}, bf16[14,384,128]{2,1,0:T(8,128)(2,1)S(1)}, f32[14,216,128]{2,1,0:T(8,128)S(1)}) custom-call(bf16[3,32,16,128]{3,2,1,0:T(8,128)(2,1)S(1)} %collective-permute-done.prev, f32[14,192,128]{2,1,0:T(8,128)S(1)} %get-tuple-element.51.icur, f32[14,144,128]{2,1,0:T(8,128)S(1)} %get-tuple-element.52.itown, ...), custom_call_target="tpu_custom_call" | custom-call | flops 2305999872 | tf_op jit(solution)/shard_map/middle/pallas_call | solution.py:66
  23.5 0.0 collective-permute-done.4.psib
  23.5 3.1 %borrowed.1 = (bf16[16,3,32,128]{3,2,1,0:T(8,128)(2,1)S(1)}, bf16[8,384,128]{2,1,0:T(8,128)(2,1)S(1)}, bf16[3,20,32,128]{3,2,1,0:T(8,128)(2,1)S(1)}, f32[3,2,24,128]{3,2,1,0:T(8,128)S(1)}) custom-call(bf16[3,32,16,128]{3,2,1,0:T(8,128)(2,1)S(1)} %collective-permute-done.4.psib, bf16[416,128]{1,0:T(8,128)(2,1)S(1)} %collective-permute-done.3.pouter, ...), custom_call_target="tpu_custom_call" | custom-call | flops 3459000064 | tf_op jit(solution)/shard_map/borrowed/pallas_call | solution.py:66
  26.6 4.4 %collective-permute-start.5 = (bf16[16,3,32,128]{3,2,1,0:T(8,128)(2,1)S(1)}, bf16[16,3,32,128]{3,2,1,0:T(8,128)(2,1)S(1)}, u32[]{:S(2)}, u32[]{:S(2)}) collective-permute-start(bf16[16,3,32,128]{3,2,1,0:T(8,128)(2,1)S(1)} %get-tuple-element.75), channel_id=1, source_target_pairs={{0,124},{1,125},{2,126},{3,127},{4,0},{5,1},{6,2},{7,3},{8,4},{9,5... | collective-permute-start | bytes 1179656 | tf_op jit(solution)/shard_map/ppermute | solution.py:675
  31.0 2.7 %own_grad.1 = (f32[3,2,16,128]{3,2,1,0:T(8,128)}, f32[16,3,32,128]{3,2,1,0:T(8,128)S(1)}) custom-call(f32[3,2,24,128]{3,2,1,0:T(8,128)S(1)} %get-tuple-element.66.votes, bf16[3,20,32,128]{3,2,1,0:T(8,128)(2,1)S(1)} %get-tuple-element.67.g3, bf16[14,192,128]{2,1,0:T(8,128)(2,1)S(1)} %get-tuple-element.68.ihown, ...), custom_call_target="tpu_custom_call" | custom-call | flops 3459000064 | tf_op jit(solution)/shard_map/own_grad/pallas_call | solution.py:66
  33.7 6.1 %collective-permute-done.5.back = bf16[16,3,32,128]{3,2,1,0:T(8,128)(2,1)S(1)} collective-permute-done((bf16[16,3,32,128]{3,2,1,0:T(8,128)(2,1)S(1)}, bf16[16,3,32,128]{3,2,1,0:T(8,128)(2,1)S(1)}, u32[]{:S(2)}, u32[]{:S(2)}) %collective-permute-start.5) | collective-permute-done | bytes 393248 | tf_op jit(solution)/shard_map/ppermute | solution.py:675
  39.9 1.4 %finish.1 = f32[3,32,16,128]{3,2,1,0:T(8,128)} custom-call(f32[16,3,32,128]{3,2,1,0:T(8,128)S(1)} %get-tuple-element.74.grad, bf16[16,3,32,128]{3,2,1,0:T(8,128)(2,1)S(1)} %collective-permute-done.5.back), custom_call_target="tpu_custom_call" | custom-call | flops 1152999936 | tf_op jit(solution)/shard_map/finish/pallas_call | solution.py:66
Async XLA Ops:
  0.6 19.5 %collective-permute-start = (bf16[3,32,16,128]{3,2,1,0:T(8,128)(2,1)}, bf16[3,32,16,128]{3,2,1,0:T(8,128)(2,1)S(1)}, u32[]{:S(2)}, u32[]{:S(2)}) collective-permute-start(bf16[3,32,16,128]{3,2,1,0:T(8,128)(2,1)} %feat_hbm.1), channel_id=1, source_target_pairs={{0,4},{1,5},{2,6},{3,7},{4,8},{5,9},{6,10},{7,11},{8,12},{9,13},{1... | collective-permute-start | bytes 1179656 | tf_op jit(solution)/shard_map/ppermute | solution.py:675
  6.3 9.5 %collective-permute-start.2 = (bf16[416,128]{1,0:T(8,128)(2,1)S(1)}, bf16[416,128]{1,0:T(8,128)(2,1)S(1)}, u32[]{:S(2)}, u32[]{:S(2)}) collective-permute-start(bf16[416,128]{1,0:T(8,128)(2,1)S(1)} %get-tuple-element.40), channel_id=1, source_target_pairs={{0,3},{1,2},{2,1},{3,0},{4,7},{5,6},{6,5},{7,4},{8,11},{9,10},{10,... | collective-permute-start | bytes 319496 | tf_op jit(solution)/shard_map/ppermute | solution.py:675
  6.6 9.3 %collective-permute-start.1 = (bf16[416,128]{1,0:T(8,128)(2,1)S(1)}, bf16[416,128]{1,0:T(8,128)(2,1)S(1)}, u32[]{:S(2)}, u32[]{:S(2)}) collective-permute-start(bf16[416,128]{1,0:T(8,128)(2,1)S(1)} %get-tuple-element.39), channel_id=1, source_target_pairs={{0,1},{1,0},{2,3},{3,2},{4,5},{5,4},{6,7},{7,6},{8,9},{9,8},{10,11... | collective-permute-start | bytes 319496 | tf_op jit(solution)/shard_map/ppermute | solution.py:675
  7.6 12.6 %collective-permute-start.3 = (bf16[416,128]{1,0:T(8,128)(2,1)S(1)}, bf16[416,128]{1,0:T(8,128)(2,1)S(1)}, u32[]{:S(2)}, u32[]{:S(2)}) collective-permute-start(bf16[416,128]{1,0:T(8,128)(2,1)S(1)} %get-tuple-element.40), channel_id=1, source_target_pairs={{0,7},{1,6},{2,5},{3,4},{4,11},{5,10},{6,9},{7,8},{8,15},{9,14},{1... | collective-permute-start | bytes 319496 | tf_op jit(solution)/shard_map/ppermute | solution.py:675
  20.1 3.4 %collective-permute-start.4 = (bf16[3,32,16,128]{3,2,1,0:T(8,128)(2,1)S(1)}, bf16[3,32,16,128]{3,2,1,0:T(8,128)(2,1)S(1)}, u32[]{:S(2)}, u32[]{:S(2)}) collective-permute-start(bf16[3,32,16,128]{3,2,1,0:T(8,128)(2,1)S(1)} %collective-permute-done.prev), channel_id=1, source_target_pairs={{0,1},{1,0},{2,3},{3,2},{4,5},{5,4},{6,7},{7,6},{8,9},{9,8},{10,11... | collective-permute-start | bytes 1179656 | tf_op jit(solution)/shard_map/ppermute | solution.py:675
  26.6 13.3 %collective-permute-start.5 = (bf16[16,3,32,128]{3,2,1,0:T(8,128)(2,1)S(1)}, bf16[16,3,32,128]{3,2,1,0:T(8,128)(2,1)S(1)}, u32[]{:S(2)}, u32[]{:S(2)}) collective-permute-start(bf16[16,3,32,128]{3,2,1,0:T(8,128)(2,1)S(1)} %get-tuple-element.75), channel_id=1, source_target_pairs={{0,124},{1,125},{2,126},{3,127},{4,0},{5,1},{6,2},{7,3},{8,4},{9,5... | collective-permute-start | bytes 1179656 | tf_op jit(solution)/shard_map/ppermute | solution.py:675

commit v3 on v2

--- a/solution.py
+++ b/solution.py
@@ -55,6 +55,17 @@
 RIM = HID_ROWS - INNER
 INNER_PAIRS = [HALO + 2 * i for i in range(INNER // 2)]
 RIM_PAIRS = [0, 2, HALO + INNER, HALO + INNER + 2]
+FLD_INNER = FLD_ROWS - 2 * HALO
+DH_INNER = DH_ROWS - 2 * HALO
+OUT_INNER = TR - 2 * HALO
+
+
+def inner_rows(count, step=1):
+    return range(HALO, HALO + count, step)
+
+
+def rim_rows(count, step=1):
+    return [*range(0, HALO, step), *range(HALO + count, 2 * HALO + count, step)]
 
 
 def call(kernel, outs, scratch, mib, name, specs, *args):
@@ -101,15 +112,15 @@
 
 
 class Rows:
-    def __init__(self, inner, rim):
-        self.inner, self.rim = inner, rim
+    def __init__(self, inner, rim, count=INNER):
+        self.inner, self.rim, self.count = inner, rim, count
 
     def at(self, r):
         if r < HALO:
             return self.rim, r
-        if r < HALO + INNER:
+        if r < HALO + self.count:
             return self.inner, r - HALO
-        return self.rim, r - INNER
+        return self.rim, r - self.count
 
     def pair(self, r, first, n):
         ref, i = self.at(r)
@@ -397,7 +408,7 @@
 
 
 def rim_kernel(
-    sibling, outer, cot16, xd, wcur, wboth, bias, w2own, rcur, rhown, rtown, cot, xr
+    sibling, outer, cot16, xd, wcur, wboth, bias, w2own, rcur, rhown, rtown, rcot, xr
 ):
     odd = odd_tile()
     has = has_tiles()
@@ -407,15 +418,16 @@
         x, y = x.astype(F32), y.astype(F32)
         return jnp.where(odd, x, y) if side == 0 else jnp.where(odd, y, x)
 
-    for side, first in ((0, 0), (1, TR + 2)):
+    for side, first in ((0, 0), (1, 6)):
         ext = halo(side, EDGE, 32) * has[side]
         for s in range(OWN):
             for c in range(2):
                 at = s * 4 + c * 2
-                cot[s, c, first : first + 2, :] = ext[at : at + 2] + ext[12 + at : 14 + at]
+                rcot[s, c, first : first + 2, :] = ext[at : at + 2] + ext[12 + at : 14 + at]
     for s in range(OWN):
         for c in range(2):
-            cot[s, c, 2 : 2 + TR, :] = cot16[s, c]
+            rcot[s, c, 2:4, :] = cot16[s, c, 0:2, :]
+            rcot[s, c, 4:6, :] = cot16[s, c, TR - 2 :, :]
     spread_rim(lambda side, s, r: halo(side, (r * OWN + s) * CH, CH), has, xr)
     hidden_own(
         RIM_PAIRS, feature_rows(xd, xr), wcur, wboth, bias, w2own,
@@ -426,7 +438,7 @@
 def own_rim(*args):
     return call(
         rim_kernel,
-        hidden_outs(RIM) + [((OWN, 2, 24, COLS), F32)],
+        hidden_outs(RIM) + [((OWN, 2, 8, COLS), F32)],
         [((OWN, 2 * HALO, 3 * CH, COLS), BF16)],
         2,
         "own_rim",
@@ -435,53 +447,75 @@
     )
 
 
-def middle_kernel(prev, icur, itown, wear, w2first, w2rest, xp, ihmid, itsum, wide):
+def middle_kernel(
+    prev, icur, itown, cot16, consts, wear, w2first, w2rest, w2b, w2brest, wgear,
+    low, xp, ihmid, itsum, ig3, ivotes, idlow,
+    wide, fld, grd,
+):
     keep = (lax.axis_index("sec") > 0).astype(F32)
     for s in range(OWN):
         wide[s] = prev[s].astype(F32)
     spread_own(wide, keep, xp)
+    hmid, tsum = Rows(ihmid, None), Rows(itsum, None)
     hidden_borrowed(
         INNER_PAIRS, feature_rows(xp, None), wear, w2first, w2rest,
-        Rows(icur, None), Rows(itown, None), Rows(ihmid, None), Rows(itsum, None),
-    )
+        Rows(icur, None), Rows(itown, None), hmid, tsum,
+    )
+    fields_stage(inner_rows(FLD_INNER), tsum, consts.at[OWN], None, fld)
+    vote_stage(
+        FLD_INNER, consts, lambda s, c: cot16[s, c, 2 : TR - 2, :], fld, grd, ig3, ivotes
+    )
+    dlow = Rows(idlow, None, DH_INNER)
+    low_grad_stage(
+        inner_rows(DH_INNER, 2), w2b, w2brest, grad_rows(ig3, None), hmid, dlow
+    )
+    low_stage(inner_rows(OUT_INNER, 2), wgear, dlow, Rows(low, None, OUT_INNER))
 
 
 def middle(*args):
     return call(
         middle_kernel,
         [
+            ((OUT_INNER, OWN, CH, COLS), BF16),
             ((OWN, TR, 3 * CH, COLS), BF16),
             ((INNER, 6 * HID, COLS), BF16),
             ((INNER, OWN * 72, COLS), F32),
-        ],
-        [((OWN, CH, TR, COLS), F32)],
-        3,
+            ((OWN, FLD_INNER, 32, COLS), BF16),
+            ((OWN, 2, 16, COLS), F32),
+            ((DH_INNER, 3 * HID, COLS), BF16),
+        ],
+        [
+            ((OWN, CH, TR, COLS), F32),
+            ((OWN, FLD_INNER, 8, COLS), F32),
+            ((OWN, FLD_INNER, 8, COLS), F32),
+        ],
+        4,
         "middle",
         "v" * len(args),
         *args,
     )
 
 
-def fields_stage(tsum, bias2, has, fld):
-    for r in range(FLD_ROWS):
+def fields_stage(rows, tsum, bias2, has, fld):
+    for i, r in enumerate(rows):
         for s in range(OWN):
             sums = []
             for dx in range(3):
                 terms = []
                 for dy in range(3):
                     at = 72 * s + 8 * (3 * dy + dx)
-                    ref, i = tsum.at(r + dy)
-                    t = ref[i, at : at + 8, :]
+                    ref, j = tsum.at(r + dy)
+                    t = ref[j, at : at + 8, :]
                     if r + dy < 3:
                         t = t * has[0]
                     elif r + dy > HID_ROWS - 4:
                         t = t * has[1]
                     terms.append(t)
                 sums.append(terms[0] + terms[1] + terms[2])
-            fld[s, r] = (sums[1] + bias2[...]) + (from_left(sums[0]) + from_right(sums[2]))
-
-
-def vote_stage(consts, cot, fld, grd, g3, votes):
+            fld[s, i] = (sums[1] + bias2[...]) + (from_left(sums[0]) + from_right(sums[2]))
+
+
+def vote_stage(n, consts, cot_of, fld, grd, g3, votes):
     for s in range(OWN):
         f = [[fld[s, :, 2 * k + c, :] for c in range(2)] for k in range(3)]
         beta = consts[s, 0:1, :]
@@ -498,8 +532,8 @@
         w = [q * inv for q in expo]
         v = [w[0] * f[0][c] + w[1] * f[1][c] + w[2] * f[2][c] for c in range(2)]
         for c in range(2):
-            votes[s, c, 0:FLD_ROWS, :] = v[c]
-        g = [cot[s, c, 0:FLD_ROWS, :] for c in range(2)]
+            votes[s, c, 0:n, :] = v[c]
+        g = [cot_of(s, c) for c in range(2)]
         e = [
             -beta * w[k] * (g[0] * (f[k][0] - v[0]) + g[1] * (f[k][1] - v[1])) for k in range(3)
         ]
@@ -511,9 +545,9 @@
             grd[s, :, 0 + c, :] = w[0] * g[c] + m01 + m02
             grd[s, :, 2 + c, :] = w[1] * g[c] - m01 + m12
             grd[s, :, 4 + c, :] = w[2] * g[c] - m02 - m12
-        grd[s, :, 6, :] = jnp.zeros((FLD_ROWS, COLS), F32)
-        grd[s, :, 7, :] = jnp.zeros((FLD_ROWS, COLS), F32)
-    for r in range(FLD_ROWS):
+        grd[s, :, 6, :] = jnp.zeros((n, COLS), F32)
+        grd[s, :, 7, :] = jnp.zeros((n, COLS), F32)
+    for r in range(n):
         for s in range(OWN):
             x = grd[s, r]
             g3[s, r] = jnp.concatenate(
@@ -522,13 +556,13 @@
 
 
 def inside(ref, has):
-    for r, h in ((0, has[0]), (DH_ROWS - 1, has[1])):
+    for r, h in ((0, has[0]), (ref.shape[0] - 1, has[1])):
         ref[r] = (ref[r].astype(F32) * h).astype(BF16)
 
 
-def low_grad_stage(w2b, w2brest, g3, hmid, has, dlow):
-    for q in range(0, DH_ROWS, 2):
-        rhs = [taps((q + 2, q + 1, q), lambda r, s=s: g3[s, r]) for s in range(OWN)]
+def low_grad_stage(rows, w2b, w2brest, g3, hmid, dlow):
+    for q in rows:
+        rhs = [taps((q + 2, q + 1, q), lambda r, s=s: g3(s, r)) for s in range(OWN)]
         h = [hmid.pair(q + 2, 192 * j, 192).astype(F32) for j in range(2)]
         first = jnp.where(h[0] > 0.0, dot(w2b[...], rhs[0]), 0.0)
         rest = jnp.where(
@@ -542,8 +576,31 @@
             ],
             axis=0,
         ).astype(BF16)
-        halves(dlow, q, 0, low)
-    inside(dlow, has)
+        dlow.put(q, 0, low)
+
+
+def low_stage(rows, wgear, dlow, low):
+    for r in rows:
+        for s in range(OWN):
+
+            def pick(q, s=s):
+                ref, i = dlow.at(q)
+                return ref[i, HID * s : HID * s + HID, :]
+
+            p = dot(wgear[...], taps((r + 2, r + 1, r), pick))
+            for d in range(2):
+                ref, i = low.at(r + d)
+                ref[i, s] = gather_columns(p[:, COLS * d : COLS * d + COLS]).astype(BF16)
+
+
+def grad_rows(ig3, rg3):
+    rows = Rows(ig3, rg3, FLD_INNER)
+
+    def pick(s, r):
+        ref, i = rows.at(r)
+        return ref[s, i]
+
+    return pick
 
 
 def feature_grad_stage(dref, jobs, unroll):
@@ -560,10 +617,10 @@
 
 
 def borrowed_kernel(
-    psib, pouter, xp, rcur, rtown, itsum, ihmid, cot, consts,
+    psib, pouter, xp, rcur, rtown, itsum, ihmid, ig3, idlow, rcot, consts,
     wear, w2first, w2rest, w2b, w2brest, wgear,
-    low, rhmid, g3, votes,
-    wide, xr, rtsum, fld, grd, dlow,
+    low, rhmid, rg3, rvotes,
+    wide, xr, rtsum, fld, grd, rdlow,
 ):
     odd = odd_tile()
     has = has_tiles()
@@ -584,28 +641,30 @@
         RIM_PAIRS, feature_rows(xp, xr), wear, w2first, w2rest,
         Rows(None, rcur), Rows(None, rtown), hmid, tsum,
     )
-    fields_stage(tsum, consts.at[OWN], has, fld)
-    vote_stage(consts, cot, fld, grd, g3, votes)
-    low_grad_stage(w2b, w2brest, g3, hmid, has, dlow)
-    feature_grad_stage(dlow, [(64 * s, 64, wgear, low, s) for s in range(OWN)], True)
+    fields_stage(rim_rows(FLD_INNER), tsum, consts.at[OWN], has, fld)
+    vote_stage(2 * HALO, consts, lambda s, c: rcot[s, c], fld, grd, rg3, rvotes)
+    dlow = Rows(idlow, rdlow, DH_INNER)
+    low_grad_stage(rim_rows(DH_INNER, 2), w2b, w2brest, grad_rows(ig3, rg3), hmid, dlow)
+    inside(rdlow, has)
+    low_stage(rim_rows(OUT_INNER, 2), wgear, dlow, Rows(None, low, OUT_INNER))
 
 
 def borrowed(*args):
     return call(
         borrowed_kernel,
         [
-            ((TR, OWN, CH, COLS), BF16),
+            ((2 * HALO, OWN, CH, COLS), BF16),
             ((RIM, 6 * HID, COLS), BF16),
-            ((OWN, FLD_ROWS, 32, COLS), BF16),
-            ((OWN, 2, 24, COLS), F32),
+            ((OWN, 2 * HALO, 32, COLS), BF16),
+            ((OWN, 2, 8, COLS), F32),
         ],
         [
             ((OWN, CH, TR, COLS), F32),
             ((OWN, 2 * HALO, 3 * CH, COLS), BF16),
             ((RIM, OWN * 72, COLS), F32),
-            ((OWN, FLD_ROWS, 8, COLS), F32),
-            ((OWN, FLD_ROWS, 8, COLS), F32),
-            ((DH_ROWS, 3 * HID, COLS), BF16),
+            ((OWN, 2 * HALO, 8, COLS), F32),
+            ((OWN, 2 * HALO, 8, COLS), F32),
+            ((2 * HALO, 3 * HID, COLS), BF16),
         ],
         6,
         "borrowed",
@@ -615,13 +674,16 @@
 
 
 def own_grad_kernel(
-    votes, g3, ihown, rhown, ihmid, rhmid, w2b, wgcur, wgboth, voted, grad, down
+    ivotes, rvotes, ig3, rg3, ihown, rhown, ihmid, rhmid, w2b, wgcur, wgboth, voted, grad, down
 ):
     has = has_tiles()
     hown, hmid = Rows(ihown, rhown), Rows(ihmid, rhmid)
+    g3 = grad_rows(ig3, rg3)
     for s in range(OWN):
         for c in range(2):
-            voted[s, c] = votes[s, c, 2 : 2 + TR, :]
+            voted[s, c, 0:2, :] = rvotes[s, c, 2:4, :]
+            voted[s, c, 2 : TR - 2, :] = ivotes[s, c, 0:FLD_INNER, :]
+            voted[s, c, TR - 2 :, :] = rvotes[s, c, 4:6, :]
     for q in range(0, DH_ROWS, 2):
         ho = hown.pair(q + 2, 0, 192)
         hm = hmid.pair(q + 2, 0, 384)
@@ -632,7 +694,7 @@
         ]
         m = []
         for s in range(OWN):
-            dh = dot(w2b[...], taps((q + 2, q + 1, q), lambda r, s=s: g3[s, r]))
+            dh = dot(w2b[...], taps((q + 2, q + 1, q), lambda r, s=s: g3(s, r)))
             dh = jnp.where(h[s].astype(F32) > 0.0, dh, 0.0)
             m.append([dh[HID * k : HID * k + HID] for k in range(3)])
         c = [m[s][0] + m[s][1] + m[s][2] for s in range(OWN)]
@@ -658,20 +720,44 @@
     )
 
 
-def finish_kernel(grad, back, out):
+def finish_kernel(grad, iback, rback, out, block, sems):
     keep = (lax.axis_index("sec") < lax.axis_size("sec") - 1).astype(F32)
+    back = Rows(iback, rback, OUT_INNER)
+    copies = []
     for s in range(OWN):
         for r in range(TR):
-            out[s, :, r, :] = grad[r, s] + back[r, s].astype(F32) * keep
-
-
-def finish(grad, back):
-    return call(finish_kernel, [((OWN, CH, TR, COLS), F32)], [], 4, "finish", "vv", grad, back)[0]
-
-
-def move(value, secs, tile_to):
+            ref, i = back.at(r)
+            block[s, :, r, :] = grad[r, s] + ref[i, s].astype(F32) * keep
+        copies.append(pltpu.make_async_copy(block.at[s], out.at[s], sems.at[s]))
+        copies[-1].start()
+    for c in copies:
+        c.wait()
+
+
+def finish(*args):
+    vmem = pl.BlockSpec(memory_space=pltpu.VMEM)
+    return pl.pallas_call(
+        finish_kernel,
+        out_shape=jax.ShapeDtypeStruct((OWN, CH, TR, COLS), F32),
+        in_specs=[vmem] * len(args),
+        out_specs=pl.BlockSpec(memory_space=pltpu.HBM),
+        scratch_shapes=[
+            pltpu.VMEM((OWN, CH, TR, COLS), F32),
+            pltpu.SemaphoreType.DMA((OWN,)),
+        ],
+        compiler_params=params(2),
+        name="finish",
+    )(*args)
+
+
+def move(value, secs, tile_to, wrap=True):
     n, m = lax.axis_size("sec"), lax.axis_size("tile")
-    pairs = [(a * m + b, ((a + secs) % n) * m + tile_to(b)) for a in range(n) for b in range(m)]
+    pairs = [
+        (a * m + b, ((a + secs) % n) * m + tile_to(b))
+        for a in range(n)
+        for b in range(m)
+        if tile_to(b) is not None and (wrap or 0 <= a + secs < n)
+    ]
     return lax.ppermute(value, ("sec", "tile"), pairs)
 
 
@@ -687,7 +773,8 @@
         return b + 1 - 2 * (b % 2)
 
     def to_outer(b):
-        return (b - 1 + 2 * (b % 2)) % tiles
+        other = b - 1 + 2 * (b % 2)
+        return other if 0 <= other < tiles else None
 
     prev = move(features, 1, same)
     for_sibling, for_outer, wide, cot16, consts = edges(
@@ -695,24 +782,29 @@
     )
     sibling = move(for_sibling, 0, to_sibling)
     outer = move(for_outer, 0, to_outer)
-    pouter = move(for_outer, 1, to_outer)
+    pouter = move(for_outer, 1, to_outer, False)
     (
         wcur, wear, wboth, w2own, w2first, w2rest, w2b, w2brest, wgear, wgcur, wgboth, bias,
     ) = weights(first_kernel, second_kernel, first_bias[None])
     xd, icur, ihown, itown = own_inner(wide, wcur, wboth, bias, w2own)
-    rcur, rhown, rtown, cot = own_rim(
+    rcur, rhown, rtown, rcot = own_rim(
         sibling, outer, cot16, xd, wcur, wboth, bias, w2own
     )
     prev, rcur, pouter = lax.optimization_barrier((prev, rcur, pouter))
     psib = move(prev, 0, to_sibling)
-    xp, ihmid, itsum = middle(prev, icur, itown, wear, w2first, w2rest)
-    low, rhmid, g3, votes = borrowed(
-        psib, pouter, xp, rcur, rtown, itsum, ihmid, cot, consts,
+    ilow, xp, ihmid, itsum, ig3, ivotes, idlow = middle(
+        prev, icur, itown, cot16, consts, wear, w2first, w2rest, w2b, w2brest, wgear
+    )
+    iback = move(ilow, -1, same)
+    rlow, rhmid, rg3, rvotes = borrowed(
+        psib, pouter, xp, rcur, rtown, itsum, ihmid, ig3, idlow, rcot, consts,
         wear, w2first, w2rest, w2b, w2brest, wgear,
     )
-    back = move(low, -1, same)
-    voted, grad = own_grad(votes, g3, ihown, rhown, ihmid, rhmid, w2b, wgcur, wgboth)
-    return (voted, finish(grad, back))
+    rback = move(rlow, -1, same)
+    voted, grad = own_grad(
+        ivotes, rvotes, ig3, rg3, ihown, rhown, ihmid, rhmid, w2b, wgcur, wgboth
+    )
+    return (voted, finish(grad, iback, rback))
 
 
 def solution(mesh):

time: 41.9 us -> 40 us (0.955); the launches traced: 41.3 us -> 39.8 us
  waiting for transfers between devices: 12.6 us -> 6.82 us
  starting transfers between devices: 11.2 us -> 15 us
  Pallas kernels: 16.8 us -> 17.3 us
    ppermute x6 -> x7, waiting for transfers between devices: 12.6 us -> 6.82 us  [move(): return lax.ppermute(value, ('sec', 'tile'), pairs)]
    ppermute x6 -> x7, starting transfers between devices: 11.2 us -> 15 us  [move(): return lax.ppermute(value, ('sec', 'tile'), pairs)]
    pallas_call x0 -> x1, Pallas kernels: none -> 1.23 us  [finish(): pl.pallas_call(finish_kernel, out_shape=jax.ShapeDtypeStruct((OWN, CH, TR...]
    pallas_call x8 -> x7, Pallas kernels: 16.8 us -> 16 us  [call(): pl.pallas_call(kernel, out_shape=tuple((jax.ShapeDtypeStruct(shape, kind)...]
  transfers between devices with their start and end apart: 6 -> 7, of which waited for: 3 -> 2; matrix products, arithmetic and copies ran while one was open for 0% -> 0% of each run, Pallas kernels for 30% -> 40%
where the time goes in v3:
time: 40 us; the launch traced here: 39.8 us
  Pallas kernels  17.3 us (43%)
  starting transfers between devices  15 us (38%)
  waiting for transfers between devices  6.82 us (17%)
  between operations  0.72 us (2%)
    pallas_call x7, Pallas kernels, call(): pl.pallas_call(kernel, out_shape=tuple((jax.ShapeDtypeStruct(shape, kind)...  16 us
    ppermute x7, starting transfers between devices, move(): return lax.ppermute(value, ('sec', 'tile'), pairs)  15 us
    ppermute x7, waiting for transfers between devices, move(): return lax.ppermute(value, ('sec', 'tile'), pairs)  6.82 us
    pallas_call x1, Pallas kernels, finish(): pl.pallas_call(finish_kernel, out_shape=jax.ShapeDtypeStruct((OWN, CH, TR...  1.23 us
  transfers between devices with their start and end apart: 7, of which 2 were waited for; matrix products, arithmetic and copies ran while one was open for 0% of the time, Pallas kernels for 40%

profile of v3, /device:TPU:0, one launch (start us, length us, event | category | flops | bytes accessed | tf_op | source)
XLA Modules:
  0.0 39.8 jit_solution(2213979715888762253)
XLA Ops:
  0.6 4.0 %collective-permute-start = (bf16[3,32,16,128]{3,2,1,0:T(8,128)(2,1)}, bf16[3,32,16,128]{3,2,1,0:T(8,128)(2,1)S(1)}, u32[]{:S(2)}, u32[]{:S(2)}) collective-permute-start(bf16[3,32,16,128]{3,2,1,0:T(8,128)(2,1)} %feat_hbm.1), channel_id=1, source_target_pairs={{0,4},{1,5},{2,6},{3,7},{4,8},{5,9},{6,10},{7,11},{8,12},{9,13},{1... | collective-permute-start | bytes 1179656 | tf_op jit(solution)/shard_map/ppermute | solution.py:761
  4.7 1.7 %edges.1 = (bf16[416,128]{1,0:T(8,128)(2,1)S(1)}, bf16[416,128]{1,0:T(8,128)(2,1)S(1)}, f32[3,32,16,128]{3,2,1,0:T(8,128)S(1)}, f32[3,2,16,128]{3,2,1,0:T(8,128)S(1)}, f32[4,8,128]{2,1,0:T(8,128)S(1)}) custom-call(s32[3]{0:T(128)} %valid_hbm.1, f32[3]{0:T(128)} %sharp_hbm.1, f32[2]{0:T(128)} %b2_hbm.1, bf16[3,32,16,128]{3,2,1,0:T(8,128)(2,1)} %feat_hbm.1, ...), custom_call_target="tpu_custom_call" | custom-call | tf_op jit(solution)/shard_map/edges/pallas_call | solution.py:77
  6.3 0.7 %collective-permute-start.2 = (bf16[416,128]{1,0:T(8,128)(2,1)S(1)}, bf16[416,128]{1,0:T(8,128)(2,1)S(1)}, u32[]{:S(2)}, u32[]{:S(2)}) collective-permute-start(bf16[416,128]{1,0:T(8,128)(2,1)S(1)} %get-tuple-element.44), channel_id=1, source_target_pairs={{1,2},{2,1},{5,6},{6,5},{9,10},{10,9},{13,14},{14,13},{17,18},{18,... | collective-permute-start | bytes 319496 | tf_op jit(solution)/shard_map/ppermute | solution.py:761
  7.0 2.5 %collective-permute-start.1 = (bf16[416,128]{1,0:T(8,128)(2,1)S(1)}, bf16[416,128]{1,0:T(8,128)(2,1)S(1)}, u32[]{:S(2)}, u32[]{:S(2)}) collective-permute-start(bf16[416,128]{1,0:T(8,128)(2,1)S(1)} %get-tuple-element.43), channel_id=1, source_target_pairs={{0,1},{1,0},{2,3},{3,2},{4,5},{5,4},{6,7},{7,6},{8,9},{9,8},{10,11... | collective-permute-start | bytes 319496 | tf_op jit(solution)/shard_map/ppermute | solution.py:761
  9.5 0.7 %collective-permute-start.3 = (bf16[416,128]{1,0:T(8,128)(2,1)S(1)}, bf16[416,128]{1,0:T(8,128)(2,1)S(1)}, u32[]{:S(2)}, u32[]{:S(2)}) collective-permute-start(bf16[416,128]{1,0:T(8,128)(2,1)S(1)} %get-tuple-element.44), channel_id=1, source_target_pairs={{1,6},{2,5},{5,10},{6,9},{9,14},{10,13},{13,18},{14,17},{17,22},{1... | collective-permute-start | bytes 319496 | tf_op jit(solution)/shard_map/ppermute | solution.py:761
  10.1 1.5 %weights.1 = (bf16[64,288]{1,0:T(8,128)(2,1)S(1)}, bf16[64,288]{1,0:T(8,128)(2,1)S(1)}, bf16[128,288]{1,0:T(8,128)(2,1)S(1)}, bf16[144,192]{1,0:T(8,128)(2,1)S(1...) custom-call(bf16[3,3,64,64]{3,2,1,0:T(8,128)(2,1)} %k1_hbm.1, ...), custom_call_target="tpu_custom_call" | custom-call | tf_op jit(solution)/shard_map/weights/pallas_call | solution.py:77
  11.6 2.6 %own_inner.1 = (bf16[3,16,96,128]{3,2,1,0:T(8,128)(2,1)S(1)}, f32[14,192,128]{2,1,0:T(8,128)S(1)}, bf16[14,192,128]{2,1,0:T(8,128)(2,1)S(1)}, f32[14,144,128]{2,1,0:T(8,128)S(1)}) custom-call(f32[3,32,16,128]{3,2,1,0:T(8,128)S(1)} %get-tuple-element.46.wide, bf16[64,288]{1,0:T(8,128)(2,1)S(1)} %get-tuple-element.47.wcur, ...), custom_call_target="tpu_custom_call" | custom-call | tf_op jit(solution)/shard_map/own_inner/pallas_call | solution.py:77
  14.2 0.0 collective-permute-done.2.outer
  14.2 0.0 collective-permute-done.1.sibling
  14.2 1.3 %own_rim.1 = (f32[8,192,128]{2,1,0:T(8,128)S(1)}, bf16[8,192,128]{2,1,0:T(8,128)(2,1)S(1)}, f32[8,144,128]{2,1,0:T(8,128)S(1)}, f32[3,2,8,128]{3,2,1,0:T(8,128)S(1)}) custom-call(bf16[416,128]{1,0:T(8,128)(2,1)S(1)} %collective-permute-done.1.sibling, bf16[416,128]{1,0:T(8,128)(2,1)S(1)} %collective-permute-done.2.outer, ...), custom_call_target="tpu_custom_call" | custom-call | tf_op jit(solution)/shard_map/own_rim/pallas_call | solution.py:77
  15.5 0.0 collective-permute-done.3.pouter
  15.5 3.2 %collective-permute-done.prev = bf16[3,32,16,128]{3,2,1,0:T(8,128)(2,1)S(1)} collective-permute-done((bf16[3,32,16,128]{3,2,1,0:T(8,128)(2,1)}, bf16[3,32,16,128]{3,2,1,0:T(8,128)(2,1)S(1)}, u32[]{:S(2)}, u32[]{:S(2)}) %collective-permute-start) | collective-permute-done | bytes 393248 | tf_op jit(solution)/shard_map/ppermute | solution.py:761
  18.7 0.0 collective-permute-start.4
  18.7 3.9 %middle.1 = (bf16[8,3,32,128]{3,2,1,0:T(8,128)(2,1)S(1)}, bf16[3,16,96,128]{3,2,1,0:T(8,128)(2,1)S(1)}, bf16[14,384,128]{2,1,0:T(8,128)(2,1)S(1)}, f32[14,216,12...) custom-call(bf16[3,32,16,128]{3,2,1,0:T(8,128)(2,1)S(1)} %collective, ...), custom_call_target="tpu_custom_call" | custom-call | flops 2305999872 | tf_op jit(solution)/shard_map/middle/pallas_call | solution.py:77
  22.7 5.4 %collective-permute-start.5 = (bf16[8,3,32,128]{3,2,1,0:T(8,128)(2,1)S(1)}, bf16[8,3,32,128]{3,2,1,0:T(8,128)(2,1)S(1)}, u32[]{:S(2)}, u32[]{:S(2)}) collective-permute-start(bf16[8,3,32,128]{3,2,1,0:T(8,128)(2,1)S(1)} %get-tuple-element.82), channel_id=1, source_target_pairs={{0,124},{1,125},{2,126},{3,127},{4,0},{5,1},{6,2},{7,3},{8,4},{9,5... | collective-permute-start | bytes 589832 | tf_op jit(solution)/shard_map/ppermute | solution.py:761
  28.1 0.0 collective-permute-done.4.psib
  28.1 2.4 %borrowed.1 = (bf16[8,3,32,128]{3,2,1,0:T(8,128)(2,1)S(1)}, bf16[8,384,128]{2,1,0:T(8,128)(2,1)S(1)}, bf16[3,8,32,128]{3,2,1,0:T(8,128)(2,1)S(1)}, f32[3,2,8,128]{3,2,1,0:T(8,128)S(1)}) custom-call(bf16[3,32,16,128]{3,2,1,0:T(8,128)(2,1)S(1)} %collective-permute-done.4.psib, bf16[416,128]{1,0:T(8,128)(2,1)S(1)} %collective-permute-done.3.pouter, ...), custom_call_target="tpu_custom_call" | custom-call | flops 3459000064 | tf_op jit(solution)/shard_map/borrowed/pallas_call | solution.py:77
  30.5 1.8 %collective-permute-start.6 = (bf16[8,3,32,128]{3,2,1,0:T(8,128)(2,1)S(1)}, bf16[8,3,32,128]{3,2,1,0:T(8,128)(2,1)S(1)}, u32[]{:S(2)}, u32[]{:S(2)}) collective-permute-start(bf16[8,3,32,128]{3,2,1,0:T(8,128)(2,1)S(1)} %get-tuple-element.83), channel_id=1, source_target_pairs={{0,124},{1,125},{2,126},{3,127},{4,0},{5,1},{6,2},{7,3},{8,4},{9,5... | collective-permute-start | bytes 589832 | tf_op jit(solution)/shard_map/ppermute | solution.py:761
  32.3 2.8 %own_grad.1 = (f32[3,2,16,128]{3,2,1,0:T(8,128)}, f32[16,3,32,128]{3,2,1,0:T(8,128)S(1)}) custom-call(f32[3,2,16,128]{3,2,1,0:T(8,128)S(1)} %get-tuple-element.63.ivotes, f32[3,2,8,128]{3,2,1,0:T(8,128)S(1)} %get-tuple-element.73.rvotes, bf16[3,12,32,128]{3,2,1,0:T(8,128)(2,1)S(1)} %get-tuple-element.70.ig3, ...), custom_call_target="tpu_custom_call" | custom-call | flops 3459000064 | tf_op jit(solution)/shard_map/own_grad/pallas_call | solution.py:77
  35.0 0.0 collective-permute-done.5.iback
  35.0 3.6 %collective-permute-done.6.rback = bf16[8,3,32,128]{3,2,1,0:T(8,128)(2,1)S(1)} collective-permute-done((bf16[8,3,32,128]{3,2,1,0:T(8,128)(2,1)S(1)}, bf16[8,3,32,128]{3,2,1,0:T(8,128)(2,1)S(1)}, u32[]{:S(2)}, u32[]{:S(2)}) %collective-permute-start.6) | collective-permute-done | bytes 196640 | tf_op jit(solution)/shard_map/ppermute | solution.py:761
  38.6 1.2 %finish.1 = f32[3,32,16,128]{3,2,1,0:T(8,128)} custom-call(f32[16,3,32,128]{3,2,1,0:T(8,128)S(1)} %get-tuple-element.81.grad, bf16[8,3,32,128]{3,2,1,0:T(8,128)(2,1)S(1)} %collective-permute-done.5.iback, bf16[8,3,32,128]{3,2,1,0:T(8,128)(2,1)S(1)} %collective-permute-done.6.rback), custom_call_target="tpu_custom_call" | custom-call | tf_op jit(solution)/shard_map/finish/pallas_call | solution.py:739
Async XLA Ops:
  0.6 18.1 %collective-permute-start = (bf16[3,32,16,128]{3,2,1,0:T(8,128)(2,1)}, bf16[3,32,16,128]{3,2,1,0:T(8,128)(2,1)S(1)}, u32[]{:S(2)}, u32[]{:S(2)}) collective-permute-start(bf16[3,32,16,128]{3,2,1,0:T(8,128)(2,1)} %feat_hbm.1), channel_id=1, source_target_pairs={{0,4},{1,5},{2,6},{3,7},{4,8},{5,9},{6,10},{7,11},{8,12},{9,13},{1... | collective-permute-start | bytes 1179656 | tf_op jit(solution)/shard_map/ppermute | solution.py:761
  6.3 7.8 %collective-permute-start.2 = (bf16[416,128]{1,0:T(8,128)(2,1)S(1)}, bf16[416,128]{1,0:T(8,128)(2,1)S(1)}, u32[]{:S(2)}, u32[]{:S(2)}) collective-permute-start(bf16[416,128]{1,0:T(8,128)(2,1)S(1)} %get-tuple-element.44), channel_id=1, source_target_pairs={{1,2},{2,1},{5,6},{6,5},{9,10},{10,9},{13,14},{14,13},{17,18},{18,... | collective-permute-start | bytes 319496 | tf_op jit(solution)/shard_map/ppermute | solution.py:761
  7.0 7.2 %collective-permute-start.1 = (bf16[416,128]{1,0:T(8,128)(2,1)S(1)}, bf16[416,128]{1,0:T(8,128)(2,1)S(1)}, u32[]{:S(2)}, u32[]{:S(2)}) collective-permute-start(bf16[416,128]{1,0:T(8,128)(2,1)S(1)} %get-tuple-element.43), channel_id=1, source_target_pairs={{0,1},{1,0},{2,3},{3,2},{4,5},{5,4},{6,7},{7,6},{8,9},{9,8},{10,11... | collective-permute-start | bytes 319496 | tf_op jit(solution)/shard_map/ppermute | solution.py:761
  9.5 6.0 %collective-permute-start.3 = (bf16[416,128]{1,0:T(8,128)(2,1)S(1)}, bf16[416,128]{1,0:T(8,128)(2,1)S(1)}, u32[]{:S(2)}, u32[]{:S(2)}) collective-permute-start(bf16[416,128]{1,0:T(8,128)(2,1)S(1)} %get-tuple-element.44), channel_id=1, source_target_pairs={{1,6},{2,5},{5,10},{6,9},{9,14},{10,13},{13,18},{14,17},{17,22},{1... | collective-permute-start | bytes 319496 | tf_op jit(solution)/shard_map/ppermute | solution.py:761
  18.7 9.4 %collective-permute-start.4 = (bf16[3,32,16,128]{3,2,1,0:T(8,128)(2,1)S(1)}, bf16[3,32,16,128]{3,2,1,0:T(8,128)(2,1)S(1)}, u32[]{:S(2)}, u32[]{:S(2)}) collective-permute-start(bf16[3,32,16,128]{3,2,1,0:T(8,128)(2,1)S(1)} %collective-permute-done.prev), channel_id=1, source_target_pairs={{0,1},{1,0},{2,3},{3,2},{4,5},{5,4},{6,7},{7,6},{8,9},{9,8},{10,11... | collective-permute-start | bytes 1179656 | tf_op jit(solution)/shard_map/ppermute | solution.py:761
  22.7 12.3 %collective-permute-start.5 = (bf16[8,3,32,128]{3,2,1,0:T(8,128)(2,1)S(1)}, bf16[8,3,32,128]{3,2,1,0:T(8,128)(2,1)S(1)}, u32[]{:S(2)}, u32[]{:S(2)}) collective-permute-start(bf16[8,3,32,128]{3,2,1,0:T(8,128)(2,1)S(1)} %get-tuple-element.82), channel_id=1, source_target_pairs={{0,124},{1,125},{2,126},{3,127},{4,0},{5,1},{6,2},{7,3},{8,4},{9,5... | collective-permute-start | bytes 589832 | tf_op jit(solution)/shard_map/ppermute | solution.py:761
  30.5 8.1 %collective-permute-start.6 = (bf16[8,3,32,128]{3,2,1,0:T(8,128)(2,1)S(1)}, bf16[8,3,32,128]{3,2,1,0:T(8,128)(2,1)S(1)}, u32[]{:S(2)}, u32[]{:S(2)}) collective-permute-start(bf16[8,3,32,128]{3,2,1,0:T(8,128)(2,1)S(1)} %get-tuple-element.83), channel_id=1, source_target_pairs={{0,124},{1,125},{2,126},{3,127},{4,0},{5,1},{6,2},{7,3},{8,4},{9,5... | collective-permute-start | bytes 589832 | tf_op jit(solution)/shard_map/ppermute | solution.py:761

commit v4 on v3

--- a/solution.py
+++ b/solution.py
@@ -98,8 +98,7 @@
     copies = [pltpu.make_async_copy(a, b, sems.at[i]) for i, (a, b) in enumerate(moves)]
     for c in copies:
         c.start()
-    for c in copies:
-        c.wait()
+    return copies
 
 
 def odd_tile():
@@ -132,14 +131,17 @@
 
 
 def edges_kernel(
-    valid_hbm, sharp_hbm, b2_hbm, feat_hbm, vgrad_hbm,
-    sibling, outer, wide, cot, consts,
+    valid_hbm, sharp_hbm, b2_hbm, feat_hbm, vgrad_hbm, k1_hbm, k2_hbm, b1_hbm,
+    sibling, outer, wide, cot, consts, k1, k2, b1,
     valid, sharp, b2, feat, vgrad, ext, sems,
 ):
-    fetch(
+    copies = fetch(
         sems,
         (feat_hbm, feat), (vgrad_hbm, vgrad), (valid_hbm, valid), (sharp_hbm, sharp), (b2_hbm, b2),
-    )
+        (k1_hbm, k1), (k2_hbm, k2), (b1_hbm, b1),
+    )
+    for c in copies[:5]:
+        c.wait()
     row0 = lax.axis_index("tile") * TR
     odd = odd_tile()
     for s in range(OWN):
@@ -160,14 +162,18 @@
                 ext[at : at + 2, :] = high
                 ext[12 + at : 14 + at, :] = x - high
         out[EDGE:, :] = ext[...].astype(BF16)
-        for s in range(OWN):
-            for r in range(HALO):
-                at = (r * OWN + s) * CH
-                x = jnp.where(last, wide[s, :, TR - HALO + r, :], wide[s, :, r, :])
-                out[at : at + CH, :] = x.astype(BF16)
+    for s in range(OWN):
+        for r in range(HALO):
+            at = (r * OWN + s) * CH
+            top, bottom = wide[s, :, r, :], wide[s, :, TR - HALO + r, :]
+            sibling[at : at + CH, :] = jnp.where(odd, top, bottom).astype(BF16)
+            outer[at : at + CH, :] = jnp.where(odd, bottom, top).astype(BF16)
+    for c in copies[5:]:
+        c.wait()
 
 
 def edges(*args):
+    k1, k2, b1 = args[5:]
     return call(
         edges_kernel,
         [
@@ -176,6 +182,9 @@
             ((OWN, CH, TR, COLS), F32),
             ((OWN, 2, TR, COLS), F32),
             ((OWN + 1, 8, COLS), F32),
+            (k1.shape, BF16),
+            (k2.shape, BF16),
+            (b1.shape, F32),
         ],
         [
             (pltpu.SMEM, (OWN,), jnp.int32),
@@ -184,20 +193,19 @@
             ((OWN, CH, TR, COLS), BF16),
             ((OWN, 2, TR, COLS), F32),
             ((32, COLS), F32),
-            (sems, (5,), None),
+            (sems, (8,), None),
         ],
         3,
         "edges",
-        "hhhhh",
+        "hhhhhhhh",
         *args,
     )
 
 
 def weights_kernel(
-    k1_hbm, k2_hbm, b1_hbm, wcur, wear, wboth, w2own, w2first, w2rest, w2b, w2brest, wgear, wgcur, wgboth, bias,
-    k1, k2, b1, fwd, bwd, both, two, sq, sems,
+    k1, k2, b1, wcur, wear, wboth, w2own, w2first, w2rest, w2b, w2brest, wgear, wgcur, wgboth, bias,
+    fwd, bwd, both, two, sq,
 ):
-    fetch(sems, (k1_hbm, k1), (k2_hbm, k2), (b1_hbm, b1))
     bias[...] = jnp.broadcast_to(b1[...], (COLS, HID)).T
     for dy in range(3):
         for dx in range(3):
@@ -273,19 +281,15 @@
             ((HID, COLS), F32),
         ],
         [
-            (k1.shape, BF16),
-            (k2.shape, BF16),
-            (b1.shape, F32),
             ((2 * HID, 9 * CH), F32),
             ((6 * CH, 3 * HID), F32),
             ((3 * CH, 6 * HID), F32),
             ((144, 192), F32),
             ((192, 192), F32),
-            (sems, (3,), None),
         ],
         4,
         "weights",
-        "hhh",
+        "vvv",
         k1,
         k2,
         b1,
@@ -752,12 +756,14 @@
 
 def move(value, secs, tile_to, wrap=True):
     n, m = lax.axis_size("sec"), lax.axis_size("tile")
-    pairs = [
-        (a * m + b, ((a + secs) % n) * m + tile_to(b))
-        for a in range(n)
-        for b in range(m)
-        if tile_to(b) is not None and (wrap or 0 <= a + secs < n)
-    ]
+    pairs = []
+    for a in range(n):
+        for b in range(m):
+            to = tile_to(b)
+            if wrap:
+                pairs.append((a * m + b, a * m + b if to is None else ((a + secs) % n) * m + to))
+            elif to is not None and 0 <= a + secs < n:
+                pairs.append((a * m + b, (a + secs) * m + to))
     return lax.ppermute(value, ("sec", "tile"), pairs)
 
 
@@ -777,15 +783,16 @@
         return other if 0 <= other < tiles else None
 
     prev = move(features, 1, same)
-    for_sibling, for_outer, wide, cot16, consts = edges(
-        valid_rows, sharpness, second_bias, features, vote_grad
+    for_sibling, for_outer, wide, cot16, consts, k1, k2, b1 = edges(
+        valid_rows, sharpness, second_bias, features, vote_grad,
+        first_kernel, second_kernel, first_bias[None],
     )
     sibling = move(for_sibling, 0, to_sibling)
     outer = move(for_outer, 0, to_outer)
     pouter = move(for_outer, 1, to_outer, False)
     (
         wcur, wear, wboth, w2own, w2first, w2rest, w2b, w2brest, wgear, wgcur, wgboth, bias,
-    ) = weights(first_kernel, second_kernel, first_bias[None])
+    ) = weights(k1, k2, b1)
     xd, icur, ihown, itown = own_inner(wide, wcur, wboth, bias, w2own)
     rcur, rhown, rtown, rcot = own_rim(
         sibling, outer, cot16, xd, wcur, wboth, bias, w2own

time: 40 us -> 40 us (level)
  Pallas kernels: 17.3 us -> 16.5 us
  waiting for transfers between devices: 6.82 us -> 7.52 us
    pallas_call x7, Pallas kernels: 16 us -> 15.2 us  [call(): pl.pallas_call(kernel, out_shape=tuple((jax.ShapeDtypeStruct(shape, kind)...]
    ppermute x7, waiting for transfers between devices: 6.82 us -> 7.52 us  [move(): return lax.ppermute(value, ('sec', 'tile'), pairs)]
  transfers between devices with their start and end apart: 7 -> 7, of which waited for: 2 -> 2; matrix products, arithmetic and copies ran while one was open for 0% -> 0% of each run, Pallas kernels for 40% -> 38%
where the time goes in v4:
time: 40 us; the launch traced here: 39.8 us
  Pallas kernels  16.5 us (41%)
  starting transfers between devices  15.1 us (38%)
  waiting for transfers between devices  7.52 us (19%)
  between operations  0.72 us (2%)
    pallas_call x7, Pallas kernels, call(): pl.pallas_call(kernel, out_shape=tuple((jax.ShapeDtypeStruct(shape, kind)...  15.2 us
    ppermute x7, starting transfers between devices, move(): return lax.ppermute(value, ('sec', 'tile'), pairs)  15.1 us
    ppermute x7, waiting for transfers between devices, move(): return lax.ppermute(value, ('sec', 'tile'), pairs)  7.52 us
    pallas_call x1, Pallas kernels, finish(): pl.pallas_call(finish_kernel, out_shape=jax.ShapeDtypeStruct((OWN, CH, TR...  1.23 us
  transfers between devices with their start and end apart: 7, of which 2 were waited for; matrix products, arithmetic and copies ran while one was open for 0% of the time, Pallas kernels for 38%

profile of v4, /device:TPU:0, one launch (start us, length us, event | category | flops | bytes accessed | tf_op | source)
XLA Modules:
  0.0 39.8 jit_solution(11083583624546869188)
XLA Ops:
  0.6 4.0 %collective-permute-start = (bf16[3,32,16,128]{3,2,1,0:T(8,128)(2,1)}, bf16[3,32,16,128]{3,2,1,0:T(8,128)(2,1)S(1)}, u32[]{:S(2)}, u32[]{:S(2)}) collective-permute-start(bf16[3,32,16,128]{3,2,1,0:T(8,128)(2,1)} %feat_hbm.1), channel_id=1, source_target_pairs={{0,4},{1,5},{2,6},{3,7},{4,8},{5,9},{6,10},{7,11},{8,12},{9,13},{1... | collective-permute-start | bytes 1179656 | tf_op jit(solution)/shard_map/ppermute | solution.py:767
  4.7 1.8 %edges.1 = (bf16[416,128]{1,0:T(8,128)(2,1)S(1)}, bf16[416,128]{1,0:T(8,128)(2,1)S(1)}, f32[3,32,16,128]{3,2,1,0:T(8,128)S(1)}, f32[3,2,16,128]{3,2,1,0:T(8,128)...) custom-call(s32[3]{0:T(128)} %valid_hbm.1, ...), custom_call_target="tpu_custom_call" | custom-call | tf_op jit(solution)/shard_map/edges/pallas_call | solution.py:77
  6.5 0.7 %collective-permute-start.2 = (bf16[416,128]{1,0:T(8,128)(2,1)S(1)}, bf16[416,128]{1,0:T(8,128)(2,1)S(1)}, u32[]{:S(2)}, u32[]{:S(2)}) collective-permute-start(bf16[416,128]{1,0:T(8,128)(2,1)S(1)} %get-tuple-element.47), channel_id=1, source_target_pairs={{0,0},{1,2},{2,1},{3,3},{4,4},{5,6},{6,5},{7,7},{8,8},{9,10},{10,9... | collective-permute-start | bytes 319496 | tf_op jit(solution)/shard_map/ppermute | solution.py:767
  7.1 2.5 %collective-permute-start.1 = (bf16[416,128]{1,0:T(8,128)(2,1)S(1)}, bf16[416,128]{1,0:T(8,128)(2,1)S(1)}, u32[]{:S(2)}, u32[]{:S(2)}) collective-permute-start(bf16[416,128]{1,0:T(8,128)(2,1)S(1)} %get-tuple-element.46), channel_id=1, source_target_pairs={{0,1},{1,0},{2,3},{3,2},{4,5},{5,4},{6,7},{7,6},{8,9},{9,8},{10,11... | collective-permute-start | bytes 319496 | tf_op jit(solution)/shard_map/ppermute | solution.py:767
  9.6 0.7 %collective-permute-start.3 = (bf16[416,128]{1,0:T(8,128)(2,1)S(1)}, bf16[416,128]{1,0:T(8,128)(2,1)S(1)}, u32[]{:S(2)}, u32[]{:S(2)}) collective-permute-start(bf16[416,128]{1,0:T(8,128)(2,1)S(1)} %get-tuple-element.47), channel_id=1, source_target_pairs={{1,6},{2,5},{5,10},{6,9},{9,14},{10,13},{13,18},{14,17},{17,22},{1... | collective-permute-start | bytes 319496 | tf_op jit(solution)/shard_map/ppermute | solution.py:767
  10.3 0.5 %weights.1 = (bf16[64,288]{1,0:T(8,128)(2,1)S(1)}, bf16[64,288]{1,0:T(8,128)(2,1)S(1)}, bf16[128,288]{1,0:T(8,128)(2,1)S(1)}, bf16[144,192]{1,0:T(8,128)(2,1)S(1...) custom-call(bf16[3,3,64,64]{3,2,1,0:T(8,128)(2,1)S(1)} %get-tuple-el, ...), custom_call_target="tpu_custom_call" | custom-call | tf_op jit(solution)/shard_map/weights/pallas_call | solution.py:77
  10.8 2.6 %own_inner.1 = (bf16[3,16,96,128]{3,2,1,0:T(8,128)(2,1)S(1)}, f32[14,192,128]{2,1,0:T(8,128)S(1)}, bf16[14,192,128]{2,1,0:T(8,128)(2,1)S(1)}, f32[14,144,128]{2,1,0:T(8,128)S(1)}) custom-call(f32[3,32,16,128]{3,2,1,0:T(8,128)S(1)} %get-tuple-element.49.wide, bf16[64,288]{1,0:T(8,128)(2,1)S(1)} %get-tuple-element.53.wcur, ...), custom_call_target="tpu_custom_call" | custom-call | tf_op jit(solution)/shard_map/own_inner/pallas_call | solution.py:77
  13.3 0.0 collective-permute-done.2.outer
  13.4 0.0 collective-permute-done.1.sibling
  13.4 1.3 %own_rim.1 = (f32[8,192,128]{2,1,0:T(8,128)S(1)}, bf16[8,192,128]{2,1,0:T(8,128)(2,1)S(1)}, f32[8,144,128]{2,1,0:T(8,128)S(1)}, f32[3,2,8,128]{3,2,1,0:T(8,128)S(1)}) custom-call(bf16[416,128]{1,0:T(8,128)(2,1)S(1)} %collective-permute-done.1.sibling, bf16[416,128]{1,0:T(8,128)(2,1)S(1)} %collective-permute-done.2.outer, ...), custom_call_target="tpu_custom_call" | custom-call | tf_op jit(solution)/shard_map/own_rim/pallas_call | solution.py:77
  14.7 0.0 collective-permute-done.3.pouter
  14.7 4.1 %collective-permute-done.prev = bf16[3,32,16,128]{3,2,1,0:T(8,128)(2,1)S(1)} collective-permute-done((bf16[3,32,16,128]{3,2,1,0:T(8,128)(2,1)}, bf16[3,32,16,128]{3,2,1,0:T(8,128)(2,1)S(1)}, u32[]{:S(2)}, u32[]{:S(2)}) %collective-permute-start) | collective-permute-done | bytes 393248 | tf_op jit(solution)/shard_map/ppermute | solution.py:767
  18.7 0.0 collective-permute-start.4
  18.7 3.9 %middle.1 = (bf16[8,3,32,128]{3,2,1,0:T(8,128)(2,1)S(1)}, bf16[3,16,96,128]{3,2,1,0:T(8,128)(2,1)S(1)}, bf16[14,384,128]{2,1,0:T(8,128)(2,1)S(1)}, f32[14,216,12...) custom-call(bf16[3,32,16,128]{3,2,1,0:T(8,128)(2,1)S(1)} %collective, ...), custom_call_target="tpu_custom_call" | custom-call | flops 2305999872 | tf_op jit(solution)/shard_map/middle/pallas_call | solution.py:77
  22.7 5.4 %collective-permute-start.5 = (bf16[8,3,32,128]{3,2,1,0:T(8,128)(2,1)S(1)}, bf16[8,3,32,128]{3,2,1,0:T(8,128)(2,1)S(1)}, u32[]{:S(2)}, u32[]{:S(2)}) collective-permute-start(bf16[8,3,32,128]{3,2,1,0:T(8,128)(2,1)S(1)} %get-tuple-element.88), channel_id=1, source_target_pairs={{0,124},{1,125},{2,126},{3,127},{4,0},{5,1},{6,2},{7,3},{8,4},{9,5... | collective-permute-start | bytes 589832 | tf_op jit(solution)/shard_map/ppermute | solution.py:767
  28.1 0.0 collective-permute-done.4.psib
  28.1 2.4 %borrowed.1 = (bf16[8,3,32,128]{3,2,1,0:T(8,128)(2,1)S(1)}, bf16[8,384,128]{2,1,0:T(8,128)(2,1)S(1)}, bf16[3,8,32,128]{3,2,1,0:T(8,128)(2,1)S(1)}, f32[3,2,8,128]{3,2,1,0:T(8,128)S(1)}) custom-call(bf16[3,32,16,128]{3,2,1,0:T(8,128)(2,1)S(1)} %collective-permute-done.4.psib, bf16[416,128]{1,0:T(8,128)(2,1)S(1)} %collective-permute-done.3.pouter, ...), custom_call_target="tpu_custom_call" | custom-call | flops 3459000064 | tf_op jit(solution)/shard_map/borrowed/pallas_call | solution.py:77
  30.5 1.9 %collective-permute-start.6 = (bf16[8,3,32,128]{3,2,1,0:T(8,128)(2,1)S(1)}, bf16[8,3,32,128]{3,2,1,0:T(8,128)(2,1)S(1)}, u32[]{:S(2)}, u32[]{:S(2)}) collective-permute-start(bf16[8,3,32,128]{3,2,1,0:T(8,128)(2,1)S(1)} %get-tuple-element.89), channel_id=1, source_target_pairs={{0,124},{1,125},{2,126},{3,127},{4,0},{5,1},{6,2},{7,3},{8,4},{9,5... | collective-permute-start | bytes 589832 | tf_op jit(solution)/shard_map/ppermute | solution.py:767
  32.4 2.8 %own_grad.1 = (f32[3,2,16,128]{3,2,1,0:T(8,128)}, f32[16,3,32,128]{3,2,1,0:T(8,128)S(1)}) custom-call(f32[3,2,16,128]{3,2,1,0:T(8,128)S(1)} %get-tuple-element.69.ivotes, f32[3,2,8,128]{3,2,1,0:T(8,128)S(1)} %get-tuple-element.79.rvotes, bf16[3,12,32,128]{3,2,1,0:T(8,128)(2,1)S(1)} %get-tuple-element.76.ig3, ...), custom_call_target="tpu_custom_call" | custom-call | flops 3459000064 | tf_op jit(solution)/shard_map/own_grad/pallas_call | solution.py:77
  35.1 0.0 collective-permute-done.5.iback
  35.1 3.5 %collective-permute-done.6.rback = bf16[8,3,32,128]{3,2,1,0:T(8,128)(2,1)S(1)} collective-permute-done((bf16[8,3,32,128]{3,2,1,0:T(8,128)(2,1)S(1)}, bf16[8,3,32,128]{3,2,1,0:T(8,128)(2,1)S(1)}, u32[]{:S(2)}, u32[]{:S(2)}) %collective-permute-start.6) | collective-permute-done | bytes 196640 | tf_op jit(solution)/shard_map/ppermute | solution.py:767
  38.6 1.2 %finish.1 = f32[3,32,16,128]{3,2,1,0:T(8,128)} custom-call(f32[16,3,32,128]{3,2,1,0:T(8,128)S(1)} %get-tuple-element.87.grad, bf16[8,3,32,128]{3,2,1,0:T(8,128)(2,1)S(1)} %collective-permute-done.5.iback, bf16[8,3,32,128]{3,2,1,0:T(8,128)(2,1)S(1)} %collective-permute-done.6.rback), custom_call_target="tpu_custom_call" | custom-call | tf_op jit(solution)/shard_map/finish/pallas_call | solution.py:743
Async XLA Ops:
  0.6 18.1 %collective-permute-start = (bf16[3,32,16,128]{3,2,1,0:T(8,128)(2,1)}, bf16[3,32,16,128]{3,2,1,0:T(8,128)(2,1)S(1)}, u32[]{:S(2)}, u32[]{:S(2)}) collective-permute-start(bf16[3,32,16,128]{3,2,1,0:T(8,128)(2,1)} %feat_hbm.1), channel_id=1, source_target_pairs={{0,4},{1,5},{2,6},{3,7},{4,8},{5,9},{6,10},{7,11},{8,12},{9,13},{1... | collective-permute-start | bytes 1179656 | tf_op jit(solution)/shard_map/ppermute | solution.py:767
  6.5 6.9 %collective-permute-start.2 = (bf16[416,128]{1,0:T(8,128)(2,1)S(1)}, bf16[416,128]{1,0:T(8,128)(2,1)S(1)}, u32[]{:S(2)}, u32[]{:S(2)}) collective-permute-start(bf16[416,128]{1,0:T(8,128)(2,1)S(1)} %get-tuple-element.47), channel_id=1, source_target_pairs={{0,0},{1,2},{2,1},{3,3},{4,4},{5,6},{6,5},{7,7},{8,8},{9,10},{10,9... | collective-permute-start | bytes 319496 | tf_op jit(solution)/shard_map/ppermute | solution.py:767
  7.1 6.2 %collective-permute-start.1 = (bf16[416,128]{1,0:T(8,128)(2,1)S(1)}, bf16[416,128]{1,0:T(8,128)(2,1)S(1)}, u32[]{:S(2)}, u32[]{:S(2)}) collective-permute-start(bf16[416,128]{1,0:T(8,128)(2,1)S(1)} %get-tuple-element.46), channel_id=1, source_target_pairs={{0,1},{1,0},{2,3},{3,2},{4,5},{5,4},{6,7},{7,6},{8,9},{9,8},{10,11... | collective-permute-start | bytes 319496 | tf_op jit(solution)/shard_map/ppermute | solution.py:767
  9.6 5.1 %collective-permute-start.3 = (bf16[416,128]{1,0:T(8,128)(2,1)S(1)}, bf16[416,128]{1,0:T(8,128)(2,1)S(1)}, u32[]{:S(2)}, u32[]{:S(2)}) collective-permute-start(bf16[416,128]{1,0:T(8,128)(2,1)S(1)} %get-tuple-element.47), channel_id=1, source_target_pairs={{1,6},{2,5},{5,10},{6,9},{9,14},{10,13},{13,18},{14,17},{17,22},{1... | collective-permute-start | bytes 319496 | tf_op jit(solution)/shard_map/ppermute | solution.py:767
  18.7 9.4 %collective-permute-start.4 = (bf16[3,32,16,128]{3,2,1,0:T(8,128)(2,1)S(1)}, bf16[3,32,16,128]{3,2,1,0:T(8,128)(2,1)S(1)}, u32[]{:S(2)}, u32[]{:S(2)}) collective-permute-start(bf16[3,32,16,128]{3,2,1,0:T(8,128)(2,1)S(1)} %collective-permute-done.prev), channel_id=1, source_target_pairs={{0,1},{1,0},{2,3},{3,2},{4,5},{5,4},{6,7},{7,6},{8,9},{9,8},{10,11... | collective-permute-start | bytes 1179656 | tf_op jit(solution)/shard_map/ppermute | solution.py:767
  22.7 12.4 %collective-permute-start.5 = (bf16[8,3,32,128]{3,2,1,0:T(8,128)(2,1)S(1)}, bf16[8,3,32,128]{3,2,1,0:T(8,128)(2,1)S(1)}, u32[]{:S(2)}, u32[]{:S(2)}) collective-permute-start(bf16[8,3,32,128]{3,2,1,0:T(8,128)(2,1)S(1)} %get-tuple-element.88), channel_id=1, source_target_pairs={{0,124},{1,125},{2,126},{3,127},{4,0},{5,1},{6,2},{7,3},{8,4},{9,5... | collective-permute-start | bytes 589832 | tf_op jit(solution)/shard_map/ppermute | solution.py:767
  30.5 8.1 %collective-permute-start.6 = (bf16[8,3,32,128]{3,2,1,0:T(8,128)(2,1)S(1)}, bf16[8,3,32,128]{3,2,1,0:T(8,128)(2,1)S(1)}, u32[]{:S(2)}, u32[]{:S(2)}) collective-permute-start(bf16[8,3,32,128]{3,2,1,0:T(8,128)(2,1)S(1)} %get-tuple-element.89), channel_id=1, source_target_pairs={{0,124},{1,125},{2,126},{3,127},{4,0},{5,1},{6,2},{7,3},{8,4},{9,5... | collective-permute-start | bytes 589832 | tf_op jit(solution)/shard_map/ppermute | solution.py:767

commit v5 on v3

--- a/solution.py
+++ b/solution.py
@@ -724,12 +724,17 @@
     keep = (lax.axis_index("sec") < lax.axis_size("sec") - 1).astype(F32)
     back = Rows(iback, rback, OUT_INNER)
     copies = []
+    part = CH // 2
     for s in range(OWN):
-        for r in range(TR):
-            ref, i = back.at(r)
-            block[s, :, r, :] = grad[r, s] + ref[i, s].astype(F32) * keep
-        copies.append(pltpu.make_async_copy(block.at[s], out.at[s], sems.at[s]))
-        copies[-1].start()
+        for half in range(2):
+            at = slice(part * half, part * half + part)
+            for r in range(TR):
+                ref, i = back.at(r)
+                block[s, at, r, :] = grad[r, s, at, :] + ref[i, s, at, :].astype(F32) * keep
+            copies.append(
+                pltpu.make_async_copy(block.at[s, at], out.at[s, at], sems.at[2 * s + half])
+            )
+            copies[-1].start()
     for c in copies:
         c.wait()
 
@@ -743,21 +748,20 @@
         out_specs=pl.BlockSpec(memory_space=pltpu.HBM),
         scratch_shapes=[
             pltpu.VMEM((OWN, CH, TR, COLS), F32),
-            pltpu.SemaphoreType.DMA((OWN,)),
+            pltpu.SemaphoreType.DMA((2 * OWN,)),
         ],
         compiler_params=params(2),
         name="finish",
     )(*args)
 
 
-def move(value, secs, tile_to, wrap=True):
+def move(value, secs, tile_to):
     n, m = lax.axis_size("sec"), lax.axis_size("tile")
-    pairs = [
-        (a * m + b, ((a + secs) % n) * m + tile_to(b))
-        for a in range(n)
-        for b in range(m)
-        if tile_to(b) is not None and (wrap or 0 <= a + secs < n)
-    ]
+    pairs = []
+    for a in range(n):
+        for b in range(m):
+            to = tile_to(b)
+            pairs.append((a * m + b, a * m + b if to is None else ((a + secs) % n) * m + to))
     return lax.ppermute(value, ("sec", "tile"), pairs)
 
 
@@ -782,7 +786,7 @@
     )
     sibling = move(for_sibling, 0, to_sibling)
     outer = move(for_outer, 0, to_outer)
-    pouter = move(for_outer, 1, to_outer, False)
+    pouter = move(for_outer, 1, to_outer)
     (
         wcur, wear, wboth, w2own, w2first, w2rest, w2b, w2brest, wgear, wgcur, wgboth, bias,
     ) = weights(first_kernel, second_kernel, first_bias[None])

time: 40 us -> 39.9 us (level)
  no operation moved by 1% of the time
where the time goes in v5:
time: 39.9 us; the launch traced here: 39.8 us
  Pallas kernels  17.2 us (43%)
  starting transfers between devices  15 us (38%)
  waiting for transfers between devices  6.82 us (17%)
  between operations  0.72 us (2%)
    pallas_call x7, Pallas kernels, call(): pl.pallas_call(kernel, out_shape=tuple((jax.ShapeDtypeStruct(shape, kind)...  16 us
    ppermute x7, starting transfers between devices, move(): return lax.ppermute(value, ('sec', 'tile'), pairs)  15 us
    ppermute x7, waiting for transfers between devices, move(): return lax.ppermute(value, ('sec', 'tile'), pairs)  6.82 us
    pallas_call x1, Pallas kernels, finish(): pl.pallas_call(finish_kernel, out_shape=jax.ShapeDtypeStruct((OWN, CH, TR...  1.19 us
  transfers between devices with their start and end apart: 7, of which 2 were waited for; matrix products, arithmetic and copies ran while one was open for 0% of the time, Pallas kernels for 40%

profile of v5, /device:TPU:0, one launch (start us, length us, event | category | flops | bytes accessed | tf_op | source)
XLA Modules:
  0.0 39.8 jit_solution(13760153301959255721)
XLA Ops:
  0.6 4.0 %collective-permute-start = (bf16[3,32,16,128]{3,2,1,0:T(8,128)(2,1)}, bf16[3,32,16,128]{3,2,1,0:T(8,128)(2,1)S(1)}, u32[]{:S(2)}, u32[]{:S(2)}) collective-permute-start(bf16[3,32,16,128]{3,2,1,0:T(8,128)(2,1)} %feat_hbm.1), channel_id=1, source_target_pairs={{0,4},{1,5},{2,6},{3,7},{4,8},{5,9},{6,10},{7,11},{8,12},{9,13},{1... | collective-permute-start | bytes 1179656 | tf_op jit(solution)/shard_map/ppermute | solution.py:765
  4.7 1.7 %edges.1 = (bf16[416,128]{1,0:T(8,128)(2,1)S(1)}, bf16[416,128]{1,0:T(8,128)(2,1)S(1)}, f32[3,32,16,128]{3,2,1,0:T(8,128)S(1)}, f32[3,2,16,128]{3,2,1,0:T(8,128)S(1)}, f32[4,8,128]{2,1,0:T(8,128)S(1)}) custom-call(s32[3]{0:T(128)} %valid_hbm.1, f32[3]{0:T(128)} %sharp_hbm.1, f32[2]{0:T(128)} %b2_hbm.1, bf16[3,32,16,128]{3,2,1,0:T(8,128)(2,1)} %feat_hbm.1, ...), custom_call_target="tpu_custom_call" | custom-call | tf_op jit(solution)/shard_map/edges/pallas_call | solution.py:77
  6.3 0.7 %collective-permute-start.2 = (bf16[416,128]{1,0:T(8,128)(2,1)S(1)}, bf16[416,128]{1,0:T(8,128)(2,1)S(1)}, u32[]{:S(2)}, u32[]{:S(2)}) collective-permute-start(bf16[416,128]{1,0:T(8,128)(2,1)S(1)} %get-tuple-element.44), channel_id=1, source_target_pairs={{0,0},{1,2},{2,1},{3,3},{4,4},{5,6},{6,5},{7,7},{8,8},{9,10},{10,9... | collective-permute-start | bytes 319496 | tf_op jit(solution)/shard_map/ppermute | solution.py:765
  7.0 2.5 %collective-permute-start.1 = (bf16[416,128]{1,0:T(8,128)(2,1)S(1)}, bf16[416,128]{1,0:T(8,128)(2,1)S(1)}, u32[]{:S(2)}, u32[]{:S(2)}) collective-permute-start(bf16[416,128]{1,0:T(8,128)(2,1)S(1)} %get-tuple-element.43), channel_id=1, source_target_pairs={{0,1},{1,0},{2,3},{3,2},{4,5},{5,4},{6,7},{7,6},{8,9},{9,8},{10,11... | collective-permute-start | bytes 319496 | tf_op jit(solution)/shard_map/ppermute | solution.py:765
  9.5 0.7 %collective-permute-start.3 = (bf16[416,128]{1,0:T(8,128)(2,1)S(1)}, bf16[416,128]{1,0:T(8,128)(2,1)S(1)}, u32[]{:S(2)}, u32[]{:S(2)}) collective-permute-start(bf16[416,128]{1,0:T(8,128)(2,1)S(1)} %get-tuple-element.44), channel_id=1, source_target_pairs={{0,0},{1,6},{2,5},{3,3},{4,4},{5,10},{6,9},{7,7},{8,8},{9,14},{10,... | collective-permute-start | bytes 319496 | tf_op jit(solution)/shard_map/ppermute | solution.py:765
  10.1 1.5 %weights.1 = (bf16[64,288]{1,0:T(8,128)(2,1)S(1)}, bf16[64,288]{1,0:T(8,128)(2,1)S(1)}, bf16[128,288]{1,0:T(8,128)(2,1)S(1)}, bf16[144,192]{1,0:T(8,128)(2,1)S(1...) custom-call(bf16[3,3,64,64]{3,2,1,0:T(8,128)(2,1)} %k1_hbm.1, ...), custom_call_target="tpu_custom_call" | custom-call | tf_op jit(solution)/shard_map/weights/pallas_call | solution.py:77
  11.6 2.6 %own_inner.1 = (bf16[3,16,96,128]{3,2,1,0:T(8,128)(2,1)S(1)}, f32[14,192,128]{2,1,0:T(8,128)S(1)}, bf16[14,192,128]{2,1,0:T(8,128)(2,1)S(1)}, f32[14,144,128]{2,1,0:T(8,128)S(1)}) custom-call(f32[3,32,16,128]{3,2,1,0:T(8,128)S(1)} %get-tuple-element.46.wide, bf16[64,288]{1,0:T(8,128)(2,1)S(1)} %get-tuple-element.47.wcur, ...), custom_call_target="tpu_custom_call" | custom-call | tf_op jit(solution)/shard_map/own_inner/pallas_call | solution.py:77
  14.2 0.0 collective-permute-done.2.outer
  14.2 0.0 collective-permute-done.1.sibling
  14.2 1.3 %own_rim.1 = (f32[8,192,128]{2,1,0:T(8,128)S(1)}, bf16[8,192,128]{2,1,0:T(8,128)(2,1)S(1)}, f32[8,144,128]{2,1,0:T(8,128)S(1)}, f32[3,2,8,128]{3,2,1,0:T(8,128)S(1)}) custom-call(bf16[416,128]{1,0:T(8,128)(2,1)S(1)} %collective-permute-done.1.sibling, bf16[416,128]{1,0:T(8,128)(2,1)S(1)} %collective-permute-done.2.outer, ...), custom_call_target="tpu_custom_call" | custom-call | tf_op jit(solution)/shard_map/own_rim/pallas_call | solution.py:77
  15.5 0.0 collective-permute-done.3.pouter
  15.5 3.2 %collective-permute-done.prev = bf16[3,32,16,128]{3,2,1,0:T(8,128)(2,1)S(1)} collective-permute-done((bf16[3,32,16,128]{3,2,1,0:T(8,128)(2,1)}, bf16[3,32,16,128]{3,2,1,0:T(8,128)(2,1)S(1)}, u32[]{:S(2)}, u32[]{:S(2)}) %collective-permute-start) | collective-permute-done | bytes 393248 | tf_op jit(solution)/shard_map/ppermute | solution.py:765
  18.7 2.2 %collective-permute-start.4 = (bf16[3,32,16,128]{3,2,1,0:T(8,128)(2,1)S(1)}, bf16[3,32,16,128]{3,2,1,0:T(8,128)(2,1)S(1)}, u32[]{:S(2)}, u32[]{:S(2)}) collective-permute-start(bf16[3,32,16,128]{3,2,1,0:T(8,128)(2,1)S(1)} %collective-permute-done.prev), channel_id=1, source_target_pairs={{0,1},{1,0},{2,3},{3,2},{4,5},{5,4},{6,7},{7,6},{8,9},{9,8},{10,11... | collective-permute-start | bytes 1179656 | tf_op jit(solution)/shard_map/ppermute | solution.py:765
  20.9 3.9 %middle.1 = (bf16[8,3,32,128]{3,2,1,0:T(8,128)(2,1)S(1)}, bf16[3,16,96,128]{3,2,1,0:T(8,128)(2,1)S(1)}, bf16[14,384,128]{2,1,0:T(8,128)(2,1)S(1)}, f32[14,216,12...) custom-call(bf16[3,32,16,128]{3,2,1,0:T(8,128)(2,1)S(1)} %collective, ...), custom_call_target="tpu_custom_call" | custom-call | flops 2305999872 | tf_op jit(solution)/shard_map/middle/pallas_call | solution.py:77
  24.9 3.2 %collective-permute-start.5 = (bf16[8,3,32,128]{3,2,1,0:T(8,128)(2,1)S(1)}, bf16[8,3,32,128]{3,2,1,0:T(8,128)(2,1)S(1)}, u32[]{:S(2)}, u32[]{:S(2)}) collective-permute-start(bf16[8,3,32,128]{3,2,1,0:T(8,128)(2,1)S(1)} %get-tuple-element.82), channel_id=1, source_target_pairs={{0,124},{1,125},{2,126},{3,127},{4,0},{5,1},{6,2},{7,3},{8,4},{9,5... | collective-permute-start | bytes 589832 | tf_op jit(solution)/shard_map/ppermute | solution.py:765
  28.1 0.0 collective-permute-done.4.psib
  28.1 2.4 %borrowed.1 = (bf16[8,3,32,128]{3,2,1,0:T(8,128)(2,1)S(1)}, bf16[8,384,128]{2,1,0:T(8,128)(2,1)S(1)}, bf16[3,8,32,128]{3,2,1,0:T(8,128)(2,1)S(1)}, f32[3,2,8,128]{3,2,1,0:T(8,128)S(1)}) custom-call(bf16[3,32,16,128]{3,2,1,0:T(8,128)(2,1)S(1)} %collective-permute-done.4.psib, bf16[416,128]{1,0:T(8,128)(2,1)S(1)} %collective-permute-done.3.pouter, ...), custom_call_target="tpu_custom_call" | custom-call | flops 3459000064 | tf_op jit(solution)/shard_map/borrowed/pallas_call | solution.py:77
  30.5 1.8 %collective-permute-start.6 = (bf16[8,3,32,128]{3,2,1,0:T(8,128)(2,1)S(1)}, bf16[8,3,32,128]{3,2,1,0:T(8,128)(2,1)S(1)}, u32[]{:S(2)}, u32[]{:S(2)}) collective-permute-start(bf16[8,3,32,128]{3,2,1,0:T(8,128)(2,1)S(1)} %get-tuple-element.83), channel_id=1, source_target_pairs={{0,124},{1,125},{2,126},{3,127},{4,0},{5,1},{6,2},{7,3},{8,4},{9,5... | collective-permute-start | bytes 589832 | tf_op jit(solution)/shard_map/ppermute | solution.py:765
  32.3 2.8 %own_grad.1 = (f32[3,2,16,128]{3,2,1,0:T(8,128)}, f32[16,3,32,128]{3,2,1,0:T(8,128)S(1)}) custom-call(f32[3,2,16,128]{3,2,1,0:T(8,128)S(1)} %get-tuple-element.63.ivotes, f32[3,2,8,128]{3,2,1,0:T(8,128)S(1)} %get-tuple-element.73.rvotes, bf16[3,12,32,128]{3,2,1,0:T(8,128)(2,1)S(1)} %get-tuple-element.70.ig3, ...), custom_call_target="tpu_custom_call" | custom-call | flops 3459000064 | tf_op jit(solution)/shard_map/own_grad/pallas_call | solution.py:77
  35.0 0.0 collective-permute-done.5.iback
  35.0 3.6 %collective-permute-done.6.rback = bf16[8,3,32,128]{3,2,1,0:T(8,128)(2,1)S(1)} collective-permute-done((bf16[8,3,32,128]{3,2,1,0:T(8,128)(2,1)S(1)}, bf16[8,3,32,128]{3,2,1,0:T(8,128)(2,1)S(1)}, u32[]{:S(2)}, u32[]{:S(2)}) %collective-permute-start.6) | collective-permute-done | bytes 196640 | tf_op jit(solution)/shard_map/ppermute | solution.py:765
  38.6 1.2 %finish.1 = f32[3,32,16,128]{3,2,1,0:T(8,128)} custom-call(f32[16,3,32,128]{3,2,1,0:T(8,128)S(1)} %get-tuple-element.81.grad, bf16[8,3,32,128]{3,2,1,0:T(8,128)(2,1)S(1)} %collective-permute-done.5.iback, bf16[8,3,32,128]{3,2,1,0:T(8,128)(2,1)S(1)} %collective-permute-done.6.rback), custom_call_target="tpu_custom_call" | custom-call | tf_op jit(solution)/shard_map/finish/pallas_call | solution.py:744
Async XLA Ops:
  0.6 18.1 %collective-permute-start = (bf16[3,32,16,128]{3,2,1,0:T(8,128)(2,1)}, bf16[3,32,16,128]{3,2,1,0:T(8,128)(2,1)S(1)}, u32[]{:S(2)}, u32[]{:S(2)}) collective-permute-start(bf16[3,32,16,128]{3,2,1,0:T(8,128)(2,1)} %feat_hbm.1), channel_id=1, source_target_pairs={{0,4},{1,5},{2,6},{3,7},{4,8},{5,9},{6,10},{7,11},{8,12},{9,13},{1... | collective-permute-start | bytes 1179656 | tf_op jit(solution)/shard_map/ppermute | solution.py:765
  6.3 7.8 %collective-permute-start.2 = (bf16[416,128]{1,0:T(8,128)(2,1)S(1)}, bf16[416,128]{1,0:T(8,128)(2,1)S(1)}, u32[]{:S(2)}, u32[]{:S(2)}) collective-permute-start(bf16[416,128]{1,0:T(8,128)(2,1)S(1)} %get-tuple-element.44), channel_id=1, source_target_pairs={{0,0},{1,2},{2,1},{3,3},{4,4},{5,6},{6,5},{7,7},{8,8},{9,10},{10,9... | collective-permute-start | bytes 319496 | tf_op jit(solution)/shard_map/ppermute | solution.py:765
  7.0 7.2 %collective-permute-start.1 = (bf16[416,128]{1,0:T(8,128)(2,1)S(1)}, bf16[416,128]{1,0:T(8,128)(2,1)S(1)}, u32[]{:S(2)}, u32[]{:S(2)}) collective-permute-start(bf16[416,128]{1,0:T(8,128)(2,1)S(1)} %get-tuple-element.43), channel_id=1, source_target_pairs={{0,1},{1,0},{2,3},{3,2},{4,5},{5,4},{6,7},{7,6},{8,9},{9,8},{10,11... | collective-permute-start | bytes 319496 | tf_op jit(solution)/shard_map/ppermute | solution.py:765
  9.5 6.0 %collective-permute-start.3 = (bf16[416,128]{1,0:T(8,128)(2,1)S(1)}, bf16[416,128]{1,0:T(8,128)(2,1)S(1)}, u32[]{:S(2)}, u32[]{:S(2)}) collective-permute-start(bf16[416,128]{1,0:T(8,128)(2,1)S(1)} %get-tuple-element.44), channel_id=1, source_target_pairs={{0,0},{1,6},{2,5},{3,3},{4,4},{5,10},{6,9},{7,7},{8,8},{9,14},{10,... | collective-permute-start | bytes 319496 | tf_op jit(solution)/shard_map/ppermute | solution.py:765
  18.7 9.4 %collective-permute-start.4 = (bf16[3,32,16,128]{3,2,1,0:T(8,128)(2,1)S(1)}, bf16[3,32,16,128]{3,2,1,0:T(8,128)(2,1)S(1)}, u32[]{:S(2)}, u32[]{:S(2)}) collective-permute-start(bf16[3,32,16,128]{3,2,1,0:T(8,128)(2,1)S(1)} %collective-permute-done.prev), channel_id=1, source_target_pairs={{0,1},{1,0},{2,3},{3,2},{4,5},{5,4},{6,7},{7,6},{8,9},{9,8},{10,11... | collective-permute-start | bytes 1179656 | tf_op jit(solution)/shard_map/ppermute | solution.py:765
  24.9 10.1 %collective-permute-start.5 = (bf16[8,3,32,128]{3,2,1,0:T(8,128)(2,1)S(1)}, bf16[8,3,32,128]{3,2,1,0:T(8,128)(2,1)S(1)}, u32[]{:S(2)}, u32[]{:S(2)}) collective-permute-start(bf16[8,3,32,128]{3,2,1,0:T(8,128)(2,1)S(1)} %get-tuple-element.82), channel_id=1, source_target_pairs={{0,124},{1,125},{2,126},{3,127},{4,0},{5,1},{6,2},{7,3},{8,4},{9,5... | collective-permute-start | bytes 589832 | tf_op jit(solution)/shard_map/ppermute | solution.py:765
  30.5 8.1 %collective-permute-start.6 = (bf16[8,3,32,128]{3,2,1,0:T(8,128)(2,1)S(1)}, bf16[8,3,32,128]{3,2,1,0:T(8,128)(2,1)S(1)}, u32[]{:S(2)}, u32[]{:S(2)}) collective-permute-start(bf16[8,3,32,128]{3,2,1,0:T(8,128)(2,1)S(1)} %get-tuple-element.83), channel_id=1, source_target_pairs={{0,124},{1,125},{2,126},{3,127},{4,0},{5,1},{6,2},{7,3},{8,4},{9,5... | collective-permute-start | bytes 589832 | tf_op jit(solution)/shard_map/ppermute | solution.py:765

commit v6 on v3

--- a/solution.py
+++ b/solution.py
@@ -750,14 +750,13 @@
     )(*args)
 
 
-def move(value, secs, tile_to, wrap=True):
+def move(value, secs, tile_to):
     n, m = lax.axis_size("sec"), lax.axis_size("tile")
-    pairs = [
-        (a * m + b, ((a + secs) % n) * m + tile_to(b))
-        for a in range(n)
-        for b in range(m)
-        if tile_to(b) is not None and (wrap or 0 <= a + secs < n)
-    ]
+    pairs = []
+    for a in range(n):
+        for b in range(m):
+            to = tile_to(b)
+            pairs.append((a * m + b, a * m + b if to is None else ((a + secs) % n) * m + to))
     return lax.ppermute(value, ("sec", "tile"), pairs)
 
 
@@ -782,7 +781,7 @@
     )
     sibling = move(for_sibling, 0, to_sibling)
     outer = move(for_outer, 0, to_outer)
-    pouter = move(for_outer, 1, to_outer, False)
+    pouter = move(for_outer, 1, to_outer)
     (
         wcur, wear, wboth, w2own, w2first, w2rest, w2b, w2brest, wgear, wgcur, wgboth, bias,
     ) = weights(first_kernel, second_kernel, first_bias[None])

time: 40 us -> 40 us (level)
  no operation moved by 1% of the time
where the time goes in v6:
time: 40 us; the launch traced here: 39.8 us
  Pallas kernels  17.3 us (43%)
  starting transfers between devices  15 us (38%)
  waiting for transfers between devices  6.82 us (17%)
  between operations  0.72 us (2%)
    pallas_call x7, Pallas kernels, call(): pl.pallas_call(kernel, out_shape=tuple((jax.ShapeDtypeStruct(shape, kind)...  16 us
    ppermute x7, starting transfers between devices, move(): return lax.ppermute(value, ('sec', 'tile'), pairs)  15 us
    ppermute x7, waiting for transfers between devices, move(): return lax.ppermute(value, ('sec', 'tile'), pairs)  6.82 us
    pallas_call x1, Pallas kernels, finish(): pl.pallas_call(finish_kernel, out_shape=jax.ShapeDtypeStruct((OWN, CH, TR...  1.23 us
  transfers between devices with their start and end apart: 7, of which 2 were waited for; matrix products, arithmetic and copies ran while one was open for 0% of the time, Pallas kernels for 40%

profile of v6, /device:TPU:0, one launch (start us, length us, event | category | flops | bytes accessed | tf_op | source)
XLA Modules:
  0.0 39.8 jit_solution(16895178756419539936)
XLA Ops:
  0.6 4.0 %collective-permute-start = (bf16[3,32,16,128]{3,2,1,0:T(8,128)(2,1)}, bf16[3,32,16,128]{3,2,1,0:T(8,128)(2,1)S(1)}, u32[]{:S(2)}, u32[]{:S(2)}) collective-permute-start(bf16[3,32,16,128]{3,2,1,0:T(8,128)(2,1)} %feat_hbm.1), channel_id=1, source_target_pairs={{0,4},{1,5},{2,6},{3,7},{4,8},{5,9},{6,10},{7,11},{8,12},{9,13},{1... | collective-permute-start | bytes 1179656 | tf_op jit(solution)/shard_map/ppermute | solution.py:760
  4.7 1.7 %edges.1 = (bf16[416,128]{1,0:T(8,128)(2,1)S(1)}, bf16[416,128]{1,0:T(8,128)(2,1)S(1)}, f32[3,32,16,128]{3,2,1,0:T(8,128)S(1)}, f32[3,2,16,128]{3,2,1,0:T(8,128)S(1)}, f32[4,8,128]{2,1,0:T(8,128)S(1)}) custom-call(s32[3]{0:T(128)} %valid_hbm.1, f32[3]{0:T(128)} %sharp_hbm.1, f32[2]{0:T(128)} %b2_hbm.1, bf16[3,32,16,128]{3,2,1,0:T(8,128)(2,1)} %feat_hbm.1, ...), custom_call_target="tpu_custom_call" | custom-call | tf_op jit(solution)/shard_map/edges/pallas_call | solution.py:77
  6.3 0.7 %collective-permute-start.2 = (bf16[416,128]{1,0:T(8,128)(2,1)S(1)}, bf16[416,128]{1,0:T(8,128)(2,1)S(1)}, u32[]{:S(2)}, u32[]{:S(2)}) collective-permute-start(bf16[416,128]{1,0:T(8,128)(2,1)S(1)} %get-tuple-element.44), channel_id=1, source_target_pairs={{0,0},{1,2},{2,1},{3,3},{4,4},{5,6},{6,5},{7,7},{8,8},{9,10},{10,9... | collective-permute-start | bytes 319496 | tf_op jit(solution)/shard_map/ppermute | solution.py:760
  7.0 2.5 %collective-permute-start.1 = (bf16[416,128]{1,0:T(8,128)(2,1)S(1)}, bf16[416,128]{1,0:T(8,128)(2,1)S(1)}, u32[]{:S(2)}, u32[]{:S(2)}) collective-permute-start(bf16[416,128]{1,0:T(8,128)(2,1)S(1)} %get-tuple-element.43), channel_id=1, source_target_pairs={{0,1},{1,0},{2,3},{3,2},{4,5},{5,4},{6,7},{7,6},{8,9},{9,8},{10,11... | collective-permute-start | bytes 319496 | tf_op jit(solution)/shard_map/ppermute | solution.py:760
  9.5 0.7 %collective-permute-start.3 = (bf16[416,128]{1,0:T(8,128)(2,1)S(1)}, bf16[416,128]{1,0:T(8,128)(2,1)S(1)}, u32[]{:S(2)}, u32[]{:S(2)}) collective-permute-start(bf16[416,128]{1,0:T(8,128)(2,1)S(1)} %get-tuple-element.44), channel_id=1, source_target_pairs={{0,0},{1,6},{2,5},{3,3},{4,4},{5,10},{6,9},{7,7},{8,8},{9,14},{10,... | collective-permute-start | bytes 319496 | tf_op jit(solution)/shard_map/ppermute | solution.py:760
  10.1 1.5 %weights.1 = (bf16[64,288]{1,0:T(8,128)(2,1)S(1)}, bf16[64,288]{1,0:T(8,128)(2,1)S(1)}, bf16[128,288]{1,0:T(8,128)(2,1)S(1)}, bf16[144,192]{1,0:T(8,128)(2,1)S(1...) custom-call(bf16[3,3,64,64]{3,2,1,0:T(8,128)(2,1)} %k1_hbm.1, ...), custom_call_target="tpu_custom_call" | custom-call | tf_op jit(solution)/shard_map/weights/pallas_call | solution.py:77
  11.6 2.6 %own_inner.1 = (bf16[3,16,96,128]{3,2,1,0:T(8,128)(2,1)S(1)}, f32[14,192,128]{2,1,0:T(8,128)S(1)}, bf16[14,192,128]{2,1,0:T(8,128)(2,1)S(1)}, f32[14,144,128]{2,1,0:T(8,128)S(1)}) custom-call(f32[3,32,16,128]{3,2,1,0:T(8,128)S(1)} %get-tuple-element.46.wide, bf16[64,288]{1,0:T(8,128)(2,1)S(1)} %get-tuple-element.47.wcur, ...), custom_call_target="tpu_custom_call" | custom-call | tf_op jit(solution)/shard_map/own_inner/pallas_call | solution.py:77
  14.2 0.0 collective-permute-done.2.outer
  14.2 0.0 collective-permute-done.1.sibling
  14.2 1.3 %own_rim.1 = (f32[8,192,128]{2,1,0:T(8,128)S(1)}, bf16[8,192,128]{2,1,0:T(8,128)(2,1)S(1)}, f32[8,144,128]{2,1,0:T(8,128)S(1)}, f32[3,2,8,128]{3,2,1,0:T(8,128)S(1)}) custom-call(bf16[416,128]{1,0:T(8,128)(2,1)S(1)} %collective-permute-done.1.sibling, bf16[416,128]{1,0:T(8,128)(2,1)S(1)} %collective-permute-done.2.outer, ...), custom_call_target="tpu_custom_call" | custom-call | tf_op jit(solution)/shard_map/own_rim/pallas_call | solution.py:77
  15.5 0.0 collective-permute-done.3.pouter
  15.5 3.2 %collective-permute-done.prev = bf16[3,32,16,128]{3,2,1,0:T(8,128)(2,1)S(1)} collective-permute-done((bf16[3,32,16,128]{3,2,1,0:T(8,128)(2,1)}, bf16[3,32,16,128]{3,2,1,0:T(8,128)(2,1)S(1)}, u32[]{:S(2)}, u32[]{:S(2)}) %collective-permute-start) | collective-permute-done | bytes 393248 | tf_op jit(solution)/shard_map/ppermute | solution.py:760
  18.7 2.2 %collective-permute-start.4 = (bf16[3,32,16,128]{3,2,1,0:T(8,128)(2,1)S(1)}, bf16[3,32,16,128]{3,2,1,0:T(8,128)(2,1)S(1)}, u32[]{:S(2)}, u32[]{:S(2)}) collective-permute-start(bf16[3,32,16,128]{3,2,1,0:T(8,128)(2,1)S(1)} %collective-permute-done.prev), channel_id=1, source_target_pairs={{0,1},{1,0},{2,3},{3,2},{4,5},{5,4},{6,7},{7,6},{8,9},{9,8},{10,11... | collective-permute-start | bytes 1179656 | tf_op jit(solution)/shard_map/ppermute | solution.py:760
  20.9 3.9 %middle.1 = (bf16[8,3,32,128]{3,2,1,0:T(8,128)(2,1)S(1)}, bf16[3,16,96,128]{3,2,1,0:T(8,128)(2,1)S(1)}, bf16[14,384,128]{2,1,0:T(8,128)(2,1)S(1)}, f32[14,216,12...) custom-call(bf16[3,32,16,128]{3,2,1,0:T(8,128)(2,1)S(1)} %collective, ...), custom_call_target="tpu_custom_call" | custom-call | flops 2305999872 | tf_op jit(solution)/shard_map/middle/pallas_call | solution.py:77
  24.9 3.2 %collective-permute-start.5 = (bf16[8,3,32,128]{3,2,1,0:T(8,128)(2,1)S(1)}, bf16[8,3,32,128]{3,2,1,0:T(8,128)(2,1)S(1)}, u32[]{:S(2)}, u32[]{:S(2)}) collective-permute-start(bf16[8,3,32,128]{3,2,1,0:T(8,128)(2,1)S(1)} %get-tuple-element.82), channel_id=1, source_target_pairs={{0,124},{1,125},{2,126},{3,127},{4,0},{5,1},{6,2},{7,3},{8,4},{9,5... | collective-permute-start | bytes 589832 | tf_op jit(solution)/shard_map/ppermute | solution.py:760
  28.1 0.0 collective-permute-done.4.psib
  28.1 2.4 %borrowed.1 = (bf16[8,3,32,128]{3,2,1,0:T(8,128)(2,1)S(1)}, bf16[8,384,128]{2,1,0:T(8,128)(2,1)S(1)}, bf16[3,8,32,128]{3,2,1,0:T(8,128)(2,1)S(1)}, f32[3,2,8,128]{3,2,1,0:T(8,128)S(1)}) custom-call(bf16[3,32,16,128]{3,2,1,0:T(8,128)(2,1)S(1)} %collective-permute-done.4.psib, bf16[416,128]{1,0:T(8,128)(2,1)S(1)} %collective-permute-done.3.pouter, ...), custom_call_target="tpu_custom_call" | custom-call | flops 3459000064 | tf_op jit(solution)/shard_map/borrowed/pallas_call | solution.py:77
  30.5 1.8 %collective-permute-start.6 = (bf16[8,3,32,128]{3,2,1,0:T(8,128)(2,1)S(1)}, bf16[8,3,32,128]{3,2,1,0:T(8,128)(2,1)S(1)}, u32[]{:S(2)}, u32[]{:S(2)}) collective-permute-start(bf16[8,3,32,128]{3,2,1,0:T(8,128)(2,1)S(1)} %get-tuple-element.83), channel_id=1, source_target_pairs={{0,124},{1,125},{2,126},{3,127},{4,0},{5,1},{6,2},{7,3},{8,4},{9,5... | collective-permute-start | bytes 589832 | tf_op jit(solution)/shard_map/ppermute | solution.py:760
  32.3 2.8 %own_grad.1 = (f32[3,2,16,128]{3,2,1,0:T(8,128)}, f32[16,3,32,128]{3,2,1,0:T(8,128)S(1)}) custom-call(f32[3,2,16,128]{3,2,1,0:T(8,128)S(1)} %get-tuple-element.63.ivotes, f32[3,2,8,128]{3,2,1,0:T(8,128)S(1)} %get-tuple-element.73.rvotes, bf16[3,12,32,128]{3,2,1,0:T(8,128)(2,1)S(1)} %get-tuple-element.70.ig3, ...), custom_call_target="tpu_custom_call" | custom-call | flops 3459000064 | tf_op jit(solution)/shard_map/own_grad/pallas_call | solution.py:77
  35.0 0.0 collective-permute-done.5.iback
  35.0 3.6 %collective-permute-done.6.rback = bf16[8,3,32,128]{3,2,1,0:T(8,128)(2,1)S(1)} collective-permute-done((bf16[8,3,32,128]{3,2,1,0:T(8,128)(2,1)S(1)}, bf16[8,3,32,128]{3,2,1,0:T(8,128)(2,1)S(1)}, u32[]{:S(2)}, u32[]{:S(2)}) %collective-permute-start.6) | collective-permute-done | bytes 196640 | tf_op jit(solution)/shard_map/ppermute | solution.py:760
  38.6 1.2 %finish.1 = f32[3,32,16,128]{3,2,1,0:T(8,128)} custom-call(f32[16,3,32,128]{3,2,1,0:T(8,128)S(1)} %get-tuple-element.81.grad, bf16[8,3,32,128]{3,2,1,0:T(8,128)(2,1)S(1)} %collective-permute-done.5.iback, bf16[8,3,32,128]{3,2,1,0:T(8,128)(2,1)S(1)} %collective-permute-done.6.rback), custom_call_target="tpu_custom_call" | custom-call | tf_op jit(solution)/shard_map/finish/pallas_call | solution.py:739
Async XLA Ops:
  0.6 18.1 %collective-permute-start = (bf16[3,32,16,128]{3,2,1,0:T(8,128)(2,1)}, bf16[3,32,16,128]{3,2,1,0:T(8,128)(2,1)S(1)}, u32[]{:S(2)}, u32[]{:S(2)}) collective-permute-start(bf16[3,32,16,128]{3,2,1,0:T(8,128)(2,1)} %feat_hbm.1), channel_id=1, source_target_pairs={{0,4},{1,5},{2,6},{3,7},{4,8},{5,9},{6,10},{7,11},{8,12},{9,13},{1... | collective-permute-start | bytes 1179656 | tf_op jit(solution)/shard_map/ppermute | solution.py:760
  6.3 7.8 %collective-permute-start.2 = (bf16[416,128]{1,0:T(8,128)(2,1)S(1)}, bf16[416,128]{1,0:T(8,128)(2,1)S(1)}, u32[]{:S(2)}, u32[]{:S(2)}) collective-permute-start(bf16[416,128]{1,0:T(8,128)(2,1)S(1)} %get-tuple-element.44), channel_id=1, source_target_pairs={{0,0},{1,2},{2,1},{3,3},{4,4},{5,6},{6,5},{7,7},{8,8},{9,10},{10,9... | collective-permute-start | bytes 319496 | tf_op jit(solution)/shard_map/ppermute | solution.py:760
  7.0 7.2 %collective-permute-start.1 = (bf16[416,128]{1,0:T(8,128)(2,1)S(1)}, bf16[416,128]{1,0:T(8,128)(2,1)S(1)}, u32[]{:S(2)}, u32[]{:S(2)}) collective-permute-start(bf16[416,128]{1,0:T(8,128)(2,1)S(1)} %get-tuple-element.43), channel_id=1, source_target_pairs={{0,1},{1,0},{2,3},{3,2},{4,5},{5,4},{6,7},{7,6},{8,9},{9,8},{10,11... | collective-permute-start | bytes 319496 | tf_op jit(solution)/shard_map/ppermute | solution.py:760
  9.5 6.0 %collective-permute-start.3 = (bf16[416,128]{1,0:T(8,128)(2,1)S(1)}, bf16[416,128]{1,0:T(8,128)(2,1)S(1)}, u32[]{:S(2)}, u32[]{:S(2)}) collective-permute-start(bf16[416,128]{1,0:T(8,128)(2,1)S(1)} %get-tuple-element.44), channel_id=1, source_target_pairs={{0,0},{1,6},{2,5},{3,3},{4,4},{5,10},{6,9},{7,7},{8,8},{9,14},{10,... | collective-permute-start | bytes 319496 | tf_op jit(solution)/shard_map/ppermute | solution.py:760
  18.7 9.4 %collective-permute-start.4 = (bf16[3,32,16,128]{3,2,1,0:T(8,128)(2,1)S(1)}, bf16[3,32,16,128]{3,2,1,0:T(8,128)(2,1)S(1)}, u32[]{:S(2)}, u32[]{:S(2)}) collective-permute-start(bf16[3,32,16,128]{3,2,1,0:T(8,128)(2,1)S(1)} %collective-permute-done.prev), channel_id=1, source_target_pairs={{0,1},{1,0},{2,3},{3,2},{4,5},{5,4},{6,7},{7,6},{8,9},{9,8},{10,11... | collective-permute-start | bytes 1179656 | tf_op jit(solution)/shard_map/ppermute | solution.py:760
  24.9 10.1 %collective-permute-start.5 = (bf16[8,3,32,128]{3,2,1,0:T(8,128)(2,1)S(1)}, bf16[8,3,32,128]{3,2,1,0:T(8,128)(2,1)S(1)}, u32[]{:S(2)}, u32[]{:S(2)}) collective-permute-start(bf16[8,3,32,128]{3,2,1,0:T(8,128)(2,1)S(1)} %get-tuple-element.82), channel_id=1, source_target_pairs={{0,124},{1,125},{2,126},{3,127},{4,0},{5,1},{6,2},{7,3},{8,4},{9,5... | collective-permute-start | bytes 589832 | tf_op jit(solution)/shard_map/ppermute | solution.py:760
  30.5 8.1 %collective-permute-start.6 = (bf16[8,3,32,128]{3,2,1,0:T(8,128)(2,1)S(1)}, bf16[8,3,32,128]{3,2,1,0:T(8,128)(2,1)S(1)}, u32[]{:S(2)}, u32[]{:S(2)}) collective-permute-start(bf16[8,3,32,128]{3,2,1,0:T(8,128)(2,1)S(1)} %get-tuple-element.83), channel_id=1, source_target_pairs={{0,124},{1,125},{2,126},{3,127},{4,0},{5,1},{6,2},{7,3},{8,4},{9,5... | collective-permute-start | bytes 589832 | tf_op jit(solution)/shard_map/ppermute | solution.py:760
